TPU v7x, 32 devices: a whole 2x2x4 slice. The times are simulated.
32 devices in a mesh: ch: 32 (over z, y, x, core).
Axes of the slice: x: 2, y: 2, z: 4, core: 2. Of those that a mesh axis runs over, the one named last changes fastest.
Arguments:
- spectra: bfloat16 [4, 16384, 128], P(None, 'ch'), may hold values from -6 to 6
- offsets: int32 [16384], P('ch'), may hold values from 0 to 7
- bins: int32 [4], replicated, may hold values from 1 to 63
Outputs:
- gradient: float32 [4, 16384, 128], P(None, 'ch')
All inputs are finite; a program needn't handle non-finite values.
Results may differ from a plain program's by a relative error of at most 0.0015.
Values may be sent and summed in bfloat16 or wider, within the bound.
No kernel may reach another device: no remote copies, remote signals or barrier semaphores. Data moves between devices by JAX's collectives and lax.ppermute only.
A program may use at most 64 MiB of HBM per device.

v0:
```python
import math

import jax
import jax.numpy as jnp
from jax import lax
from jax.sharding import PartitionSpec as P

spacing_metres = 8
period_metres = 4096
model_amp = 0.5


def shifted(value, axis, steps):
    count = lax.axis_size(axis)
    leading, last = (max(0, -steps), min(count, count - steps))
    return lax.ppermute(value, axis, [(source, source + steps) for source in range(leading, last)])


def block_terms(mine, mine_off, other, other_off, gap, bins):
    windows = mine.shape[2] // 2
    channels = mine.shape[1]
    other_swap = jnp.concatenate([-other[..., windows:], other[..., :windows]], axis=-1)
    mine_swap = jnp.concatenate([mine[..., windows:], -mine[..., :windows]], axis=-1)
    real_part = (
        jnp.einsum("fik,fjk->fij", mine, other, preferred_element_type=jnp.float32) / windows
    )
    imag_part = (
        jnp.einsum("fik,fjk->fij", mine, other_swap, preferred_element_type=jnp.float32) / windows
    )
    rows = jnp.arange(channels, dtype=jnp.int32)
    distance = (
        (gap + rows[None, :] - rows[:, None]) * spacing_metres
        + other_off[None, :]
        - mine_off[:, None]
    )
    wrapped = jnp.mod(bins[:, None, None] * distance[None, :, :], period_metres)
    phase = wrapped.astype(jnp.float32) * (2.0 * math.pi / period_metres)
    grad_real = jnp.tanh(real_part - model_amp * jnp.cos(phase)).astype(jnp.bfloat16)
    grad_imag = jnp.tanh(imag_part - model_amp * jnp.sin(phase)).astype(jnp.bfloat16)
    forward_term = jnp.einsum("fij,fjk->fik", grad_real, other, preferred_element_type=jnp.float32)
    forward_term = forward_term + jnp.einsum(
        "fij,fjk->fik", grad_imag, other_swap, preferred_element_type=jnp.float32
    )
    back_term = jnp.einsum("fij,fik->fjk", grad_real, mine, preferred_element_type=jnp.float32)
    back_term = back_term + jnp.einsum(
        "fij,fik->fjk", grad_imag, mine_swap, preferred_element_type=jnp.float32
    )
    return (forward_term, back_term)


def local(spectra, offsets, bins):
    channels = spectra.shape[1]
    windows = spectra.shape[2] // 2
    off_wire = offsets.astype(jnp.bfloat16)
    partners = [(spectra, off_wire)]
    for distance in range(1, 4):
        partners.append(shifted((spectra, off_wire), "ch", -distance))
    total = jnp.zeros(spectra.shape, jnp.float32)
    returns = []
    for distance in range(4):
        other, other_off = partners[distance]
        forward_term, back_term = block_terms(
            spectra, offsets, other, other_off.astype(jnp.int32), distance * channels, bins
        )
        total = total + forward_term
        returns.append(back_term)
    total = total + returns[0]
    for distance in range(1, 4):
        total = total + shifted(returns[distance].astype(jnp.bfloat16), "ch", distance).astype(
            jnp.float32
        )
    return total / windows


def solution(mesh):
    return jax.shard_map(
        local,
        mesh=mesh,
        in_specs=(P(None, "ch", None), P("ch"), P()),
        out_specs=P(None, "ch", None),
        check_vma=False,
    )
```

profile of v0, /device:TPU:19, one launch (start us, length us, event | category | flops | bytes accessed | tf_op | source)
XLA Modules:
  0.0 208.5 jit_solution(8669910676881977790)
XLA Ops:
  0.8 2.2 %collective-permute-start.3 = (bf16[512]{0:T(512)(128)(2,1)S(1)}, bf16[512]{0:T(512)(128)(2,1)S(1)}, u32[]{:S(2)}, u32[]{:S(2)}) collective-permute-start(bf16[512]{0:T(512)(128)(2,1)S(1)} %get-tuple-element.6), channel_id=1, source_target_pairs={{2,0},{3,1},{4,2},{5,3},{6,4},{7,5},{8,6},{9,7},{10,8},{11,9},{12,... | collective-permute-start | bytes 3080 | tf_op jit(solution)/shard_map/ppermute | solution.py:16
  2.9 2.9 %collective-permute-start.1 = (bf16[512]{0:T(512)(128)(2,1)S(1)}, bf16[512]{0:T(512)(128)(2,1)S(1)}, u32[]{:S(2)}, u32[]{:S(2)}) collective-permute-start(bf16[512]{0:T(512)(128)(2,1)S(1)} %get-tuple-element.6), channel_id=1, source_target_pairs={{1,0},{2,1},{3,2},{4,3},{5,4},{6,5},{7,6},{8,7},{9,8},{10,9},{11,1... | collective-permute-start | bytes 3080 | tf_op jit(solution)/shard_map/ppermute | solution.py:16
  5.8 3.9 %collective-permute-start.5 = (bf16[512]{0:T(512)(128)(2,1)S(1)}, bf16[512]{0:T(512)(128)(2,1)S(1)}, u32[]{:S(2)}, u32[]{:S(2)}) collective-permute-start(bf16[512]{0:T(512)(128)(2,1)S(1)} %get-tuple-element.6), channel_id=1, source_target_pairs={{3,0},{4,1},{5,2},{6,3},{7,4},{8,5},{9,6},{10,7},{11,8},{12,9},{13... | collective-permute-start | bytes 3080 | tf_op jit(solution)/shard_map/ppermute | solution.py:16
  9.7 2.5 %collective-permute-start.4 = (bf16[4,512,128]{2,1,0:T(8,128)(2,1)}, bf16[4,512,128]{2,1,0:T(8,128)(2,1)}, u32[]{:S(2)}, u32[]{:S(2)}) collective-permute-start(bf16[4,512,128]{2,1,0:T(8,128)(2,1)} %param.3), channel_id=1, source_target_pairs={{3,0},{4,1},{5,2},{6,3},{7,4},{8,5},{9,6},{10,7},{11,8},{12,9},{13... | collective-permute-start | bytes 1572872 | tf_op jit(solution)/shard_map/ppermute | solution.py:16
  12.2 1.9 collective-permute-start
  14.1 2.5 %fusion.45 = (bf16[4,512,64]{2,1,0:T(8,128)(2,1)S(1)}, bf16[4,512,64]{2,1,0:T(8,128)(2,1)}, bf16[4,512,64]{2,1,0:T(8,128)(2,1)S(1)}, bf16[4,512,64]{2,1,0:T(8,128)(2,1)}) fusion(bf16[4,512,128]{2,1,0:T(8,128)(2,1)} %param.3), kind=kLoop, calls=%fused_computation.98 | loop fusion | flops 262144 | bytes 1572864 | tf_op jit(solution)/shard_map/slice | solution.py:22
  16.9 3.6 %collective-permute-start.2 = (bf16[4,512,128]{2,1,0:T(8,128)(2,1)S(1)}, bf16[4,512,128]{2,1,0:T(8,128)(2,1)}, u32[]{:S(2)}, u32[]{:S(2)}) collective-permute-start(bf16[4,512,128]{2,1,0:T(8,128)(2,1)S(1)} %copy-done), channel_id=1, source_target_pairs={{2,0},{3,1},{4,2},{5,3},{6,4},{7,5},{8,6},{9,7},{10,8},{11,9},{12,... | collective-permute-start | bytes 1572872 | tf_op jit(solution)/shard_map/ppermute | solution.py:16
  22.4 31.8 %fusion.20 = (f32[4,512,512]{1,2,0:T(8,128)}, f32[4,512,512]{1,2,0:T(8,128)}) fusion(s32[512,512]{0,1:T(8,128)S(1)} %get-tuple-element.19, s32[4]{0:T(128)S(1)} %copy-done.10, s32[512,512]{0,1:T(8,128)S(1)} %get-tuple-element.20), kind=kLoop, calls=%fused_computation.48 | loop fusion | flops 29360128 | bytes 10485776 | tf_op jit(solution)/shard_map/sin | solution.py:39
  54.2 5.3 %copy.5 = f32[4,512,512]{2,1,0:T(8,128)} copy(f32[4,512,512]{1,2,0:T(8,128)} %get-tuple-element.22) | data formatting | bytes 8388608 | tf_op jit(solution)/shard_map/cos | solution.py:38
  59.5 3.0 %tanh_convert_fusion.3 = bf16[4,512,512]{2,1,0:T(8,128)(2,1)S(1)} fusion(f32[4,512,512]{2,1,0:T(8,128)} %copy.5, bf16[4,512,128]{2,1,0:T(8,128)(2,1)S(1)} %copy-done), kind=kOutput, calls=%fused_computation.47 | convolution fusion | flops 272629760 | bytes 6815744 | tf_op jit(solution)/shard_map/fik,fjk->fij/dot_general | solution.py:25
  62.4 5.3 %copy.25 = f32[4,512,512]{2,1,0:T(8,128)} copy(f32[4,512,512]{1,2,0:T(8,128)} %get-tuple-element.21) | data formatting | bytes 8388608 | tf_op jit(solution)/shard_map/sin | solution.py:39
  68.5 18.4 %fusion.19 = bf16[4,512,512]{1,2,0:T(8,128)(2,1)S(1)} fusion(bf16[4,512,128]{2,1,0:T(8,128)(2,1)S(1)} %copy-done, s32[512,512]{0,1:T(8,128)} %copy-done.4, s32[4]{0:T(128)S(1)} %copy-done.10, bf16[4,512,64]{2,1,0:T(8,128)(2,1)} %get-tuple-element.16, bf16[4,512,64]{2,1,0:T(8,128)(2,1)} %get-tuple-element.14), kind=kOutput, calls=%fused_computation.43 | convolution fusion | flops 288358400 | bytes 4194320 | tf_op jit(solution)/shard_map/fik,fjk->fij/dot_general | solution.py:28
  89.7 1.8 slice_negate_fusion
  92.7 17.5 %tanh_convert_fusion = bf16[4,512,512]{1,2,0:T(8,128)(2,1)S(1)} fusion(bf16[4,512,128]{2,1,0:T(8,128)(2,1)S(1)} %copy-done, bf16[4,512,128]{2,1,0:T(8,128)(2,1)} %collective-permute-done.4, s32[512,512]{0,1:T(8,128)S(1)} %copy-done.3, s32[4]{0:T(128)S(1)} %copy-done.10), kind=kOutput, calls=%fused_computation.44 | convolution fusion | flops 287309824 | bytes 4194320 | tf_op jit(solution)/shard_map/fik,fjk->fij/dot_general | solution.py:25
  111.9 3.4 %collective-permute-start.8 = (bf16[4,512,128]{2,1,0:T(8,128)(2,1)S(1)}, bf16[4,512,128]{2,1,0:T(8,128)(2,1)S(1)}, u32[]{:S(2)}, u32[]{:S(2)}) collective-permute-start(bf16[4,512,128]{2,1,0:T(8,128)(2,1)S(1)} %fusion.32), channel_id=1, source_target_pairs={{0,3},{1,4},{2,5},{3,6},{4,7},{5,8},{6,9},{7,10},{8,11},{9,12},{10... | collective-permute-start | bytes 1572872 | tf_op jit(solution)/shard_map/ppermute | solution.py:16
  116.7 17.2 %fusion.17 = bf16[4,512,512]{1,2,0:T(8,128)(2,1)S(1)} fusion(bf16[4,512,128]{2,1,0:T(8,128)(2,1)S(1)} %copy-done, s32[512,512]{0,1:T(8,128)S(1)} %copy-done.7, s32[4]{0:T(128)S(1)} %copy-done.10, bf16[4,512,64]{2,1,0:T(8,128)(2,1)S(1)} %get-tuple-element.10, bf16[4,512,64]{2,1,0:T(8,128)(2,1)S(1)} %get-tuple-element.9), kind=kOutput, calls=%fused_computation.40 | convolution fusion | flops 288358400 | bytes 4194320 | tf_op jit(solution)/shard_map/fik,fjk->fij/dot_general | solution.py:28
  135.8 17.6 %tanh_convert_fusion.1 = bf16[4,512,512]{1,2,0:T(8,128)(2,1)S(1)} fusion(bf16[4,512,128]{2,1,0:T(8,128)(2,1)S(1)} %copy-done, bf16[4,512,128]{2,1,0:T(8,128)(2,1)} %collective-permute-done.2, s32[512,512]{0,1:T(8,128)S(1)} %copy-done.8, s32[4]{0:T(128)S(1)} %copy-done.10), kind=kOutput, calls=%fused_computation.45 | convolution fusion | flops 287309824 | bytes 4194320 | tf_op jit(solution)/shard_map/fik,fjk->fij/dot_general | solution.py:25
  155.5 17.0 %fusion.15 = bf16[4,512,512]{1,2,0:T(8,128)(2,1)S(1)} fusion(bf16[4,512,128]{2,1,0:T(8,128)(2,1)S(1)} %copy-done, s32[512,512]{0,1:T(8,128)S(1)} %copy-done.8, s32[4]{0:T(128)S(1)} %copy-done.10, bf16[4,512,64]{2,1,0:T(8,128)(2,1)S(1)} %get-tuple-element.8, bf16[4,512,64]{2,1,0:T(8,128)(2,1)S(1)} %get-tuple-element.7), kind=kOutput, calls=%fused_computation.37 | convolution fusion | flops 288358400 | bytes 4194320 | tf_op jit(solution)/shard_map/fik,fjk->fij/dot_general | solution.py:28
  173.2 4.0 %collective-permute-start.7 = (bf16[4,512,128]{2,1,0:T(8,128)(2,1)S(1)}, bf16[4,512,128]{2,1,0:T(8,128)(2,1)S(1)}, u32[]{:S(2)}, u32[]{:S(2)}) collective-permute-start(bf16[4,512,128]{2,1,0:T(8,128)(2,1)S(1)} %fusion.31), channel_id=1, source_target_pairs={{0,2},{1,3},{2,4},{3,5},{4,6},{5,7},{6,8},{7,9},{8,10},{9,11},{10,... | collective-permute-start | bytes 1572872 | tf_op jit(solution)/shard_map/ppermute | solution.py:16
  177.2 17.8 %tanh_convert_fusion.2 = bf16[4,512,512]{1,2,0:T(8,128)(2,1)S(1)} fusion(bf16[4,512,128]{2,1,0:T(8,128)(2,1)S(1)} %copy-done, bf16[4,512,128]{2,1,0:T(8,128)(2,1)} %collective-permute-done, s32[512,512]{0,1:T(8,128)S(1)} %copy-done.7, s32[4]{0:T(128)S(1)} %copy-done.10), kind=kOutput, calls=%fused_computation.46 | convolution fusion | flops 287309824 | bytes 4194320 | tf_op jit(solution)/shard_map/fik,fjk->fij/dot_general | solution.py:25
  196.5 2.8 %collective-permute-start.6 = (bf16[4,512,128]{2,1,0:T(8,128)(2,1)S(1)}, bf16[4,512,128]{2,1,0:T(8,128)(2,1)S(1)}, u32[]{:S(2)}, u32[]{:S(2)}) collective-permute-start(bf16[4,512,128]{2,1,0:T(8,128)(2,1)S(1)} %fusion.30), channel_id=1, source_target_pairs={{0,1},{1,2},{2,3},{3,4},{4,5},{5,6},{6,7},{7,8},{8,9},{9,10},{10,1... | collective-permute-start | bytes 1572872 | tf_op jit(solution)/shard_map/ppermute | solution.py:16
  199.3 1.9 convolution_add_fusion.4
  202.3 1.9 fusion.29
  205.4 3.1 %fusion.28 = f32[4,512,128]{2,1,0:T(8,128)} fusion(f32[4,512,128]{2,1,0:T(8,128)S(1)} %convolution_add_fusion.3, f32[4,512,128]{2,1,0:T(8,128)S(1)} %convolution_add_fusion.4, f32[4,512,128]{2,1,0:T(8,128)S(1)} %fusion.29, f32[4,512,128]{2,1,0:T(8,128)S(1)} %fusion.34, bf16[4,512,512]{1,2,0:T(8,128)(2,1)S(1)} %tanh_convert_fusion.1, ...), kind=kOutput, calls=%fused_computation.62 | convolution fusion | flops 271319040 | bytes 9437184 | tf_op jit(solution)/shard_map/fij,fjk->fik/dot_general | solution.py:40
  (55 shorter events, 18.8 us)
Async XLA Ops:
  0.0 20.6 %copy-start.9 = (s32[512]{0:T(512)S(1)}, s32[512]{0:T(512)}, u32[]{:S(2)}) copy-start(s32[512]{0:T(512)} %param.4) | copy-start | bytes 6148
  0.0 16.9 %copy-start = (bf16[4,512,128]{2,1,0:T(8,128)(2,1)S(1)}, bf16[4,512,128]{2,1,0:T(8,128)(2,1)}, u32[]{:S(2)}) copy-start(bf16[4,512,128]{2,1,0:T(8,128)(2,1)} %param.3) | copy-start | bytes 1572868
  0.8 16.2 %collective-permute-start.3 = (bf16[512]{0:T(512)(128)(2,1)S(1)}, bf16[512]{0:T(512)(128)(2,1)S(1)}, u32[]{:S(2)}, u32[]{:S(2)}) collective-permute-start(bf16[512]{0:T(512)(128)(2,1)S(1)} %get-tuple-element.6), channel_id=1, source_target_pairs={{2,0},{3,1},{4,2},{5,3},{6,4},{7,5},{8,6},{9,7},{10,8},{11,9},{12,... | collective-permute-start | bytes 3080 | tf_op jit(solution)/shard_map/ppermute | solution.py:16
  2.9 17.7 %collective-permute-start.1 = (bf16[512]{0:T(512)(128)(2,1)S(1)}, bf16[512]{0:T(512)(128)(2,1)S(1)}, u32[]{:S(2)}, u32[]{:S(2)}) collective-permute-start(bf16[512]{0:T(512)(128)(2,1)S(1)} %get-tuple-element.6), channel_id=1, source_target_pairs={{1,0},{2,1},{3,2},{4,3},{5,4},{6,5},{7,6},{8,7},{9,8},{10,9},{11,1... | collective-permute-start | bytes 3080 | tf_op jit(solution)/shard_map/ppermute | solution.py:16
  5.8 14.8 %collective-permute-start.5 = (bf16[512]{0:T(512)(128)(2,1)S(1)}, bf16[512]{0:T(512)(128)(2,1)S(1)}, u32[]{:S(2)}, u32[]{:S(2)}) collective-permute-start(bf16[512]{0:T(512)(128)(2,1)S(1)} %get-tuple-element.6), channel_id=1, source_target_pairs={{3,0},{4,1},{5,2},{6,3},{7,4},{8,5},{9,6},{10,7},{11,8},{12,9},{13... | collective-permute-start | bytes 3080 | tf_op jit(solution)/shard_map/ppermute | solution.py:16
  9.7 80.0 %collective-permute-start.4 = (bf16[4,512,128]{2,1,0:T(8,128)(2,1)}, bf16[4,512,128]{2,1,0:T(8,128)(2,1)}, u32[]{:S(2)}, u32[]{:S(2)}) collective-permute-start(bf16[4,512,128]{2,1,0:T(8,128)(2,1)} %param.3), channel_id=1, source_target_pairs={{3,0},{4,1},{5,2},{6,3},{7,4},{8,5},{9,6},{10,7},{11,8},{12,9},{13... | collective-permute-start | bytes 1572872 | tf_op jit(solution)/shard_map/ppermute | solution.py:16
  12.2 103.1 %collective-permute-start = (bf16[4,512,128]{2,1,0:T(8,128)(2,1)}, bf16[4,512,128]{2,1,0:T(8,128)(2,1)}, u32[]{:S(2)}, u32[]{:S(2)}) collective-permute-start(bf16[4,512,128]{2,1,0:T(8,128)(2,1)} %param.3), channel_id=1, source_target_pairs={{1,0},{2,1},{3,2},{4,3},{5,4},{6,5},{7,6},{8,7},{9,8},{10,9},{11,1... | collective-permute-start | bytes 1572872 | tf_op jit(solution)/shard_map/ppermute | solution.py:16
  14.1 8.2 %copy-start.10 = (s32[4]{0:T(128)S(1)}, s32[4]{0:T(128)}, u32[]{:S(2)}) copy-start(s32[4]{0:T(128)} %param.5) | copy-start | bytes 52
  16.9 118.8 %collective-permute-start.2 = (bf16[4,512,128]{2,1,0:T(8,128)(2,1)S(1)}, bf16[4,512,128]{2,1,0:T(8,128)(2,1)}, u32[]{:S(2)}, u32[]{:S(2)}) collective-permute-start(bf16[4,512,128]{2,1,0:T(8,128)(2,1)S(1)} %copy-done), channel_id=1, source_target_pairs={{2,0},{3,1},{4,2},{5,3},{6,4},{7,5},{8,6},{9,7},{10,8},{11,9},{12,... | collective-permute-start | bytes 1572872 | tf_op jit(solution)/shard_map/ppermute | solution.py:16
  22.4 31.8 %copy-start.2 = (s32[512,512]{0,1:T(8,128)}, s32[512,512]{0,1:T(8,128)S(1)}, u32[]{:S(2)}) copy-start(s32[512,512]{0,1:T(8,128)S(1)} %get-tuple-element.19) | copy-start | bytes 3145732
  22.4 31.8 %copy-start.4 = (s32[512,512]{0,1:T(8,128)}, s32[512,512]{0,1:T(8,128)S(1)}, u32[]{:S(2)}) copy-start(s32[512,512]{0,1:T(8,128)S(1)} %get-tuple-element.20) | copy-start | bytes 3145732
  68.5 18.4 %copy-start.5 = (bf16[4,512,64]{2,1,0:T(8,128)(2,1)S(1)}, bf16[4,512,64]{2,1,0:T(8,128)(2,1)}, u32[]{:S(2)}) copy-start(bf16[4,512,64]{2,1,0:T(8,128)(2,1)} %get-tuple-element.14) | copy-start | bytes 786436
  68.5 18.4 %copy-start.6 = (bf16[4,512,64]{2,1,0:T(8,128)(2,1)S(1)}, bf16[4,512,64]{2,1,0:T(8,128)(2,1)}, u32[]{:S(2)}) copy-start(bf16[4,512,64]{2,1,0:T(8,128)(2,1)} %get-tuple-element.16) | copy-start | bytes 786436
  88.9 2.6 %copy-start.1 = (f32[4,512,512]{2,1,0:T(8,128)S(1)}, f32[4,512,512]{2,1,0:T(8,128)}, u32[]{:S(2)}) copy-start(f32[4,512,512]{2,1,0:T(8,128)} %copy.25) | copy-start | bytes 12582916
  91.5 1.2 copy-start.3
  110.3 6.4 %copy-start.7 = (s32[512,512]{0,1:T(8,128)S(1)}, s32[512,512]{0,1:T(8,128)}, u32[]{:S(2)}) copy-start(s32[512,512]{0,1:T(8,128)} %get-tuple-element.18) | copy-start | bytes 3145732
  111.9 92.4 %collective-permute-start.8 = (bf16[4,512,128]{2,1,0:T(8,128)(2,1)S(1)}, bf16[4,512,128]{2,1,0:T(8,128)(2,1)S(1)}, u32[]{:S(2)}, u32[]{:S(2)}) collective-permute-start(bf16[4,512,128]{2,1,0:T(8,128)(2,1)S(1)} %fusion.32), channel_id=1, source_target_pairs={{0,3},{1,4},{2,5},{3,6},{4,7},{5,8},{6,9},{7,10},{8,11},{9,12},{10... | collective-permute-start | bytes 1572872 | tf_op jit(solution)/shard_map/ppermute | solution.py:16
  133.9 1.9 copy-start.8
  173.2 31.1 %collective-permute-start.7 = (bf16[4,512,128]{2,1,0:T(8,128)(2,1)S(1)}, bf16[4,512,128]{2,1,0:T(8,128)(2,1)S(1)}, u32[]{:S(2)}, u32[]{:S(2)}) collective-permute-start(bf16[4,512,128]{2,1,0:T(8,128)(2,1)S(1)} %fusion.31), channel_id=1, source_target_pairs={{0,2},{1,3},{2,4},{3,5},{4,6},{5,7},{6,8},{7,9},{8,10},{9,11},{10,... | collective-permute-start | bytes 1572872 | tf_op jit(solution)/shard_map/ppermute | solution.py:16
  196.5 9.0 %collective-permute-start.6 = (bf16[4,512,128]{2,1,0:T(8,128)(2,1)S(1)}, bf16[4,512,128]{2,1,0:T(8,128)(2,1)S(1)}, u32[]{:S(2)}, u32[]{:S(2)}) collective-permute-start(bf16[4,512,128]{2,1,0:T(8,128)(2,1)S(1)} %fusion.30), channel_id=1, source_target_pairs={{0,1},{1,2},{2,3},{3,4},{4,5},{5,6},{6,7},{7,8},{8,9},{9,10},{10,1... | collective-permute-start | bytes 1572872 | tf_op jit(solution)/shard_map/ppermute | solution.py:16
where the time goes:
time: 211 us; the launch traced here: 209 us
  matrix products  127 us (60%)
  other arithmetic  41.7 us (20%)
  starting transfers between devices  27.2 us (13%)
  local copies, waits for them, and re-layouts  10.8 us (5%)
    dot_general x4, matrix products, block_terms(): jnp.einsum('fik,fjk->fij', mine, other, preferred_element_type=jnp.float32)  55.9 us
    dot_general x4, matrix products, block_terms(): jnp.einsum('fik,fjk->fij', mine, other_swap, preferred_element_type=jnp.f...  53.6 us
    sin x1, other arithmetic, block_terms(): jnp.sin(phase)  31.8 us
    ppermute x9, starting transfers between devices, shifted(): lax.ppermute(value, axis, [(source, source + steps) for source in range(l...  27.2 us
    dot_general x4, matrix products, block_terms(): jnp.einsum('fij,fjk->fik', grad_real, other, preferred_element_type=jnp.f...  7.68 us
    sin x1, local copies, waits for them, and re-layouts, block_terms(): jnp.sin(phase)  5.34 us
    cos x1, local copies, waits for them, and re-layouts, block_terms(): jnp.cos(phase)  5.27 us
    neg x3, other arithmetic, block_terms(): -other[..., windows:]  4.64 us
  transfers between devices with their start and end apart: 9, of which 1 were waited for; matrix products, arithmetic and copies ran while one was open for 84% of the time, Pallas kernels for 0%

commit v1 on v0

v1 whole, which is shorter than its diff:
```python
import functools
import math

import jax
import jax.numpy as jnp
from jax import lax
from jax.experimental import pallas as pl
from jax.experimental.pallas import tpu as pltpu
from jax.sharding import PartitionSpec as P

spacing_metres = 8
period_metres = 4096
model_amp = 0.5
reach = 3

OWN = (0, 0)
PAIR = (1, -1)
NEXT = (2, 2)
PREV = (-2, -2)
FAR = (-3, 3)
NEXT_OF_PAIR = (3, 1)
PREV_OF_PAIR = (-1, -3)


def sine(steps):
    half, quarter = period_metres // 2, period_metres // 4
    turn = jnp.bitwise_and(steps + half, period_metres - 1) - half
    turn = jnp.where(turn > quarter, half - turn, jnp.where(turn < -quarter, -half - turn, turn))
    x = turn.astype(jnp.float32) * (2.0 * math.pi / period_metres)
    square = x * x
    total = jnp.full_like(x, -1.0 / math.factorial(11))
    for order in (9, 7, 5, 3, 1):
        total = total * square + (-1.0) ** (order // 2) / math.factorial(order)
    return total * x


def halves(value):
    high = value.astype(jnp.bfloat16).astype(jnp.float32)
    return high, value - high


def rows_of(freqs):
    return -(-2 * freqs // 8) * 8


def angles(bins_ref, off_ref, block, freqs, channels):
    shape = (rows_of(freqs), channels)
    row = lax.broadcasted_iota(jnp.int32, shape, 0)
    offsets = off_ref[...].astype(jnp.float32)
    lines = channels // offsets.shape[1]
    offsets = jnp.concatenate([offsets[i : i + 1] for i in range(lines)], axis=1).astype(jnp.int32)
    channel = lax.broadcasted_iota(jnp.int32, shape, 1) + block * channels
    pos = channel * spacing_metres + offsets
    factor = jnp.zeros(shape, jnp.int32)
    for f in range(freqs):
        factor = jnp.where((row == f) | (row == freqs + f), bins_ref[f], factor)
    return factor * pos, row < freqs


def columns(parts, width):
    rows = jnp.concatenate(parts, axis=0)
    rows = jnp.concatenate(
        [rows, jnp.zeros((width - rows.shape[0], rows.shape[1]), jnp.float32)], axis=0
    )
    return rows.T.astype(jnp.bfloat16)


def key_columns(bins_ref, off_ref, block, freqs, channels, width):
    angle, is_cos = angles(bins_ref, off_ref, block, freqs, channels)
    high, low = halves(sine(angle + jnp.where(is_cos, period_metres // 4, 0)))
    return columns([high, low, high, low], width)


def query_columns(bins_ref, off_ref, block, freqs, channels, width):
    angle, is_cos = angles(bins_ref, off_ref, block, freqs, channels)
    quarter = period_metres // 4
    high, low = halves(-model_amp * sine(angle + jnp.where(is_cos, quarter, 0)))
    real = columns([high, high, low, low], width)
    high, low = halves(model_amp * sine(angle - jnp.where(is_cos, 0, quarter)))
    imag = columns([high, high, low, low], width)
    return real, imag


def turned(value):
    width = value.shape[1]
    lane = lax.broadcasted_iota(jnp.int32, value.shape, 1)
    moved = pltpu.roll(value, width // 2, 1)
    return jnp.where(lane < width // 2, -moved, moved)


def band_kernel(freqs, places, weight, axis, has_total, *refs):
    count = len(places)
    bins_ref, own_ref, own_off_ref = refs[:3]
    key_refs = refs[3 : 3 + 2 * count]
    total_ref = refs[3 + 2 * count] if has_total else None
    out_ref, query_ref = refs[3 + 2 * count + has_total :]
    width = own_ref.shape[1]
    channels = out_ref.shape[1]
    windows = width // 2
    me = lax.axis_index(axis)
    odd = lax.rem(me, 2)
    real, imag = query_columns(bins_ref, own_off_ref, me, freqs, channels, width)
    lane = lax.broadcasted_iota(jnp.int32, (channels, width), 1)
    period = rows_of(freqs)
    lane_row = lax.rem(lane, period)
    used = lane < 4 * period
    extra = []
    for (even_step, odd_step), off_ref in zip(places, key_refs[1::2]):
        block = me + even_step + odd * (odd_step - even_step)
        extra.append(key_columns(bins_ref, off_ref, block, freqs, channels, width))
    zero = jnp.zeros((), jnp.bfloat16)
    for f in range(freqs):
        rows = pl.ds(f * channels, channels)
        own = own_ref[rows, :].astype(jnp.float32) / windows
        mine = used & ((lane_row == f) | (lane_row == freqs + f))
        query_ref[f, :channels, :width] = own.astype(jnp.bfloat16)
        query_ref[f, channels:, :width] = (-turned(own)).astype(jnp.bfloat16)
        query_ref[f, :channels, width:] = jnp.where(mine, real, zero)
        query_ref[f, channels:, width:] = jnp.where(mine, imag, zero)
    for f in range(freqs):
        rows = pl.ds(f * channels, channels)
        sums = []
        for half in range(2):
            query = query_ref[f, pl.ds(half * channels, channels), :]
            part = None
            for key_ref, columns_j in zip(key_refs[0::2], extra):
                key = key_ref[rows, :]
                misfit = lax.dot_general(
                    query,
                    jnp.concatenate([key, columns_j], axis=1),
                    (((1,), (1,)), ((), ())),
                    preferred_element_type=jnp.float32,
                )
                grad = jnp.tanh(misfit).astype(jnp.bfloat16)
                term = jnp.dot(grad, key, preferred_element_type=jnp.float32)
                part = term if part is None else part + term
            sums.append(part)
        term = (sums[0] + turned(sums[1])) * (weight / windows)
        if has_total:
            term = term + total_ref[f]
        out_ref[f] = term


def band_terms(shape, axis, bins, own, keys, places, weight=1, total=None):
    freqs, channels, width = shape
    tail_rows = own.shape[0] - freqs * channels
    whole = pl.BlockSpec((freqs * channels, width), lambda i: (0, 0))
    tail = pl.BlockSpec((tail_rows, width), lambda i: (freqs * channels // tail_rows, 0))
    plain = pl.BlockSpec((freqs, channels, width), lambda i: (0, 0, 0))
    has_total = total is not None
    operands = [bins, own, own]
    specs = [pl.BlockSpec(memory_space=pltpu.SMEM), whole, tail]
    for key in keys:
        operands += [key, key]
        specs += [whole, tail]
    if has_total:
        operands.append(total)
        specs.append(plain)
    pairs = len(keys) * freqs * channels * channels
    return pl.pallas_call(
        functools.partial(band_kernel, freqs, tuple(places), weight, axis, has_total),
        grid=(1,),
        out_shape=jax.ShapeDtypeStruct(shape, jnp.float32),
        in_specs=specs,
        out_specs=plain,
        scratch_shapes=[pltpu.VMEM((freqs, 2 * channels, 2 * width), jnp.bfloat16)],
        input_output_aliases={len(operands) - 1: 0} if has_total else {},
        compiler_params=pltpu.CompilerParams(vmem_limit_bytes=40 << 20),
        cost_estimate=pl.CostEstimate(
            flops=16 * pairs * width, bytes_accessed=1 << 21, transcendentals=2 * pairs
        ),
    )(*operands)


def local(axis, count, spectra, offsets, bins):
    shape = spectra.shape
    freqs, channels, width = shape

    def moved(value, target):
        pairs = [(i, target(i)) for i in range(count)]
        return lax.ppermute(value, axis, [(i, t) for i, t in pairs if 0 <= t < count])

    lines = channels // width
    tail = jnp.zeros((-(-lines // 16) * 16, width), jnp.bfloat16)
    tail = tail.at[:lines].set(offsets.astype(jnp.bfloat16).reshape(lines, width))
    own = jnp.concatenate([spectra.reshape(freqs * channels, width), tail], axis=0)

    nxt = moved(own, lambda i: i - 2)
    prev = moved(own, lambda i: i + 2)
    far = moved(own, lambda i: i + 3 if i % 2 else i - 3)
    pair = moved(own, lambda i: i ^ 1)
    nxt_pair = moved(nxt, lambda i: i ^ 1)
    prev_pair = moved(prev, lambda i: i ^ 1)

    terms = functools.partial(band_terms, shape, axis, bins, own)
    total = terms([own], [OWN], weight=2)
    total = terms([pair], [PAIR], total=total)
    total = terms([nxt], [NEXT], total=total)
    total = terms([nxt_pair, far], [NEXT_OF_PAIR, FAR], total=total)
    total = terms([prev], [PREV], total=total)
    total = terms([prev_pair], [PREV_OF_PAIR], total=total)
    return total


def solution(mesh):
    (axis,) = mesh.axis_names
    return jax.shard_map(
        functools.partial(local, axis, mesh.shape[axis]),
        mesh=mesh,
        in_specs=(P(None, axis, None), P(axis), P()),
        out_specs=P(None, axis, None),
        check_vma=False,
    )
```

time: 211 us -> 62.9 us (0.30)
  the two profiles are of different devices: /device:TPU:19 before, /device:TPU:21 now
where the time goes in v1:
time: 62.9 us; the launch traced here: 62.5 us
  Pallas kernels  31.5 us (50%)
  starting transfers between devices  15.2 us (24%)
  waiting for transfers between devices  13.9 us (22%)
  other arithmetic  1.77 us (3%)
    pallas_call x6, Pallas kernels, band_terms(): pl.pallas_call(functools.partial(band_kernel, freqs, tuple(places), weigh...  31.5 us
    ppermute x6, starting transfers between devices, moved(): lax.ppermute(value, axis, [(i, t) for i, t in pairs if 0 <= t < count])  15.2 us
    ppermute x6, waiting for transfers between devices, moved(): lax.ppermute(value, axis, [(i, t) for i, t in pairs if 0 <= t < count])  13.9 us
  transfers between devices with their start and end apart: 6, of which 1 were waited for; matrix products, arithmetic and copies ran while one was open for 0% of the time, Pallas kernels for 43%

profile of v1, /device:TPU:21, one launch (start us, length us, event | category | flops | bytes accessed | tf_op | source)
XLA Modules:
  0.0 62.5 jit_solution(17435366472290189554)
XLA Ops:
  0.0 0.0 copy-start
  0.0 0.7 %convert_bitcast_fusion = bf16[4,128]{1,0:T(4,128)(2,1)S(1)} fusion(s32[512]{0:T(512)} %param.6), kind=kLoop, calls=%fused_computation.3 | loop fusion | flops 512 | bytes 3072 | tf_op jit(solution)/shard_map/reshape.20
  0.7 1.1 %fusion.1.refs_1_.refs_2_.refs_3_.refs_4_ = bf16[2064,128]{1,0:T(8,128)(2,1)S(1)} fusion(bf16[4,128]{1,0:T(4,128)(2,1)S(1)} %convert_bitcast_fusion, bf16[2048,128]{1,0:T(8,128)(2,1)} %bitcast.3), kind=kLoop, calls=%fused_computation.2 | loop fusion | flops 1585152 | bytes 1053696 | tf_op jit(solution)/shard_map/concatenate | solution.py:186
  1.8 3.1 %collective-permute-start.2 = (bf16[2064,128]{1,0:T(8,128)(2,1)S(1)}, bf16[2064,128]{1,0:T(8,128)(2,1)S(1)}, u32[]{:S(2)}, u32[]{:S(2)}) collective-permute-start(bf16[2064,128]{1,0:T(8,128)(2,1)S(1)} %fusion.1.refs_1_.refs_2_.refs_3_.refs_4_), channel_id=1, source_target_pairs={{2,0},{3,1},{4,2},{5,3},{6,4},{7,5},{8,6},{9,7},{10,8},{11,9},{12,... | collective-permute-start | bytes 1585160 | tf_op jit(solution)/shard_map/ppermute | solution.py:181
  4.8 2.2 %collective-permute-start = (bf16[2064,128]{1,0:T(8,128)(2,1)S(1)}, bf16[2064,128]{1,0:T(8,128)(2,1)S(1)}, u32[]{:S(2)}, u32[]{:S(2)}) collective-permute-start(bf16[2064,128]{1,0:T(8,128)(2,1)S(1)} %fusion.1.refs_1_.refs_2_.refs_3_.refs_4_), channel_id=1, source_target_pairs={{0,2},{1,3},{2,4},{3,5},{4,6},{5,7},{6,8},{7,9},{8,10},{9,11},{10,... | collective-permute-start | bytes 1585160 | tf_op jit(solution)/shard_map/ppermute | solution.py:181
  7.1 1.3 %collective-permute-start.5 = (bf16[2064,128]{1,0:T(8,128)(2,1)S(1)}, bf16[2064,128]{1,0:T(8,128)(2,1)S(1)}, u32[]{:S(2)}, u32[]{:S(2)}) collective-permute-start(bf16[2064,128]{1,0:T(8,128)(2,1)S(1)} %fusion.1.refs_1_.refs_2_.refs_3_.refs_4_), channel_id=1, source_target_pairs={{0,1},{1,0},{2,3},{3,2},{4,5},{5,4},{6,7},{7,6},{8,9},{9,8},{10,11... | collective-permute-start | bytes 1585160 | tf_op jit(solution)/shard_map/ppermute | solution.py:181
  8.4 3.4 %collective-permute-start.4 = (bf16[2064,128]{1,0:T(8,128)(2,1)S(1)}, bf16[2064,128]{1,0:T(8,128)(2,1)S(1)}, u32[]{:S(2)}, u32[]{:S(2)}) collective-permute-start(bf16[2064,128]{1,0:T(8,128)(2,1)S(1)} %fusion.1.refs_1_.refs_2_.refs_3_.refs_4_), channel_id=1, source_target_pairs={{1,4},{3,6},{4,1},{5,8},{6,3},{7,10},{8,5},{9,12},{10,7},{11,14},{... | collective-permute-start | bytes 1585160 | tf_op jit(solution)/shard_map/ppermute | solution.py:181
  11.8 13.9 %collective-permute-done.2.refs_3_.refs_4_ = bf16[2064,128]{1,0:T(8,128)(2,1)S(1)} collective-permute-done((bf16[2064,128]{1,0:T(8,128)(2,1)S(1)}, bf16[2064,128]{1,0:T(8,128)(2,1)S(1)}, u32[]{:S(2)}, u32[]{:S(2)}) %collective-permute-start.2) | collective-permute-done | bytes 528416 | tf_op jit(solution)/shard_map/ppermute | solution.py:181
  25.7 3.7 %collective-permute-start.3 = (bf16[2064,128]{1,0:T(8,128)(2,1)S(1)}, bf16[2064,128]{1,0:T(8,128)(2,1)S(1)}, u32[]{:S(2)}, u32[]{:S(2)}) collective-permute-start(bf16[2064,128]{1,0:T(8,128)(2,1)S(1)} %collective-permute-done.2.refs_3_.refs_4_), channel_id=1, source_target_pairs={{0,1},{1,0},{2,3},{3,2},{4,5},{5,4},{6,7},{7,6},{8,9},{9,8},{10,11... | collective-permute-start | bytes 1585160 | tf_op jit(solution)/shard_map/ppermute | solution.py:181
  29.4 0.0 copy-done
  29.4 4.2 %shard_map.37.refs_5_ = f32[4,512,128]{2,1,0:T(8,128)} custom-call(s32[4]{0:T(128)S(1)} %copy-done, bf16[2064,128]{1,0:T(8,128)(2,1)S(1)} %fusion.1.refs_1_.refs_2_.refs_3_.refs_4_, bf16[2064,128]{1,0:T(8,128)(2,1)S(1)} %fusion.1.refs_1_.refs_2_.refs_3_.refs_4_, bf16[2064,128]{1,0:T(8,128)(2,1)S(1)} %fusion.1.refs_1_.refs_2_.refs_3_.refs_4_, ...), custom_call_target="tpu_custom_call" | custom-call | flops 2147483648 | bytes 2097152 | tf_op jit(solution)/shard_map/pallas_call | solution.py:160
  33.6 0.0 collective-permute-done.refs_3_.refs_4_
  33.6 1.6 %collective-permute-start.1 = (bf16[2064,128]{1,0:T(8,128)(2,1)S(1)}, bf16[2064,128]{1,0:T(8,128)(2,1)S(1)}, u32[]{:S(2)}, u32[]{:S(2)}) collective-permute-start(bf16[2064,128]{1,0:T(8,128)(2,1)S(1)} %collective-permute-done.refs_3_.refs_4_), channel_id=1, source_target_pairs={{0,1},{1,0},{2,3},{3,2},{4,5},{5,4},{6,7},{7,6},{8,9},{9,8},{10,11... | collective-permute-start | bytes 1585160 | tf_op jit(solution)/shard_map/ppermute | solution.py:181
  35.1 0.0 collective-permute-done.5.refs_3_.refs_4_
  35.1 4.9 %shard_map.38.refs_5_ = f32[4,512,128]{2,1,0:T(8,128)} custom-call(s32[4]{0:T(128)S(1)} %copy-done, bf16[2064,128]{1,0:T(8,128)(2,1)S(1)} %fusion.1.refs_1_.refs_2_.refs_3_.refs_4_, bf16[2064,128]{1,0:T(8,128)(2,1)S(1)} %fusion.1.refs_1_.refs_2_.refs_3_.refs_4_, ...), custom_call_target="tpu_custom_call", output_to_operand_aliasing={{}: (5, {})} | custom-call | flops 2147483648 | bytes 2097152 | tf_op jit(solution)/shard_map/pallas_call | solution.py:160
  40.1 4.9 %shard_map.39.refs_7_ = f32[4,512,128]{2,1,0:T(8,128)} custom-call(s32[4]{0:T(128)S(1)} %copy-done, bf16[2064,128]{1,0:T(8,128)(2,1)S(1)} %fusion.1.refs_1_.refs_2_.refs_3_.refs_4_, bf16[2064,128]{1,0:T(8,128)(2,1)S(1)} %fusion.1.refs_1_.refs_2_.refs_3_.refs_4_, ...), custom_call_target="tpu_custom_call", output_to_operand_aliasing={{}: (5, {})} | custom-call | flops 2147483648 | bytes 2097152 | tf_op jit(solution)/shard_map/pallas_call | solution.py:160
  45.0 0.0 collective-permute-done.4.refs_5_.refs_6_
  45.0 0.0 collective-permute-done.3.refs_3_.refs_4_
  45.0 7.6 %shard_map.40.refs_5_ = f32[4,512,128]{2,1,0:T(8,128)} custom-call(s32[4]{0:T(128)S(1)} %copy-done, bf16[2064,128]{1,0:T(8,128)(2,1)S(1)} %fusion.1.refs_1_.refs_2_.refs_3_.refs_4_, bf16[2064,128]{1,0:T(8,128)(2,1)S(1)} %fusion.1.refs_1_.refs_2_.refs_3_.refs_4_, ...), custom_call_target="tpu_custom_call", output_to_operand_aliasing={{}: (7, {})} | custom-call | flops 4294967296 | bytes 2097152 | tf_op jit(solution)/shard_map/pallas_call | solution.py:160
  52.6 4.9 %shard_map.41.refs_5_ = f32[4,512,128]{2,1,0:T(8,128)} custom-call(s32[4]{0:T(128)S(1)} %copy-done, bf16[2064,128]{1,0:T(8,128)(2,1)S(1)} %fusion.1.refs_1_.refs_2_.refs_3_.refs_4_, bf16[2064,128]{1,0:T(8,128)(2,1)S(1)} %fusion.1.refs_1_.refs_2_.refs_3_.refs_4_, ...), custom_call_target="tpu_custom_call", output_to_operand_aliasing={{}: (5, {})} | custom-call | flops 2147483648 | bytes 2097152 | tf_op jit(solution)/shard_map/pallas_call | solution.py:160
  57.6 0.0 collective-permute-done.1.refs_3_.refs_4_
  57.6 4.9 %shard_map.42 = f32[4,512,128]{2,1,0:T(8,128)} custom-call(s32[4]{0:T(128)S(1)} %copy-done, bf16[2064,128]{1,0:T(8,128)(2,1)S(1)} %fusion.1.refs_1_.refs_2_.refs_3_.refs_4_, bf16[2064,128]{1,0:T(8,128)(2,1)S(1)} %fusion.1.refs_1_.refs_2_.refs_3_.refs_4_, ...), custom_call_target="tpu_custom_call", output_to_operand_aliasing={{}: (5, {})} | custom-call | flops 2147483648 | bytes 2097152 | tf_op jit(solution)/shard_map/pallas_call | solution.py:160
Async XLA Ops:
  0.0 29.4 %copy-start = (s32[4]{0:T(128)S(1)}, s32[4]{0:T(128)}, u32[]{:S(2)}) copy-start(s32[4]{0:T(128)} %refs_0_.11) | copy-start | bytes 52
  1.8 23.9 %collective-permute-start.2 = (bf16[2064,128]{1,0:T(8,128)(2,1)S(1)}, bf16[2064,128]{1,0:T(8,128)(2,1)S(1)}, u32[]{:S(2)}, u32[]{:S(2)}) collective-permute-start(bf16[2064,128]{1,0:T(8,128)(2,1)S(1)} %fusion.1.refs_1_.refs_2_.refs_3_.refs_4_), channel_id=1, source_target_pairs={{2,0},{3,1},{4,2},{5,3},{6,4},{7,5},{8,6},{9,7},{10,8},{11,9},{12,... | collective-permute-start | bytes 1585160 | tf_op jit(solution)/shard_map/ppermute | solution.py:181
  4.8 28.7 %collective-permute-start = (bf16[2064,128]{1,0:T(8,128)(2,1)S(1)}, bf16[2064,128]{1,0:T(8,128)(2,1)S(1)}, u32[]{:S(2)}, u32[]{:S(2)}) collective-permute-start(bf16[2064,128]{1,0:T(8,128)(2,1)S(1)} %fusion.1.refs_1_.refs_2_.refs_3_.refs_4_), channel_id=1, source_target_pairs={{0,2},{1,3},{2,4},{3,5},{4,6},{5,7},{6,8},{7,9},{8,10},{9,11},{10,... | collective-permute-start | bytes 1585160 | tf_op jit(solution)/shard_map/ppermute | solution.py:181
  7.1 28.1 %collective-permute-start.5 = (bf16[2064,128]{1,0:T(8,128)(2,1)S(1)}, bf16[2064,128]{1,0:T(8,128)(2,1)S(1)}, u32[]{:S(2)}, u32[]{:S(2)}) collective-permute-start(bf16[2064,128]{1,0:T(8,128)(2,1)S(1)} %fusion.1.refs_1_.refs_2_.refs_3_.refs_4_), channel_id=1, source_target_pairs={{0,1},{1,0},{2,3},{3,2},{4,5},{5,4},{6,7},{7,6},{8,9},{9,8},{10,11... | collective-permute-start | bytes 1585160 | tf_op jit(solution)/shard_map/ppermute | solution.py:181
  8.4 36.6 %collective-permute-start.4 = (bf16[2064,128]{1,0:T(8,128)(2,1)S(1)}, bf16[2064,128]{1,0:T(8,128)(2,1)S(1)}, u32[]{:S(2)}, u32[]{:S(2)}) collective-permute-start(bf16[2064,128]{1,0:T(8,128)(2,1)S(1)} %fusion.1.refs_1_.refs_2_.refs_3_.refs_4_), channel_id=1, source_target_pairs={{1,4},{3,6},{4,1},{5,8},{6,3},{7,10},{8,5},{9,12},{10,7},{11,14},{... | collective-permute-start | bytes 1585160 | tf_op jit(solution)/shard_map/ppermute | solution.py:181
  25.7 19.3 %collective-permute-start.3 = (bf16[2064,128]{1,0:T(8,128)(2,1)S(1)}, bf16[2064,128]{1,0:T(8,128)(2,1)S(1)}, u32[]{:S(2)}, u32[]{:S(2)}) collective-permute-start(bf16[2064,128]{1,0:T(8,128)(2,1)S(1)} %collective-permute-done.2.refs_3_.refs_4_), channel_id=1, source_target_pairs={{0,1},{1,0},{2,3},{3,2},{4,5},{5,4},{6,7},{7,6},{8,9},{9,8},{10,11... | collective-permute-start | bytes 1585160 | tf_op jit(solution)/shard_map/ppermute | solution.py:181
  33.6 24.0 %collective-permute-start.1 = (bf16[2064,128]{1,0:T(8,128)(2,1)S(1)}, bf16[2064,128]{1,0:T(8,128)(2,1)S(1)}, u32[]{:S(2)}, u32[]{:S(2)}) collective-permute-start(bf16[2064,128]{1,0:T(8,128)(2,1)S(1)} %collective-permute-done.refs_3_.refs_4_), channel_id=1, source_target_pairs={{0,1},{1,0},{2,3},{3,2},{4,5},{5,4},{6,7},{7,6},{8,9},{9,8},{10,11... | collective-permute-start | bytes 1585160 | tf_op jit(solution)/shard_map/ppermute | solution.py:181

commit v2 on v1

v2 whole, which is shorter than its diff:
```python
import functools
import math

import jax
import jax.numpy as jnp
from jax import lax
from jax.experimental import pallas as pl
from jax.experimental.pallas import tpu as pltpu
from jax.sharding import PartitionSpec as P

spacing_metres = 8
period_metres = 4096
model_amp = 0.5
vmem = 24 << 20

OWN = (0, 0)
PAIR = (1, -1)
NEXT = (2, 2)
PREV = (-2, -2)
FAR = (-3, 3)
NEXT_OF_PAIR = (3, 1)
PREV_OF_PAIR = (-1, -3)


def sine(steps):
    half, quarter = period_metres // 2, period_metres // 4
    turn = jnp.bitwise_and(steps + half, period_metres - 1) - half
    turn = jnp.where(turn > quarter, half - turn, jnp.where(turn < -quarter, -half - turn, turn))
    x = turn.astype(jnp.float32) * (2.0 * math.pi / period_metres)
    square = x * x
    total = jnp.full_like(x, -1.0 / math.factorial(11))
    for order in (9, 7, 5, 3, 1):
        total = total * square + (-1.0) ** (order // 2) / math.factorial(order)
    return total * x


def halves(value):
    high = value.astype(jnp.bfloat16).astype(jnp.float32)
    return high, value - high


def rows_of(freqs):
    return -(-2 * freqs // 8) * 8


def angles(tail_ref, block, freqs, channels):
    rows, width = rows_of(freqs), tail_ref.shape[1]
    row = lax.broadcasted_iota(jnp.int32, (rows, channels), 0)
    tail = tail_ref[...].astype(jnp.float32)
    lines = channels // width
    offsets = jnp.concatenate([tail[i : i + 1] for i in range(lines)], axis=1).astype(jnp.int32)
    factor = jnp.concatenate([tail[-rows:]] * lines, axis=1).astype(jnp.int32)
    channel = lax.broadcasted_iota(jnp.int32, (rows, channels), 1) + block * channels
    return factor * (channel * spacing_metres + offsets), row < freqs


def columns(parts, width):
    rows = jnp.concatenate(parts, axis=0)
    rows = jnp.concatenate(
        [rows, jnp.zeros((width - rows.shape[0], rows.shape[1]), jnp.float32)], axis=0
    )
    return rows.T.astype(jnp.bfloat16)


def key_columns(tail_ref, block, freqs, channels, width):
    angle, is_cos = angles(tail_ref, block, freqs, channels)
    high, low = halves(sine(angle + jnp.where(is_cos, period_metres // 4, 0)))
    return columns([high, low, high, low], width)


def query_columns(tail_ref, block, freqs, channels, width):
    angle, is_cos = angles(tail_ref, block, freqs, channels)
    quarter = period_metres // 4
    high, low = halves(-model_amp * sine(angle + jnp.where(is_cos, quarter, 0)))
    real = columns([high, high, low, low], width)
    high, low = halves(model_amp * sine(angle - jnp.where(is_cos, 0, quarter)))
    imag = columns([high, high, low, low], width)
    return real, imag


def turned(value):
    width = value.shape[1]
    lane = lax.broadcasted_iota(jnp.int32, value.shape, 1)
    moved = pltpu.roll(value, width // 2, 1)
    return jnp.where(lane < width // 2, -moved, moved)


def block_of(axis, place):
    me = lax.axis_index(axis)
    return me + place[0] + lax.rem(me, 2) * (place[1] - place[0])


def pack_kernel(spectra_ref, off_ref, bins_ref, out_ref, off, bins, sems):
    rows, width = spectra_ref.shape
    freqs = bins_ref.shape[0]
    sources, targets = (spectra_ref, off_ref, bins_ref), (out_ref.at[pl.ds(0, rows)], off, bins)
    copies = [pltpu.make_async_copy(a, b, sems.at[i]) for i, (a, b) in enumerate(zip(sources, targets))]
    for copy in copies:
        copy.start()
    for copy in copies[1:]:
        copy.wait()
    tail = (out_ref.shape[0] - rows, width)
    row = lax.broadcasted_iota(jnp.int32, tail, 0)
    value = jnp.zeros(tail, jnp.int32)
    for i in range(off.shape[1] // width):
        value = jnp.where(row == i, off[:, i * width : (i + 1) * width], value)
    first = tail[0] - rows_of(freqs)
    for f in range(freqs):
        value = jnp.where((row == first + f) | (row == first + freqs + f), bins[f], value)
    out_ref[rows:, :] = value.astype(jnp.float32).astype(jnp.bfloat16)
    copies[0].wait()


def pack(spectra, offsets, bins):
    freqs, channels, width = spectra.shape
    tail = -(-(channels // width + rows_of(freqs)) // 16) * 16
    return pl.pallas_call(
        pack_kernel,
        out_shape=jax.ShapeDtypeStruct((freqs * channels + tail, width), spectra.dtype),
        in_specs=[pl.BlockSpec(memory_space=pltpu.HBM)] * 3,
        out_specs=pl.BlockSpec(memory_space=pltpu.VMEM),
        scratch_shapes=[
            pltpu.VMEM((1, channels), jnp.int32),
            pltpu.SMEM((freqs,), jnp.int32),
            pltpu.SemaphoreType.DMA((3,)),
        ],
        compiler_params=pltpu.CompilerParams(vmem_limit_bytes=vmem),
        cost_estimate=pl.CostEstimate(flops=0, bytes_accessed=1 << 20, transcendentals=0),
    )(
        *(
            pltpu.with_memory_space_constraint(value, pltpu.HBM)
            for value in (spectra.reshape(freqs * channels, width), offsets.reshape(1, channels), bins)
        )
    )


def fill_queries(own_ref, query_ref, block):
    freqs, channels, width = query_ref.shape[0], query_ref.shape[1] // 2, own_ref.shape[1]
    windows = width // 2
    real, imag = query_columns(
        own_ref.at[pl.ds(freqs * channels, own_ref.shape[0] - freqs * channels)],
        block,
        freqs,
        channels,
        width,
    )
    lane = lax.broadcasted_iota(jnp.int32, (channels, width), 1)
    lane_row = lax.rem(lane, rows_of(freqs))
    used = lane < 4 * rows_of(freqs)
    zero = jnp.zeros((), jnp.bfloat16)
    for f in range(freqs):
        own = own_ref[pl.ds(f * channels, channels), :].astype(jnp.float32) / windows
        mine = used & ((lane_row == f) | (lane_row == freqs + f))
        query_ref[f, :channels, :width] = own.astype(jnp.bfloat16)
        query_ref[f, channels:, :width] = (-turned(own)).astype(jnp.bfloat16)
        query_ref[f, :channels, width:] = jnp.where(mine, real, zero)
        query_ref[f, channels:, width:] = jnp.where(mine, imag, zero)


def band_sums(query_ref, keys, f, extra):
    channels, width = query_ref.shape[1] // 2, query_ref.shape[2] // 2
    sums = []
    for half in range(2):
        query = query_ref[f, pl.ds(half * channels, channels), :]
        part = None
        for key_ref, columns_j in zip(keys, extra):
            key = key_ref[pl.ds(f * channels, channels), :]
            misfit = lax.dot_general(
                query,
                jnp.concatenate([key, columns_j], axis=1),
                (((1,), (1,)), ((), ())),
                preferred_element_type=jnp.float32,
            )
            grad = jnp.tanh(misfit).astype(jnp.bfloat16)
            term = jnp.dot(grad, key, preferred_element_type=jnp.float32)
            part = term if part is None else part + term
        sums.append(part)
    return sums[0] + turned(sums[1])


def columns_of(key_ref, block, freqs, channels, width):
    tail_ref = key_ref.at[pl.ds(freqs * channels, key_ref.shape[0] - freqs * channels)]
    return key_columns(tail_ref, block, freqs, channels, width)


def own_kernel(axis, own_ref, query_ref, total_ref):
    freqs, channels, width = total_ref.shape
    block = block_of(axis, OWN)
    extra = columns_of(own_ref, block, freqs, channels, width)
    fill_queries(own_ref, query_ref, block)
    for f in range(freqs):
        term = band_sums(query_ref, [own_ref], f, [extra])
        total_ref[f] = term * (4.0 / width)


def band_kernel(axis, places, last, query_ref, *refs):
    keys, (total_ref, out_ref) = refs[: len(places)], refs[len(places) : len(places) + 2]
    freqs, channels, width = total_ref.shape
    extra = [
        columns_of(key_ref, block_of(axis, place), freqs, channels, width)
        for key_ref, place in zip(keys, places)
    ]
    copies = []
    for f in range(freqs):
        term = band_sums(query_ref, keys, f, extra)
        term = total_ref[f] + term * (2.0 / width)
        if last:
            result_ref, sems = refs[len(places) + 2 :]
            result_ref[f] = term
            copies.append(pltpu.make_async_copy(result_ref.at[f], out_ref.at[f], sems.at[f]))
            copies[f].start()
        else:
            out_ref[f] = term
    for copy in copies:
        copy.wait()


def cost(shape, blocks):
    pairs = blocks * shape[0] * shape[1] * shape[1]
    return pl.CostEstimate(
        flops=64 * pairs * shape[2], bytes_accessed=1 << 21, transcendentals=2 * pairs
    )


def own_terms(shape, axis, own):
    freqs, channels, width = shape
    whole = pl.BlockSpec(memory_space=pltpu.VMEM)
    return pl.pallas_call(
        functools.partial(own_kernel, axis),
        out_shape=[
            jax.ShapeDtypeStruct((freqs, 2 * channels, 2 * width), jnp.bfloat16),
            jax.ShapeDtypeStruct(shape, jnp.float32),
        ],
        in_specs=[whole],
        out_specs=[whole, whole],
        compiler_params=pltpu.CompilerParams(vmem_limit_bytes=vmem),
        cost_estimate=cost(shape, 1),
    )(own)


def band_terms(shape, axis, query, total, keys, places, last=False):
    whole = pl.BlockSpec(memory_space=pltpu.VMEM)
    scratch = [pltpu.VMEM(shape, jnp.float32), pltpu.SemaphoreType.DMA((shape[0],))]
    return pl.pallas_call(
        functools.partial(band_kernel, axis, tuple(places), last),
        out_shape=jax.ShapeDtypeStruct(shape, jnp.float32),
        in_specs=[whole] * (len(keys) + 2),
        out_specs=pl.BlockSpec(memory_space=pl.ANY) if last else whole,
        scratch_shapes=scratch if last else [],
        compiler_params=pltpu.CompilerParams(vmem_limit_bytes=vmem),
        cost_estimate=cost(shape, len(keys)),
    )(query, *keys, total)


def local(axis, count, spectra, offsets, bins):
    shape = spectra.shape

    def moved(value, target):
        pairs = [(i, target(i)) for i in range(count)]
        return lax.ppermute(value, axis, [(i, t) for i, t in pairs if 0 <= t < count])

    own = pack(spectra, offsets, bins)
    nxt = moved(own, lambda i: i - 2)
    prev = moved(own, lambda i: i + 2)
    far = moved(own, lambda i: i + 3 if i % 2 else i - 3)
    pair = moved(own, lambda i: i ^ 1)

    query, total = own_terms(shape, axis, own)
    terms = functools.partial(band_terms, shape, axis, query)
    total = terms(total, [pair], [PAIR])
    nxt, total = lax.optimization_barrier((nxt, total))
    nxt_pair = moved(nxt, lambda i: i ^ 1)
    total = terms(total, [nxt], [NEXT])
    total = terms(total, [nxt_pair, far], [NEXT_OF_PAIR, FAR])
    prev, total = lax.optimization_barrier((prev, total))
    prev_pair = moved(prev, lambda i: i ^ 1)
    total = terms(total, [prev], [PREV])
    total = terms(total, [prev_pair], [PREV_OF_PAIR], last=True)
    return total


def solution(mesh):
    (axis,) = mesh.axis_names
    return jax.shard_map(
        functools.partial(local, axis, mesh.shape[axis]),
        mesh=mesh,
        in_specs=(P(None, axis, None), P(axis), P()),
        out_specs=P(None, axis, None),
        check_vma=False,
    )
```

time: 62.9 us -> 46.1 us (0.73)
  Pallas kernels: 31.5 us -> 20.2 us
  starting transfers between devices: 15.2 us -> 10.8 us
  other arithmetic: 1.77 us -> 0 us
  waiting for transfers between devices: 13.9 us -> 14.6 us
    pallas_call x6 -> x7, Pallas kernels: 31.5 us -> 20.2 us  [the longest x5 16.4 us: band_terms(): pl.pallas_call(functools.partial(band_kernel, axis, tuple(places), last),...]
    ppermute x6, starting transfers between devices: 15.2 us -> 10.8 us  [moved(): lax.ppermute(value, axis, [(i, t) for i, t in pairs if 0 <= t < count])]
    concatenate x1 -> x0, other arithmetic: 1.08 us -> none  [local(): jnp.concatenate([spectra.reshape(freqs * channels, width), tail], axis=0)]
    another operation x1 -> x0, other arithmetic: 0.7 us -> none
    ppermute x6, waiting for transfers between devices: 13.9 us -> 14.6 us  [moved(): lax.ppermute(value, axis, [(i, t) for i, t in pairs if 0 <= t < count])]
  transfers between devices with their start and end apart: 6 -> 6, of which waited for: 1 -> 2; matrix products, arithmetic and copies ran while one was open for 0% -> 0% of each run, Pallas kernels for 43% -> 35%
where the time goes in v2:
time: 46.1 us; the launch traced here: 45.9 us
  Pallas kernels  20.2 us (44%)
  waiting for transfers between devices  14.6 us (32%)
  starting transfers between devices  10.8 us (23%)
    pallas_call x5, Pallas kernels, band_terms(): pl.pallas_call(functools.partial(band_kernel, axis, tuple(places), last),...  16.4 us
    ppermute x6, waiting for transfers between devices, moved(): lax.ppermute(value, axis, [(i, t) for i, t in pairs if 0 <= t < count])  14.6 us
    ppermute x6, starting transfers between devices, moved(): lax.ppermute(value, axis, [(i, t) for i, t in pairs if 0 <= t < count])  10.8 us
    pallas_call x1, Pallas kernels, own_terms(): pl.pallas_call(functools.partial(own_kernel, axis), out_shape=[jax.ShapeD...  2.73 us
    pallas_call x1, Pallas kernels, pack(): pl.pallas_call(pack_kernel, out_shape=jax.ShapeDtypeStruct((freqs * chann...  1.07 us
  transfers between devices with their start and end apart: 6, of which 2 were waited for; matrix products, arithmetic and copies ran while one was open for 0% of the time, Pallas kernels for 35%

profile of v2, /device:TPU:21, one launch (start us, length us, event | category | flops | bytes accessed | tf_op | source)
XLA Modules:
  0.0 45.9 jit_solution(17270360746182494324)
XLA Ops:
  0.0 1.1 %shard_map.37.own_ref = bf16[2064,128]{1,0:T(8,128)(2,1)S(1)} custom-call(bf16[2048,128]{1,0:T(8,128)(2,1)} %bitcast.2, s32[1,512]{1,0:T(1,128)} %bitcast.3, s32[4]{0:T(128)} %bins_ref.1), custom_call_target="tpu_custom_call" | custom-call | bytes 1048576 | tf_op jit(solution)/shard_map/pallas_call | solution.py:117
  1.1 0.7 %collective-permute-start.2 = (bf16[2064,128]{1,0:T(8,128)(2,1)S(1)}, bf16[2064,128]{1,0:T(8,128)(2,1)S(1)}, u32[]{:S(2)}, u32[]{:S(2)}) collective-permute-start(bf16[2064,128]{1,0:T(8,128)(2,1)S(1)} %shard_map.37.own_ref), channel_id=1, source_target_pairs={{0,1},{1,0},{2,3},{3,2},{4,5},{5,4},{6,7},{7,6},{8,9},{9,8},{10,11... | collective-permute-start | bytes 1585160 | tf_op jit(solution)/shard_map/ppermute | solution.py:260
  1.8 3.0 %collective-permute-start.1 = (bf16[2064,128]{1,0:T(8,128)(2,1)S(1)}, bf16[2064,128]{1,0:T(8,128)(2,1)S(1)}, u32[]{:S(2)}, u32[]{:S(2)}) collective-permute-start(bf16[2064,128]{1,0:T(8,128)(2,1)S(1)} %shard_map.37.own_ref), channel_id=1, source_target_pairs={{2,0},{3,1},{4,2},{5,3},{6,4},{7,5},{8,6},{9,7},{10,8},{11,9},{12,... | collective-permute-start | bytes 1585160 | tf_op jit(solution)/shard_map/ppermute | solution.py:260
  4.9 4.2 %collective-permute-start.4 = (bf16[2064,128]{1,0:T(8,128)(2,1)S(1)}, bf16[2064,128]{1,0:T(8,128)(2,1)S(1)}, u32[]{:S(2)}, u32[]{:S(2)}) collective-permute-start(bf16[2064,128]{1,0:T(8,128)(2,1)S(1)} %shard_map.37.own_ref), channel_id=1, source_target_pairs={{1,4},{3,6},{4,1},{5,8},{6,3},{7,10},{8,5},{9,12},{10,7},{11,14},{... | collective-permute-start | bytes 1585160 | tf_op jit(solution)/shard_map/ppermute | solution.py:260
  9.1 1.9 %collective-permute-start = (bf16[2064,128]{1,0:T(8,128)(2,1)S(1)}, bf16[2064,128]{1,0:T(8,128)(2,1)S(1)}, u32[]{:S(2)}, u32[]{:S(2)}) collective-permute-start(bf16[2064,128]{1,0:T(8,128)(2,1)S(1)} %shard_map.37.own_ref), channel_id=1, source_target_pairs={{0,2},{1,3},{2,4},{3,5},{4,6},{5,7},{6,8},{7,9},{8,10},{9,11},{10,... | collective-permute-start | bytes 1585160 | tf_op jit(solution)/shard_map/ppermute | solution.py:260
  11.0 2.7 %shard_map.38 = (bf16[4,1024,256]{2,1,0:T(8,128)(2,1)S(1)}, f32[4,512,128]{2,1,0:T(8,128)S(1)}) custom-call(bf16[2064,128]{1,0:T(8,128)(2,1)S(1)} %shard_map.37.own_ref), custom_call_target="tpu_custom_call" | custom-call | flops 8589934592 | bytes 2097152 | tf_op jit(solution)/shard_map/pallas_call | solution.py:228
  13.8 0.0 collective-permute-done.2.refs_0_
  13.8 2.6 %shard_map.39.refs_1_ = f32[4,512,128]{2,1,0:T(8,128)S(1)} custom-call(bf16[4,1024,256]{2,1,0:T(8,128)(2,1)S(1)} %get-tuple-element.11.query_ref, bf16[2064,128]{1,0:T(8,128)(2,1)S(1)} %collective-permute-done.2.refs_0_, f32[4,512,128]{2,1,0:T(8,128)S(1)} %get-tuple-element.12.refs_1_), custom_call_target="tpu_custom_call" | custom-call | flops 8589934592 | bytes 2097152 | tf_op jit(solution)/shard_map/pallas_call | solution.py:244
  16.4 12.3 %collective-permute-done.1.refs_0_ = bf16[2064,128]{1,0:T(8,128)(2,1)S(1)} collective-permute-done((bf16[2064,128]{1,0:T(8,128)(2,1)S(1)}, bf16[2064,128]{1,0:T(8,128)(2,1)S(1)}, u32[]{:S(2)}, u32[]{:S(2)}) %collective-permute-start.1) | collective-permute-done | bytes 528416 | tf_op jit(solution)/shard_map/ppermute | solution.py:260
  28.6 0.8 %collective-permute-start.3 = (bf16[2064,128]{1,0:T(8,128)(2,1)S(1)}, bf16[2064,128]{1,0:T(8,128)(2,1)S(1)}, u32[]{:S(2)}, u32[]{:S(2)}) collective-permute-start(bf16[2064,128]{1,0:T(8,128)(2,1)S(1)} %collective-permute-done.1.refs_0_), channel_id=1, source_target_pairs={{0,1},{1,0},{2,3},{3,2},{4,5},{5,4},{6,7},{7,6},{8,9},{9,8},{10,11... | collective-permute-start | bytes 1585160 | tf_op jit(solution)/shard_map/ppermute | solution.py:260
  29.4 2.6 %shard_map.40.refs_2_ = f32[4,512,128]{2,1,0:T(8,128)S(1)} custom-call(bf16[4,1024,256]{2,1,0:T(8,128)(2,1)S(1)} %get-tuple-element.11.query_ref, bf16[2064,128]{1,0:T(8,128)(2,1)S(1)} %collective-permute-done.1.refs_0_, f32[4,512,128]{2,1,0:T(8,128)S(1)} %shard_map.39.refs_1_), custom_call_target="tpu_custom_call" | custom-call | flops 8589934592 | bytes 2097152 | tf_op jit(solution)/shard_map/pallas_call | solution.py:244
  32.0 2.3 %collective-permute-done.4.refs_1_ = bf16[2064,128]{1,0:T(8,128)(2,1)S(1)} collective-permute-done((bf16[2064,128]{1,0:T(8,128)(2,1)S(1)}, bf16[2064,128]{1,0:T(8,128)(2,1)S(1)}, u32[]{:S(2)}, u32[]{:S(2)}) %collective-permute-start.4) | collective-permute-done | bytes 528416 | tf_op jit(solution)/shard_map/ppermute | solution.py:260
  34.4 0.0 collective-permute-done.3.refs_0_
  34.4 5.4 %shard_map.41.refs_1_ = f32[4,512,128]{2,1,0:T(8,128)S(1)} custom-call(bf16[4,1024,256]{2,1,0:T(8,128)(2,1)S(1)} %get-tuple-element.11.query_ref, bf16[2064,128]{1,0:T(8,128)(2,1)S(1)} %collective-permute-done.3.refs_0_, bf16[2064,128]{1,0:T(8,128)(2,1)S(1)} %collective-permute-done.4.refs_1_, f32[4,512,128]{2,1,0:T(8,128)S(1)} %shard_map.40.refs_2_), custom_call_target="tpu_custom_call" | custom-call | flops 17179869184 | bytes 2097152 | tf_op jit(solution)/shard_map/pallas_call | solution.py:244
  39.8 0.0 collective-permute-done.refs_0_
  39.8 0.1 collective-permute-start.5
  39.9 2.6 %shard_map.42.refs_1_ = f32[4,512,128]{2,1,0:T(8,128)S(1)} custom-call(bf16[4,1024,256]{2,1,0:T(8,128)(2,1)S(1)} %get-tuple-element.11.query_ref, bf16[2064,128]{1,0:T(8,128)(2,1)S(1)} %collective-permute-done.refs_0_, f32[4,512,128]{2,1,0:T(8,128)S(1)} %shard_map.41.refs_1_), custom_call_target="tpu_custom_call" | custom-call | flops 8589934592 | bytes 2097152 | tf_op jit(solution)/shard_map/pallas_call | solution.py:244
  42.4 0.0 collective-permute-done.5.refs_0_
  42.5 3.3 %shard_map.43 = f32[4,512,128]{2,1,0:T(8,128)} custom-call(bf16[4,1024,256]{2,1,0:T(8,128)(2,1)S(1)} %get-tuple-element.11.query_ref, bf16[2064,128]{1,0:T(8,128)(2,1)S(1)} %collective-permute-done.5.refs_0_, f32[4,512,128]{2,1,0:T(8,128)S(1)} %shard_map.42.refs_1_), custom_call_target="tpu_custom_call" | custom-call | flops 8589934592 | bytes 2097152 | tf_op jit(solution)/shard_map/pallas_call | solution.py:244
Async XLA Ops:
  1.1 12.7 %collective-permute-start.2 = (bf16[2064,128]{1,0:T(8,128)(2,1)S(1)}, bf16[2064,128]{1,0:T(8,128)(2,1)S(1)}, u32[]{:S(2)}, u32[]{:S(2)}) collective-permute-start(bf16[2064,128]{1,0:T(8,128)(2,1)S(1)} %shard_map.37.own_ref), channel_id=1, source_target_pairs={{0,1},{1,0},{2,3},{3,2},{4,5},{5,4},{6,7},{7,6},{8,9},{9,8},{10,11... | collective-permute-start | bytes 1585160 | tf_op jit(solution)/shard_map/ppermute | solution.py:260
  1.8 26.8 %collective-permute-start.1 = (bf16[2064,128]{1,0:T(8,128)(2,1)S(1)}, bf16[2064,128]{1,0:T(8,128)(2,1)S(1)}, u32[]{:S(2)}, u32[]{:S(2)}) collective-permute-start(bf16[2064,128]{1,0:T(8,128)(2,1)S(1)} %shard_map.37.own_ref), channel_id=1, source_target_pairs={{2,0},{3,1},{4,2},{5,3},{6,4},{7,5},{8,6},{9,7},{10,8},{11,9},{12,... | collective-permute-start | bytes 1585160 | tf_op jit(solution)/shard_map/ppermute | solution.py:260
  4.9 29.5 %collective-permute-start.4 = (bf16[2064,128]{1,0:T(8,128)(2,1)S(1)}, bf16[2064,128]{1,0:T(8,128)(2,1)S(1)}, u32[]{:S(2)}, u32[]{:S(2)}) collective-permute-start(bf16[2064,128]{1,0:T(8,128)(2,1)S(1)} %shard_map.37.own_ref), channel_id=1, source_target_pairs={{1,4},{3,6},{4,1},{5,8},{6,3},{7,10},{8,5},{9,12},{10,7},{11,14},{... | collective-permute-start | bytes 1585160 | tf_op jit(solution)/shard_map/ppermute | solution.py:260
  9.1 30.6 %collective-permute-start = (bf16[2064,128]{1,0:T(8,128)(2,1)S(1)}, bf16[2064,128]{1,0:T(8,128)(2,1)S(1)}, u32[]{:S(2)}, u32[]{:S(2)}) collective-permute-start(bf16[2064,128]{1,0:T(8,128)(2,1)S(1)} %shard_map.37.own_ref), channel_id=1, source_target_pairs={{0,2},{1,3},{2,4},{3,5},{4,6},{5,7},{6,8},{7,9},{8,10},{9,11},{10,... | collective-permute-start | bytes 1585160 | tf_op jit(solution)/shard_map/ppermute | solution.py:260
  28.6 5.7 %collective-permute-start.3 = (bf16[2064,128]{1,0:T(8,128)(2,1)S(1)}, bf16[2064,128]{1,0:T(8,128)(2,1)S(1)}, u32[]{:S(2)}, u32[]{:S(2)}) collective-permute-start(bf16[2064,128]{1,0:T(8,128)(2,1)S(1)} %collective-permute-done.1.refs_0_), channel_id=1, source_target_pairs={{0,1},{1,0},{2,3},{3,2},{4,5},{5,4},{6,7},{7,6},{8,9},{9,8},{10,11... | collective-permute-start | bytes 1585160 | tf_op jit(solution)/shard_map/ppermute | solution.py:260
  39.8 2.7 %collective-permute-start.5 = (bf16[2064,128]{1,0:T(8,128)(2,1)S(1)}, bf16[2064,128]{1,0:T(8,128)(2,1)S(1)}, u32[]{:S(2)}, u32[]{:S(2)}) collective-permute-start(bf16[2064,128]{1,0:T(8,128)(2,1)S(1)} %collective-permute-done.refs_0_), channel_id=1, source_target_pairs={{0,1},{1,0},{2,3},{3,2},{4,5},{5,4},{6,7},{7,6},{8,9},{9,8},{10,11... | collective-permute-start | bytes 1585160 | tf_op jit(solution)/shard_map/ppermute | solution.py:260

commit v3 on v2

--- a/solution.py
+++ b/solution.py
@@ -15,11 +15,11 @@
 
 OWN = (0, 0)
 PAIR = (1, -1)
-NEXT = (2, 2)
-PREV = (-2, -2)
+NEAR = (2, -2)
+CROSS = (-2, 2)
 FAR = (-3, 3)
-NEXT_OF_PAIR = (3, 1)
-PREV_OF_PAIR = (-1, -3)
+NEAR_OF_PAIR = (-1, 1)
+CROSS_OF_PAIR = (3, -3)
 
 
 def sine(steps):
@@ -90,39 +90,54 @@
     return me + place[0] + lax.rem(me, 2) * (place[1] - place[0])
 
 
-def pack_kernel(spectra_ref, off_ref, bins_ref, out_ref, off, bins, sems):
-    rows, width = spectra_ref.shape
-    freqs = bins_ref.shape[0]
-    sources, targets = (spectra_ref, off_ref, bins_ref), (out_ref.at[pl.ds(0, rows)], off, bins)
-    copies = [pltpu.make_async_copy(a, b, sems.at[i]) for i, (a, b) in enumerate(zip(sources, targets))]
+def pack_kernel(spectra_ref, off_ref, bins_ref, *refs):
+    out_refs, (off, bins, sems) = refs[:-3], refs[-3:]
+    width = spectra_ref.shape[1]
+    freqs, lines = bins_ref.shape[0], off.shape[1] // width
+    tail = (-(-(lines + rows_of(freqs)) // 16) * 16, width)
+    sources, targets, start = [off_ref, bins_ref], [off, bins], 0
+    for out_ref in out_refs:
+        rows = out_ref.shape[0] - tail[0]
+        sources.append(spectra_ref.at[pl.ds(start, rows)])
+        targets.append(out_ref.at[pl.ds(0, rows)])
+        start = (start + rows) % spectra_ref.shape[0]
+    copies = [
+        pltpu.make_async_copy(source, target, sems.at[i])
+        for i, (source, target) in enumerate(zip(sources, targets))
+    ]
     for copy in copies:
         copy.start()
-    for copy in copies[1:]:
+    for copy in copies[:2]:
         copy.wait()
-    tail = (out_ref.shape[0] - rows, width)
     row = lax.broadcasted_iota(jnp.int32, tail, 0)
     value = jnp.zeros(tail, jnp.int32)
-    for i in range(off.shape[1] // width):
+    for i in range(lines):
         value = jnp.where(row == i, off[:, i * width : (i + 1) * width], value)
     first = tail[0] - rows_of(freqs)
     for f in range(freqs):
         value = jnp.where((row == first + f) | (row == first + freqs + f), bins[f], value)
-    out_ref[rows:, :] = value.astype(jnp.float32).astype(jnp.bfloat16)
-    copies[0].wait()
-
-
-def pack(spectra, offsets, bins):
+    for out_ref in out_refs:
+        out_ref[out_ref.shape[0] - tail[0] :, :] = value.astype(jnp.float32).astype(jnp.bfloat16)
+    for copy in copies[2:]:
+        copy.wait()
+
+
+def pack(spectra, offsets, bins, parts):
     freqs, channels, width = spectra.shape
     tail = -(-(channels // width + rows_of(freqs)) // 16) * 16
+    whole = pl.BlockSpec(memory_space=pltpu.VMEM)
     return pl.pallas_call(
         pack_kernel,
-        out_shape=jax.ShapeDtypeStruct((freqs * channels + tail, width), spectra.dtype),
+        out_shape=[
+            jax.ShapeDtypeStruct((part * channels + tail, width), spectra.dtype)
+            for part in (freqs, *parts)
+        ],
         in_specs=[pl.BlockSpec(memory_space=pltpu.HBM)] * 3,
-        out_specs=pl.BlockSpec(memory_space=pltpu.VMEM),
+        out_specs=[whole] * (1 + len(parts)),
         scratch_shapes=[
             pltpu.VMEM((1, channels), jnp.int32),
             pltpu.SMEM((freqs,), jnp.int32),
-            pltpu.SemaphoreType.DMA((3,)),
+            pltpu.SemaphoreType.DMA((3 + len(parts),)),
         ],
         compiler_params=pltpu.CompilerParams(vmem_limit_bytes=vmem),
         cost_estimate=pl.CostEstimate(flops=0, bytes_accessed=1 << 20, transcendentals=0),
@@ -157,14 +172,14 @@
         query_ref[f, channels:, width:] = jnp.where(mine, imag, zero)
 
 
-def band_sums(query_ref, keys, f, extra):
+def band_sums(query_ref, keys, f, extra, first=0):
     channels, width = query_ref.shape[1] // 2, query_ref.shape[2] // 2
     sums = []
     for half in range(2):
         query = query_ref[f, pl.ds(half * channels, channels), :]
         part = None
         for key_ref, columns_j in zip(keys, extra):
-            key = key_ref[pl.ds(f * channels, channels), :]
+            key = key_ref[pl.ds((f - first) * channels, channels), :]
             misfit = lax.dot_general(
                 query,
                 jnp.concatenate([key, columns_j], axis=1),
@@ -179,21 +194,25 @@
 
 
 def columns_of(key_ref, block, freqs, channels, width):
-    tail_ref = key_ref.at[pl.ds(freqs * channels, key_ref.shape[0] - freqs * channels)]
+    tail = -(-(channels // width + rows_of(freqs)) // 16) * 16
+    tail_ref = key_ref.at[pl.ds(key_ref.shape[0] - tail, tail)]
     return key_columns(tail_ref, block, freqs, channels, width)
 
 
-def own_kernel(axis, own_ref, query_ref, total_ref):
+def chip_kernel(axis, left, own_ref, pair_ref, query_ref, total_ref):
     freqs, channels, width = total_ref.shape
-    block = block_of(axis, OWN)
-    extra = columns_of(own_ref, block, freqs, channels, width)
-    fill_queries(own_ref, query_ref, block)
+    own, pair = block_of(axis, OWN), block_of(axis, PAIR)
+    fill_queries(own_ref, query_ref, own)
+    own_columns = columns_of(own_ref, own, freqs, channels, width)
+    pair_columns = columns_of(pair_ref, pair, freqs, channels, width)
     for f in range(freqs):
-        term = band_sums(query_ref, [own_ref], f, [extra])
-        total_ref[f] = term * (4.0 / width)
-
-
-def band_kernel(axis, places, last, query_ref, *refs):
+        term = 2.0 * band_sums(query_ref, [own_ref], f, [own_columns])
+        if f < freqs - left:
+            term = term + band_sums(query_ref, [pair_ref], f, [pair_columns])
+        total_ref[f] = term * (2.0 / width)
+
+
+def band_kernel(axis, places, first, count, last, query_ref, *refs):
     keys, (total_ref, out_ref) = refs[: len(places)], refs[len(places) : len(places) + 2]
     freqs, channels, width = total_ref.shape
     extra = [
@@ -202,8 +221,9 @@
     ]
     copies = []
     for f in range(freqs):
-        term = band_sums(query_ref, keys, f, extra)
-        term = total_ref[f] + term * (2.0 / width)
+        term = total_ref[f]
+        if first <= f < first + count:
+            term = term + band_sums(query_ref, keys, f, extra, first) * (2.0 / width)
         if last:
             result_ref, sems = refs[len(places) + 2 :]
             result_ref[f] = term
@@ -222,27 +242,27 @@
     )
 
 
-def own_terms(shape, axis, own):
+def chip_terms(shape, axis, own, pair, left):
     freqs, channels, width = shape
     whole = pl.BlockSpec(memory_space=pltpu.VMEM)
     return pl.pallas_call(
-        functools.partial(own_kernel, axis),
+        functools.partial(chip_kernel, axis, left),
         out_shape=[
             jax.ShapeDtypeStruct((freqs, 2 * channels, 2 * width), jnp.bfloat16),
             jax.ShapeDtypeStruct(shape, jnp.float32),
         ],
-        in_specs=[whole],
+        in_specs=[whole, whole],
         out_specs=[whole, whole],
         compiler_params=pltpu.CompilerParams(vmem_limit_bytes=vmem),
         cost_estimate=cost(shape, 1),
-    )(own)
-
-
-def band_terms(shape, axis, query, total, keys, places, last=False):
+    )(own, pair)
+
+
+def band_terms(shape, axis, query, total, keys, places, part=None, last=False):
     whole = pl.BlockSpec(memory_space=pltpu.VMEM)
     scratch = [pltpu.VMEM(shape, jnp.float32), pltpu.SemaphoreType.DMA((shape[0],))]
     return pl.pallas_call(
-        functools.partial(band_kernel, axis, tuple(places), last),
+        functools.partial(band_kernel, axis, tuple(places), *(part or (0, shape[0])), last),
         out_shape=jax.ShapeDtypeStruct(shape, jnp.float32),
         in_specs=[whole] * (len(keys) + 2),
         out_specs=pl.BlockSpec(memory_space=pl.ANY) if last else whole,
@@ -255,28 +275,35 @@
 def local(axis, count, spectra, offsets, bins):
     shape = spectra.shape
 
-    def moved(value, target):
-        pairs = [(i, target(i)) for i in range(count)]
-        return lax.ppermute(value, axis, [(i, t) for i, t in pairs if 0 <= t < count])
-
-    own = pack(spectra, offsets, bins)
-    nxt = moved(own, lambda i: i - 2)
-    prev = moved(own, lambda i: i + 2)
-    far = moved(own, lambda i: i + 3 if i % 2 else i - 3)
-    pair = moved(own, lambda i: i ^ 1)
-
-    query, total = own_terms(shape, axis, own)
+    def fetched(value, place):
+        sources = [(i + place[i % 2], i) for i in range(count)]
+        return lax.ppermute(value, axis, [(i, t) for i, t in sources if 0 <= i < count])
+
+    left = shape[0] // 2
+    low, high = (0, shape[0] - left), (shape[0] - left, left)
+    own, own_low, own_high = pack(spectra, offsets, bins, (shape[0] - left, left))
+    near = fetched(own, NEAR)
+    far = fetched(own, FAR)
+    pair_low = fetched(own_low, PAIR)
+    pair_high = fetched(own_high, PAIR)
+
+    query, total = chip_terms(shape, axis, own, pair_low, left)
     terms = functools.partial(band_terms, shape, axis, query)
-    total = terms(total, [pair], [PAIR])
-    nxt, total = lax.optimization_barrier((nxt, total))
-    nxt_pair = moved(nxt, lambda i: i ^ 1)
-    total = terms(total, [nxt], [NEXT])
-    total = terms(total, [nxt_pair, far], [NEXT_OF_PAIR, FAR])
-    prev, total = lax.optimization_barrier((prev, total))
-    prev_pair = moved(prev, lambda i: i ^ 1)
-    total = terms(total, [prev], [PREV])
-    total = terms(total, [prev_pair], [PREV_OF_PAIR], last=True)
-    return total
+    own_low, own_high, total = lax.optimization_barrier((own_low, own_high, total))
+    cross_low = fetched(own_low, CROSS)
+    cross_high = fetched(own_high, CROSS)
+    total = terms(total, [pair_high], [PAIR], part=high)
+    near, total = lax.optimization_barrier((near, total))
+    near_pair = fetched(near, PAIR)
+    total = terms(total, [near], [NEAR])
+    total = terms(total, [near_pair], [NEAR_OF_PAIR])
+    for cross, part in ((cross_low, low), (cross_high, high)):
+        cross, total = lax.optimization_barrier((cross, total))
+        cross_pair = fetched(cross, PAIR)
+        total = terms(total, [cross], [CROSS], part=part)
+        total = terms(total, [cross_pair], [CROSS_OF_PAIR], part=part)
+    far, total = lax.optimization_barrier((far, total))
+    return terms(total, [far], [FAR], last=True)
 
 
 def solution(mesh):

time: 46.1 us -> 38.7 us (0.84)
  the two profiles are of different devices: /device:TPU:21 before, /device:TPU:0 now
where the time goes in v3:
time: 38.7 us; the launch traced here: 38.5 us
  Pallas kernels  21 us (54%)
  starting transfers between devices  17.1 us (44%)
    ppermute x9, starting transfers between devices, fetched(): lax.ppermute(value, axis, [(i, t) for i, t in sources if 0 <= i < count])  17.1 us
    pallas_call x8, Pallas kernels, band_terms(): pl.pallas_call(functools.partial(band_kernel, axis, tuple(places), *(part...  15.9 us
    pallas_call x1, Pallas kernels, chip_terms(): pl.pallas_call(functools.partial(chip_kernel, axis, left), out_shape=[jax...  3.78 us
    pallas_call x1, Pallas kernels, pack(): pl.pallas_call(pack_kernel, out_shape=[jax.ShapeDtypeStruct((part * chann...  1.36 us
  transfers between devices with their start and end apart: 9, of which 0 were waited for; matrix products, arithmetic and copies ran while one was open for 0% of the time, Pallas kernels for 42%

profile of v3, /device:TPU:0, one launch (start us, length us, event | category | flops | bytes accessed | tf_op | source)
XLA Modules:
  0.0 38.5 jit_solution(12305523030998726512)
XLA Ops:
  0.0 1.4 %shard_map.37 = (bf16[2064,128]{1,0:T(8,128)(2,1)S(1)}, bf16[1040,128]{1,0:T(8,128)(2,1)S(1)}, bf16[1040,128]{1,0:T(8,128)(2,1)S(1)}) custom-call(bf16[2048,128]{1,0:T(8,128)(2,1)} %bitcast.2, s32[1,512]{1,0:T(1,128)} %bitcast.3, s32[4]{0:T(128)} %bins_ref.1), custom_call_target="tpu_custom_call" | custom-call | bytes 1048576 | tf_op jit(solution)/shard_map/pallas_call | solution.py:129
  1.4 0.5 %collective-permute-start = (bf16[1040,128]{1,0:T(8,128)(2,1)S(1)}, bf16[1040,128]{1,0:T(8,128)(2,1)S(1)}, u32[]{:S(2)}, u32[]{:S(2)}) collective-permute-start(bf16[1040,128]{1,0:T(8,128)(2,1)S(1)} %get-tuple-element.27), channel_id=1, source_target_pairs={{1,0},{0,1},{3,2},{2,3},{5,4},{4,5},{7,6},{6,7},{9,8},{8,9},{11,10... | collective-permute-start | bytes 798728 | tf_op jit(solution)/shard_map/ppermute | solution.py:280
  1.9 1.3 %collective-permute-start.4 = (bf16[2064,128]{1,0:T(8,128)(2,1)S(1)}, bf16[2064,128]{1,0:T(8,128)(2,1)S(1)}, u32[]{:S(2)}, u32[]{:S(2)}) collective-permute-start(bf16[2064,128]{1,0:T(8,128)(2,1)S(1)} %get-tuple-element.21.own_ref), channel_id=1, source_target_pairs={{2,0},{4,2},{1,3},{6,4},{3,5},{8,6},{5,7},{10,8},{7,9},{12,10},{9,... | collective-permute-start | bytes 1585160 | tf_op jit(solution)/shard_map/ppermute | solution.py:280
  3.2 0.7 %collective-permute-start.1 = (bf16[2064,128]{1,0:T(8,128)(2,1)S(1)}, bf16[2064,128]{1,0:T(8,128)(2,1)S(1)}, u32[]{:S(2)}, u32[]{:S(2)}) collective-permute-start(bf16[2064,128]{1,0:T(8,128)(2,1)S(1)} %get-tuple-element.21.own_ref), channel_id=1, source_target_pairs={{4,1},{6,3},{1,4},{8,5},{3,6},{10,7},{5,8},{12,9},{7,10},{14,11},{... | collective-permute-start | bytes 1585160 | tf_op jit(solution)/shard_map/ppermute | solution.py:280
  3.9 6.0 %collective-permute-start.5 = (bf16[1040,128]{1,0:T(8,128)(2,1)S(1)}, bf16[1040,128]{1,0:T(8,128)(2,1)S(1)}, u32[]{:S(2)}, u32[]{:S(2)}) collective-permute-start(bf16[1040,128]{1,0:T(8,128)(2,1)S(1)} %get-tuple-element.26), channel_id=1, source_target_pairs={{1,0},{0,1},{3,2},{2,3},{5,4},{4,5},{7,6},{6,7},{9,8},{8,9},{11,10... | collective-permute-start | bytes 798728 | tf_op jit(solution)/shard_map/ppermute | solution.py:280
  9.9 3.8 %shard_map.38 = (bf16[4,1024,256]{2,1,0:T(8,128)(2,1)S(1)}, f32[4,512,128]{2,1,0:T(8,128)S(1)}) custom-call(bf16[2064,128]{1,0:T(8,128)(2,1)S(1)} %get-tuple-element.21.own_ref, bf16[1040,128]{1,0:T(8,128)(2,1)S(1)} %collective-permute-done.pair_ref), custom_call_target="tpu_custom_call" | custom-call | flops 8589934592 | bytes 2097152 | tf_op jit(solution)/shard_map/pallas_call | solution.py:248
  13.7 2.5 %collective-permute-start.3 = (bf16[1040,128]{1,0:T(8,128)(2,1)S(1)}, bf16[1040,128]{1,0:T(8,128)(2,1)S(1)}, u32[]{:S(2)}, u32[]{:S(2)}) collective-permute-start(bf16[1040,128]{1,0:T(8,128)(2,1)S(1)} %get-tuple-element.27), channel_id=1, source_target_pairs={{3,1},{0,2},{5,3},{2,4},{7,5},{4,6},{9,7},{6,8},{11,9},{8,10},{13,... | collective-permute-start | bytes 798728 | tf_op jit(solution)/shard_map/ppermute | solution.py:280
  16.2 5.4 %collective-permute-start.2 = (bf16[1040,128]{1,0:T(8,128)(2,1)S(1)}, bf16[1040,128]{1,0:T(8,128)(2,1)S(1)}, u32[]{:S(2)}, u32[]{:S(2)}) collective-permute-start(bf16[1040,128]{1,0:T(8,128)(2,1)S(1)} %get-tuple-element.26), channel_id=1, source_target_pairs={{3,1},{0,2},{5,3},{2,4},{7,5},{4,6},{9,7},{6,8},{11,9},{8,10},{13,... | collective-permute-start | bytes 798728 | tf_op jit(solution)/shard_map/ppermute | solution.py:280
  21.6 1.5 %shard_map.39.refs_1_ = f32[4,512,128]{2,1,0:T(8,128)S(1)} custom-call(bf16[4,1024,256]{2,1,0:T(8,128)(2,1)S(1)} %get-tuple-element.23.query_ref, bf16[1040,128]{1,0:T(8,128)(2,1)S(1)} %collective-permute-done.5.refs_0_, f32[4,512,128]{2,1,0:T(8,128)S(1)} %get-tuple-element.28.refs_1_), custom_call_target="tpu_custom_call" | custom-call | flops 8589934592 | bytes 2097152 | tf_op jit(solution)/shard_map/pallas_call | solution.py:264
  23.1 0.1 collective-permute-start.6
  23.1 2.6 %shard_map.40.refs_1_ = f32[4,512,128]{2,1,0:T(8,128)S(1)} custom-call(bf16[4,1024,256]{2,1,0:T(8,128)(2,1)S(1)} %get-tuple-element.23.query_ref, bf16[2064,128]{1,0:T(8,128)(2,1)S(1)} %collective-permute-done.4.refs_0_, f32[4,512,128]{2,1,0:T(8,128)S(1)} %shard_map.39.refs_1_), custom_call_target="tpu_custom_call" | custom-call | flops 8589934592 | bytes 2097152 | tf_op jit(solution)/shard_map/pallas_call | solution.py:264
  25.7 2.6 %shard_map.41.refs_1_ = f32[4,512,128]{2,1,0:T(8,128)S(1)} custom-call(bf16[4,1024,256]{2,1,0:T(8,128)(2,1)S(1)} %get-tuple-element.23.query_ref, bf16[2064,128]{1,0:T(8,128)(2,1)S(1)} %collective-permute-done.6.refs_0_, f32[4,512,128]{2,1,0:T(8,128)S(1)} %shard_map.40.refs_1_), custom_call_target="tpu_custom_call" | custom-call | flops 8589934592 | bytes 2097152 | tf_op jit(solution)/shard_map/pallas_call | solution.py:264
  28.3 0.0 collective-permute-done.3.refs_0_
  28.3 0.6 %collective-permute-start.7 = (bf16[1040,128]{1,0:T(8,128)(2,1)S(1)}, bf16[1040,128]{1,0:T(8,128)(2,1)S(1)}, u32[]{:S(2)}, u32[]{:S(2)}) collective-permute-start(bf16[1040,128]{1,0:T(8,128)(2,1)S(1)} %collective-permute-done.3.refs_0_), channel_id=1, source_target_pairs={{1,0},{0,1},{3,2},{2,3},{5,4},{4,5},{7,6},{6,7},{9,8},{8,9},{11,10... | collective-permute-start | bytes 798728 | tf_op jit(solution)/shard_map/ppermute | solution.py:280
  28.9 1.5 %shard_map.42.refs_1_ = f32[4,512,128]{2,1,0:T(8,128)S(1)} custom-call(bf16[4,1024,256]{2,1,0:T(8,128)(2,1)S(1)} %get-tuple-element.23.query_ref, bf16[1040,128]{1,0:T(8,128)(2,1)S(1)} %collective-permute-done.3.refs_0_, f32[4,512,128]{2,1,0:T(8,128)S(1)} %shard_map.41.refs_1_), custom_call_target="tpu_custom_call" | custom-call | flops 8589934592 | bytes 2097152 | tf_op jit(solution)/shard_map/pallas_call | solution.py:264
  30.4 0.0 collective-permute-done.7.refs_0_
  30.4 1.5 %shard_map.43.refs_1_ = f32[4,512,128]{2,1,0:T(8,128)S(1)} custom-call(bf16[4,1024,256]{2,1,0:T(8,128)(2,1)S(1)} %get-tuple-element.23.query_ref, bf16[1040,128]{1,0:T(8,128)(2,1)S(1)} %collective-permute-done.7.refs_0_, f32[4,512,128]{2,1,0:T(8,128)S(1)} %shard_map.42.refs_1_), custom_call_target="tpu_custom_call" | custom-call | flops 8589934592 | bytes 2097152 | tf_op jit(solution)/shard_map/pallas_call | solution.py:264
  31.9 0.0 collective-permute-done.2.refs_0_
  31.9 0.1 collective-permute-start.8
  32.0 1.5 %shard_map.44.refs_1_ = f32[4,512,128]{2,1,0:T(8,128)S(1)} custom-call(bf16[4,1024,256]{2,1,0:T(8,128)(2,1)S(1)} %get-tuple-element.23.query_ref, bf16[1040,128]{1,0:T(8,128)(2,1)S(1)} %collective-permute-done.2.refs_0_, f32[4,512,128]{2,1,0:T(8,128)S(1)} %shard_map.43.refs_1_), custom_call_target="tpu_custom_call" | custom-call | flops 8589934592 | bytes 2097152 | tf_op jit(solution)/shard_map/pallas_call | solution.py:264
  33.5 0.0 collective-permute-done.8.refs_0_
  33.5 1.5 %shard_map.45.refs_1_ = f32[4,512,128]{2,1,0:T(8,128)S(1)} custom-call(bf16[4,1024,256]{2,1,0:T(8,128)(2,1)S(1)} %get-tuple-element.23.query_ref, bf16[1040,128]{1,0:T(8,128)(2,1)S(1)} %collective-permute-done.8.refs_0_, f32[4,512,128]{2,1,0:T(8,128)S(1)} %shard_map.44.refs_1_), custom_call_target="tpu_custom_call" | custom-call | flops 8589934592 | bytes 2097152 | tf_op jit(solution)/shard_map/pallas_call | solution.py:264
  35.0 0.0 collective-permute-done.1.refs_0_
  35.0 3.3 %shard_map.46 = f32[4,512,128]{2,1,0:T(8,128)} custom-call(bf16[4,1024,256]{2,1,0:T(8,128)(2,1)S(1)} %get-tuple-element.23.query_ref, bf16[2064,128]{1,0:T(8,128)(2,1)S(1)} %collective-permute-done.1.refs_0_, f32[4,512,128]{2,1,0:T(8,128)S(1)} %shard_map.45.refs_1_), custom_call_target="tpu_custom_call" | custom-call | flops 8589934592 | bytes 2097152 | tf_op jit(solution)/shard_map/pallas_call | solution.py:264
  (4 shorter events, 0.0 us)
Async XLA Ops:
  1.4 8.5 %collective-permute-start = (bf16[1040,128]{1,0:T(8,128)(2,1)S(1)}, bf16[1040,128]{1,0:T(8,128)(2,1)S(1)}, u32[]{:S(2)}, u32[]{:S(2)}) collective-permute-start(bf16[1040,128]{1,0:T(8,128)(2,1)S(1)} %get-tuple-element.27), channel_id=1, source_target_pairs={{1,0},{0,1},{3,2},{2,3},{5,4},{4,5},{7,6},{6,7},{9,8},{8,9},{11,10... | collective-permute-start | bytes 798728 | tf_op jit(solution)/shard_map/ppermute | solution.py:280
  1.9 21.2 %collective-permute-start.4 = (bf16[2064,128]{1,0:T(8,128)(2,1)S(1)}, bf16[2064,128]{1,0:T(8,128)(2,1)S(1)}, u32[]{:S(2)}, u32[]{:S(2)}) collective-permute-start(bf16[2064,128]{1,0:T(8,128)(2,1)S(1)} %get-tuple-element.21.own_ref), channel_id=1, source_target_pairs={{2,0},{4,2},{1,3},{6,4},{3,5},{8,6},{5,7},{10,8},{7,9},{12,10},{9,... | collective-permute-start | bytes 1585160 | tf_op jit(solution)/shard_map/ppermute | solution.py:280
  3.2 31.8 %collective-permute-start.1 = (bf16[2064,128]{1,0:T(8,128)(2,1)S(1)}, bf16[2064,128]{1,0:T(8,128)(2,1)S(1)}, u32[]{:S(2)}, u32[]{:S(2)}) collective-permute-start(bf16[2064,128]{1,0:T(8,128)(2,1)S(1)} %get-tuple-element.21.own_ref), channel_id=1, source_target_pairs={{4,1},{6,3},{1,4},{8,5},{3,6},{10,7},{5,8},{12,9},{7,10},{14,11},{... | collective-permute-start | bytes 1585160 | tf_op jit(solution)/shard_map/ppermute | solution.py:280
  3.9 17.7 %collective-permute-start.5 = (bf16[1040,128]{1,0:T(8,128)(2,1)S(1)}, bf16[1040,128]{1,0:T(8,128)(2,1)S(1)}, u32[]{:S(2)}, u32[]{:S(2)}) collective-permute-start(bf16[1040,128]{1,0:T(8,128)(2,1)S(1)} %get-tuple-element.26), channel_id=1, source_target_pairs={{1,0},{0,1},{3,2},{2,3},{5,4},{4,5},{7,6},{6,7},{9,8},{8,9},{11,10... | collective-permute-start | bytes 798728 | tf_op jit(solution)/shard_map/ppermute | solution.py:280
  13.7 14.7 %collective-permute-start.3 = (bf16[1040,128]{1,0:T(8,128)(2,1)S(1)}, bf16[1040,128]{1,0:T(8,128)(2,1)S(1)}, u32[]{:S(2)}, u32[]{:S(2)}) collective-permute-start(bf16[1040,128]{1,0:T(8,128)(2,1)S(1)} %get-tuple-element.27), channel_id=1, source_target_pairs={{3,1},{0,2},{5,3},{2,4},{7,5},{4,6},{9,7},{6,8},{11,9},{8,10},{13,... | collective-permute-start | bytes 798728 | tf_op jit(solution)/shard_map/ppermute | solution.py:280
  16.2 15.7 %collective-permute-start.2 = (bf16[1040,128]{1,0:T(8,128)(2,1)S(1)}, bf16[1040,128]{1,0:T(8,128)(2,1)S(1)}, u32[]{:S(2)}, u32[]{:S(2)}) collective-permute-start(bf16[1040,128]{1,0:T(8,128)(2,1)S(1)} %get-tuple-element.26), channel_id=1, source_target_pairs={{3,1},{0,2},{5,3},{2,4},{7,5},{4,6},{9,7},{6,8},{11,9},{8,10},{13,... | collective-permute-start | bytes 798728 | tf_op jit(solution)/shard_map/ppermute | solution.py:280
  23.1 2.7 %collective-permute-start.6 = (bf16[2064,128]{1,0:T(8,128)(2,1)S(1)}, bf16[2064,128]{1,0:T(8,128)(2,1)S(1)}, u32[]{:S(2)}, u32[]{:S(2)}) collective-permute-start(bf16[2064,128]{1,0:T(8,128)(2,1)S(1)} %collective-permute-done.4.refs_0_), channel_id=1, source_target_pairs={{1,0},{0,1},{3,2},{2,3},{5,4},{4,5},{7,6},{6,7},{9,8},{8,9},{11,10... | collective-permute-start | bytes 1585160 | tf_op jit(solution)/shard_map/ppermute | solution.py:280
  28.3 2.0 %collective-permute-start.7 = (bf16[1040,128]{1,0:T(8,128)(2,1)S(1)}, bf16[1040,128]{1,0:T(8,128)(2,1)S(1)}, u32[]{:S(2)}, u32[]{:S(2)}) collective-permute-start(bf16[1040,128]{1,0:T(8,128)(2,1)S(1)} %collective-permute-done.3.refs_0_), channel_id=1, source_target_pairs={{1,0},{0,1},{3,2},{2,3},{5,4},{4,5},{7,6},{6,7},{9,8},{8,9},{11,10... | collective-permute-start | bytes 798728 | tf_op jit(solution)/shard_map/ppermute | solution.py:280
  31.9 1.6 %collective-permute-start.8 = (bf16[1040,128]{1,0:T(8,128)(2,1)S(1)}, bf16[1040,128]{1,0:T(8,128)(2,1)S(1)}, u32[]{:S(2)}, u32[]{:S(2)}) collective-permute-start(bf16[1040,128]{1,0:T(8,128)(2,1)S(1)} %collective-permute-done.2.refs_0_), channel_id=1, source_target_pairs={{1,0},{0,1},{3,2},{2,3},{5,4},{4,5},{7,6},{6,7},{9,8},{8,9},{11,10... | collective-permute-start | bytes 798728 | tf_op jit(solution)/shard_map/ppermute | solution.py:280

commit v4 on v3

--- a/solution.py
+++ b/solution.py
@@ -54,35 +54,31 @@
     return factor * (channel * spacing_metres + offsets), row < freqs
 
 
-def columns(parts, width):
+def padded(parts, width):
     rows = jnp.concatenate(parts, axis=0)
-    rows = jnp.concatenate(
-        [rows, jnp.zeros((width - rows.shape[0], rows.shape[1]), jnp.float32)], axis=0
-    )
-    return rows.T.astype(jnp.bfloat16)
+    rest = jnp.zeros((width - rows.shape[0], rows.shape[1]), jnp.float32)
+    return jnp.concatenate([rows, rest], axis=0)
 
 
 def key_columns(tail_ref, block, freqs, channels, width):
     angle, is_cos = angles(tail_ref, block, freqs, channels)
     high, low = halves(sine(angle + jnp.where(is_cos, period_metres // 4, 0)))
-    return columns([high, low, high, low], width)
-
-
-def query_columns(tail_ref, block, freqs, channels, width):
+    return padded([high, low, high, low], width).T.astype(jnp.bfloat16)
+
+
+def query_rows(tail_ref, block, freqs, channels, width):
     angle, is_cos = angles(tail_ref, block, freqs, channels)
     quarter = period_metres // 4
     high, low = halves(-model_amp * sine(angle + jnp.where(is_cos, quarter, 0)))
-    real = columns([high, high, low, low], width)
+    real = padded([high, high, low, low], width)
     high, low = halves(model_amp * sine(angle - jnp.where(is_cos, 0, quarter)))
-    imag = columns([high, high, low, low], width)
+    imag = padded([high, high, low, low], width)
     return real, imag
 
 
 def turned(value):
-    width = value.shape[1]
-    lane = lax.broadcasted_iota(jnp.int32, value.shape, 1)
-    moved = pltpu.roll(value, width // 2, 1)
-    return jnp.where(lane < width // 2, -moved, moved)
+    half = value.shape[0] // 2
+    return jnp.concatenate([-value[half:], value[:half]], axis=0)
 
 
 def block_of(axis, place):
@@ -150,47 +146,30 @@
 
 
 def fill_queries(own_ref, query_ref, block):
-    freqs, channels, width = query_ref.shape[0], query_ref.shape[1] // 2, own_ref.shape[1]
-    windows = width // 2
-    real, imag = query_columns(
-        own_ref.at[pl.ds(freqs * channels, own_ref.shape[0] - freqs * channels)],
-        block,
-        freqs,
-        channels,
-        width,
-    )
-    lane = lax.broadcasted_iota(jnp.int32, (channels, width), 1)
-    lane_row = lax.rem(lane, rows_of(freqs))
-    used = lane < 4 * rows_of(freqs)
-    zero = jnp.zeros((), jnp.bfloat16)
-    for f in range(freqs):
-        own = own_ref[pl.ds(f * channels, channels), :].astype(jnp.float32) / windows
-        mine = used & ((lane_row == f) | (lane_row == freqs + f))
-        query_ref[f, :channels, :width] = own.astype(jnp.bfloat16)
-        query_ref[f, channels:, :width] = (-turned(own)).astype(jnp.bfloat16)
-        query_ref[f, :channels, width:] = jnp.where(mine, real, zero)
-        query_ref[f, channels:, width:] = jnp.where(mine, imag, zero)
+    freqs, channels, width = query_ref.shape[0], query_ref.shape[2] // 2, own_ref.shape[1]
+    tail_ref = own_ref.at[pl.ds(freqs * channels, own_ref.shape[0] - freqs * channels)]
+    real, imag = query_rows(tail_ref, block, freqs, channels, width)
+    row = lax.rem(lax.broadcasted_iota(jnp.int32, (width, channels), 0), rows_of(freqs))
+    for f in range(freqs):
+        own = own_ref[pl.ds(f * channels, channels), :].astype(jnp.float32).T * (2.0 / width)
+        mine = (row == f) | (row == freqs + f)
+        query_ref[f, :width, :channels] = own.astype(jnp.bfloat16)
+        query_ref[f, :width, channels:] = (-turned(own)).astype(jnp.bfloat16)
+        query_ref[f, width:, :channels] = jnp.where(mine, real, 0.0).astype(jnp.bfloat16)
+        query_ref[f, width:, channels:] = jnp.where(mine, imag, 0.0).astype(jnp.bfloat16)
 
 
 def band_sums(query_ref, keys, f, extra, first=0):
-    channels, width = query_ref.shape[1] // 2, query_ref.shape[2] // 2
-    sums = []
-    for half in range(2):
-        query = query_ref[f, pl.ds(half * channels, channels), :]
-        part = None
-        for key_ref, columns_j in zip(keys, extra):
-            key = key_ref[pl.ds((f - first) * channels, channels), :]
-            misfit = lax.dot_general(
-                query,
-                jnp.concatenate([key, columns_j], axis=1),
-                (((1,), (1,)), ((), ())),
-                preferred_element_type=jnp.float32,
-            )
-            grad = jnp.tanh(misfit).astype(jnp.bfloat16)
-            term = jnp.dot(grad, key, preferred_element_type=jnp.float32)
-            part = term if part is None else part + term
-        sums.append(part)
-    return sums[0] + turned(sums[1])
+    channels = query_ref.shape[2] // 2
+    spectra = [key_ref[pl.ds((f - first) * channels, channels), :] for key_ref in keys]
+    spectra = spectra[0] if len(keys) == 1 else jnp.concatenate(spectra, axis=0)
+    extra = extra[0] if len(keys) == 1 else jnp.concatenate(extra, axis=0)
+    misfit = jnp.dot(
+        jnp.concatenate([spectra, extra], axis=1), query_ref[f], preferred_element_type=jnp.float32
+    )
+    grad = jnp.tanh(misfit).astype(jnp.bfloat16)
+    sums = jnp.dot(spectra.T, grad, preferred_element_type=jnp.float32)
+    return sums[:, :channels] + turned(sums[:, channels:])
 
 
 def columns_of(key_ref, block, freqs, channels, width):
@@ -200,7 +179,7 @@
 
 
 def chip_kernel(axis, left, own_ref, pair_ref, query_ref, total_ref):
-    freqs, channels, width = total_ref.shape
+    freqs, width, channels = total_ref.shape
     own, pair = block_of(axis, OWN), block_of(axis, PAIR)
     fill_queries(own_ref, query_ref, own)
     own_columns = columns_of(own_ref, own, freqs, channels, width)
@@ -214,7 +193,7 @@
 
 def band_kernel(axis, places, first, count, last, query_ref, *refs):
     keys, (total_ref, out_ref) = refs[: len(places)], refs[len(places) : len(places) + 2]
-    freqs, channels, width = total_ref.shape
+    freqs, width, channels = total_ref.shape
     extra = [
         columns_of(key_ref, block_of(axis, place), freqs, channels, width)
         for key_ref, place in zip(keys, places)
@@ -226,7 +205,7 @@
             term = term + band_sums(query_ref, keys, f, extra, first) * (2.0 / width)
         if last:
             result_ref, sems = refs[len(places) + 2 :]
-            result_ref[f] = term
+            result_ref[f] = term.T
             copies.append(pltpu.make_async_copy(result_ref.at[f], out_ref.at[f], sems.at[f]))
             copies[f].start()
         else:
@@ -248,8 +227,8 @@
     return pl.pallas_call(
         functools.partial(chip_kernel, axis, left),
         out_shape=[
-            jax.ShapeDtypeStruct((freqs, 2 * channels, 2 * width), jnp.bfloat16),
-            jax.ShapeDtypeStruct(shape, jnp.float32),
+            jax.ShapeDtypeStruct((freqs, 2 * width, 2 * channels), jnp.bfloat16),
+            jax.ShapeDtypeStruct((freqs, width, channels), jnp.float32),
         ],
         in_specs=[whole, whole],
         out_specs=[whole, whole],
@@ -263,7 +242,7 @@
     scratch = [pltpu.VMEM(shape, jnp.float32), pltpu.SemaphoreType.DMA((shape[0],))]
     return pl.pallas_call(
         functools.partial(band_kernel, axis, tuple(places), *(part or (0, shape[0])), last),
-        out_shape=jax.ShapeDtypeStruct(shape, jnp.float32),
+        out_shape=jax.ShapeDtypeStruct(shape if last else total.shape, jnp.float32),
         in_specs=[whole] * (len(keys) + 2),
         out_specs=pl.BlockSpec(memory_space=pl.ANY) if last else whole,
         scratch_shapes=scratch if last else [],
@@ -289,10 +268,11 @@
 
     query, total = chip_terms(shape, axis, own, pair_low, left)
     terms = functools.partial(band_terms, shape, axis, query)
-    own_low, own_high, total = lax.optimization_barrier((own_low, own_high, total))
+    own_low, total = lax.optimization_barrier((own_low, total))
     cross_low = fetched(own_low, CROSS)
+    total = terms(total, [pair_high], [PAIR], part=high)
+    own_high, total = lax.optimization_barrier((own_high, total))
     cross_high = fetched(own_high, CROSS)
-    total = terms(total, [pair_high], [PAIR], part=high)
     near, total = lax.optimization_barrier((near, total))
     near_pair = fetched(near, PAIR)
     total = terms(total, [near], [NEAR])

time: 38.7 us -> 36.3 us (0.938)
  the two profiles are of different devices: /device:TPU:0 before, /device:TPU:19 now
where the time goes in v4:
time: 36.3 us; the launch traced here: 36.1 us
  Pallas kernels  17.4 us (48%)
  starting transfers between devices  15.6 us (43%)
  waiting for transfers between devices  2.82 us (8%)
    ppermute x9, starting transfers between devices, fetched(): lax.ppermute(value, axis, [(i, t) for i, t in sources if 0 <= i < count])  15.6 us
    pallas_call x8, Pallas kernels, band_terms(): pl.pallas_call(functools.partial(band_kernel, axis, tuple(places), *(part...  12.9 us
    pallas_call x1, Pallas kernels, chip_terms(): pl.pallas_call(functools.partial(chip_kernel, axis, left), out_shape=[jax...  3.11 us
    ppermute x9, waiting for transfers between devices, fetched(): lax.ppermute(value, axis, [(i, t) for i, t in sources if 0 <= i < count])  2.82 us
    pallas_call x1, Pallas kernels, pack(): pl.pallas_call(pack_kernel, out_shape=[jax.ShapeDtypeStruct((part * chann...  1.31 us
  transfers between devices with their start and end apart: 9, of which 3 were waited for; matrix products, arithmetic and copies ran while one was open for 0% of the time, Pallas kernels for 36%

profile of v4, /device:TPU:19, one launch (start us, length us, event | category | flops | bytes accessed | tf_op | source)
XLA Modules:
  0.0 36.1 jit_solution(1234402634408938597)
XLA Ops:
  0.0 1.3 %shard_map.37 = (bf16[2064,128]{1,0:T(8,128)(2,1)S(1)}, bf16[1040,128]{1,0:T(8,128)(2,1)S(1)}, bf16[1040,128]{1,0:T(8,128)(2,1)S(1)}) custom-call(bf16[2048,128]{1,0:T(8,128)(2,1)} %bitcast.2, s32[1,512]{1,0:T(1,128)} %bitcast.3, s32[4]{0:T(128)} %bins_ref.1), custom_call_target="tpu_custom_call" | custom-call | bytes 1048576 | tf_op jit(solution)/shard_map/pallas_call | solution.py:125
  1.3 0.7 %collective-permute-start = (bf16[1040,128]{1,0:T(8,128)(2,1)S(1)}, bf16[1040,128]{1,0:T(8,128)(2,1)S(1)}, u32[]{:S(2)}, u32[]{:S(2)}) collective-permute-start(bf16[1040,128]{1,0:T(8,128)(2,1)S(1)} %get-tuple-element.29), channel_id=1, source_target_pairs={{1,0},{0,1},{3,2},{2,3},{5,4},{4,5},{7,6},{6,7},{9,8},{8,9},{11,10... | collective-permute-start | bytes 798728 | tf_op jit(solution)/shard_map/ppermute | solution.py:259
  2.1 3.1 %collective-permute-start.5 = (bf16[2064,128]{1,0:T(8,128)(2,1)S(1)}, bf16[2064,128]{1,0:T(8,128)(2,1)S(1)}, u32[]{:S(2)}, u32[]{:S(2)}) collective-permute-start(bf16[2064,128]{1,0:T(8,128)(2,1)S(1)} %get-tuple-element.22.own_ref), channel_id=1, source_target_pairs={{2,0},{4,2},{1,3},{6,4},{3,5},{8,6},{5,7},{10,8},{7,9},{12,10},{9,... | collective-permute-start | bytes 1585160 | tf_op jit(solution)/shard_map/ppermute | solution.py:259
  5.2 2.4 %collective-permute-start.1 = (bf16[2064,128]{1,0:T(8,128)(2,1)S(1)}, bf16[2064,128]{1,0:T(8,128)(2,1)S(1)}, u32[]{:S(2)}, u32[]{:S(2)}) collective-permute-start(bf16[2064,128]{1,0:T(8,128)(2,1)S(1)} %get-tuple-element.22.own_ref), channel_id=1, source_target_pairs={{4,1},{6,3},{1,4},{8,5},{3,6},{10,7},{5,8},{12,9},{7,10},{14,11},{... | collective-permute-start | bytes 1585160 | tf_op jit(solution)/shard_map/ppermute | solution.py:259
  7.6 1.1 %collective-permute-start.2 = (bf16[1040,128]{1,0:T(8,128)(2,1)S(1)}, bf16[1040,128]{1,0:T(8,128)(2,1)S(1)}, u32[]{:S(2)}, u32[]{:S(2)}) collective-permute-start(bf16[1040,128]{1,0:T(8,128)(2,1)S(1)} %get-tuple-element.28), channel_id=1, source_target_pairs={{1,0},{0,1},{3,2},{2,3},{5,4},{4,5},{7,6},{6,7},{9,8},{8,9},{11,10... | collective-permute-start | bytes 798728 | tf_op jit(solution)/shard_map/ppermute | solution.py:259
  8.7 3.1 %shard_map.38 = (bf16[4,256,1024]{2,1,0:T(8,128)(2,1)S(1)}, f32[4,128,512]{2,1,0:T(8,128)S(1)}) custom-call(bf16[2064,128]{1,0:T(8,128)(2,1)S(1)} %get-tuple-element.22.own_ref, bf16[1040,128]{1,0:T(8,128)(2,1)S(1)} %collective-permute-done.pair_ref), custom_call_target="tpu_custom_call" | custom-call | flops 8589934592 | bytes 2097152 | tf_op jit(solution)/shard_map/pallas_call | solution.py:227
  11.8 0.0 collective-permute-done.2.refs_0_
  11.8 1.2 %shard_map.39.refs_1_ = f32[4,128,512]{2,1,0:T(8,128)S(1)} custom-call(bf16[4,256,1024]{2,1,0:T(8,128)(2,1)S(1)} %get-tuple-element.24.query_ref, bf16[1040,128]{1,0:T(8,128)(2,1)S(1)} %collective-permute-done.2.refs_0_, f32[4,128,512]{2,1,0:T(8,128)S(1)} %get-tuple-element.27.refs_1_), custom_call_target="tpu_custom_call" | custom-call | flops 8589934592 | bytes 2097152 | tf_op jit(solution)/shard_map/pallas_call | solution.py:243
  13.0 2.2 %collective-permute-start.4 = (bf16[1040,128]{1,0:T(8,128)(2,1)S(1)}, bf16[1040,128]{1,0:T(8,128)(2,1)S(1)}, u32[]{:S(2)}, u32[]{:S(2)}) collective-permute-start(bf16[1040,128]{1,0:T(8,128)(2,1)S(1)} %get-tuple-element.29), channel_id=1, source_target_pairs={{3,1},{0,2},{5,3},{2,4},{7,5},{4,6},{9,7},{6,8},{11,9},{8,10},{13,... | collective-permute-start | bytes 798728 | tf_op jit(solution)/shard_map/ppermute | solution.py:259
  15.1 3.2 %collective-permute-start.3 = (bf16[1040,128]{1,0:T(8,128)(2,1)S(1)}, bf16[1040,128]{1,0:T(8,128)(2,1)S(1)}, u32[]{:S(2)}, u32[]{:S(2)}) collective-permute-start(bf16[1040,128]{1,0:T(8,128)(2,1)S(1)} %get-tuple-element.28), channel_id=1, source_target_pairs={{3,1},{0,2},{5,3},{2,4},{7,5},{4,6},{9,7},{6,8},{11,9},{8,10},{13,... | collective-permute-start | bytes 798728 | tf_op jit(solution)/shard_map/ppermute | solution.py:259
  18.4 0.0 collective-permute-done.5.refs_0_
  18.4 2.8 %collective-permute-start.6 = (bf16[2064,128]{1,0:T(8,128)(2,1)S(1)}, bf16[2064,128]{1,0:T(8,128)(2,1)S(1)}, u32[]{:S(2)}, u32[]{:S(2)}) collective-permute-start(bf16[2064,128]{1,0:T(8,128)(2,1)S(1)} %collective-permute-done.5.refs_0_), channel_id=1, source_target_pairs={{1,0},{0,1},{3,2},{2,3},{5,4},{4,5},{7,6},{6,7},{9,8},{8,9},{11,10... | collective-permute-start | bytes 1585160 | tf_op jit(solution)/shard_map/ppermute | solution.py:259
  21.2 2.1 %shard_map.40.refs_1_ = f32[4,128,512]{2,1,0:T(8,128)S(1)} custom-call(bf16[4,256,1024]{2,1,0:T(8,128)(2,1)S(1)} %get-tuple-element.24.query_ref, bf16[2064,128]{1,0:T(8,128)(2,1)S(1)} %collective-permute-done.5.refs_0_, f32[4,128,512]{2,1,0:T(8,128)S(1)} %shard_map.39.refs_1_), custom_call_target="tpu_custom_call" | custom-call | flops 8589934592 | bytes 2097152 | tf_op jit(solution)/shard_map/pallas_call | solution.py:243
  23.3 2.1 %shard_map.41.refs_1_ = f32[4,128,512]{2,1,0:T(8,128)S(1)} custom-call(bf16[4,256,1024]{2,1,0:T(8,128)(2,1)S(1)} %get-tuple-element.24.query_ref, bf16[2064,128]{1,0:T(8,128)(2,1)S(1)} %collective-permute-done.6.refs_0_, f32[4,128,512]{2,1,0:T(8,128)S(1)} %shard_map.40.refs_1_), custom_call_target="tpu_custom_call" | custom-call | flops 8589934592 | bytes 2097152 | tf_op jit(solution)/shard_map/pallas_call | solution.py:243
  25.4 0.0 collective-permute-done.4.refs_0_
  25.4 0.1 collective-permute-start.7
  25.5 1.2 %shard_map.42.refs_1_ = f32[4,128,512]{2,1,0:T(8,128)S(1)} custom-call(bf16[4,256,1024]{2,1,0:T(8,128)(2,1)S(1)} %get-tuple-element.24.query_ref, bf16[1040,128]{1,0:T(8,128)(2,1)S(1)} %collective-permute-done.4.refs_0_, f32[4,128,512]{2,1,0:T(8,128)S(1)} %shard_map.41.refs_1_), custom_call_target="tpu_custom_call" | custom-call | flops 8589934592 | bytes 2097152 | tf_op jit(solution)/shard_map/pallas_call | solution.py:243
  26.7 0.4 collective-permute-done.7.refs_0_
  27.0 1.2 %shard_map.43.refs_1_ = f32[4,128,512]{2,1,0:T(8,128)S(1)} custom-call(bf16[4,256,1024]{2,1,0:T(8,128)(2,1)S(1)} %get-tuple-element.24.query_ref, bf16[1040,128]{1,0:T(8,128)(2,1)S(1)} %collective-permute-done.7.refs_0_, f32[4,128,512]{2,1,0:T(8,128)S(1)} %shard_map.42.refs_1_), custom_call_target="tpu_custom_call" | custom-call | flops 8589934592 | bytes 2097152 | tf_op jit(solution)/shard_map/pallas_call | solution.py:243
  28.2 2.1 %collective-permute-done.3.refs_0_ = bf16[1040,128]{1,0:T(8,128)(2,1)S(1)} collective-permute-done((bf16[1040,128]{1,0:T(8,128)(2,1)S(1)}, bf16[1040,128]{1,0:T(8,128)(2,1)S(1)}, u32[]{:S(2)}, u32[]{:S(2)}) %collective-permute-start.3) | collective-permute-done | bytes 266272 | tf_op jit(solution)/shard_map/ppermute | solution.py:259
  30.3 1.2 %shard_map.44.refs_1_ = f32[4,128,512]{2,1,0:T(8,128)S(1)} custom-call(bf16[4,256,1024]{2,1,0:T(8,128)(2,1)S(1)} %get-tuple-element.24.query_ref, bf16[1040,128]{1,0:T(8,128)(2,1)S(1)} %collective-permute-done.3.refs_0_, f32[4,128,512]{2,1,0:T(8,128)S(1)} %shard_map.43.refs_1_), custom_call_target="tpu_custom_call" | custom-call | flops 8589934592 | bytes 2097152 | tf_op jit(solution)/shard_map/pallas_call | solution.py:243
  31.5 0.4 %collective-permute-done.8.refs_0_ = bf16[1040,128]{1,0:T(8,128)(2,1)S(1)} collective-permute-done((bf16[1040,128]{1,0:T(8,128)(2,1)S(1)}, bf16[1040,128]{1,0:T(8,128)(2,1)S(1)}, u32[]{:S(2)}, u32[]{:S(2)}) %collective-permute-start.8) | collective-permute-done | bytes 266272 | tf_op jit(solution)/shard_map/ppermute | solution.py:259
  31.8 1.2 %shard_map.45.refs_1_ = f32[4,128,512]{2,1,0:T(8,128)S(1)} custom-call(bf16[4,256,1024]{2,1,0:T(8,128)(2,1)S(1)} %get-tuple-element.24.query_ref, bf16[1040,128]{1,0:T(8,128)(2,1)S(1)} %collective-permute-done.8.refs_0_, f32[4,128,512]{2,1,0:T(8,128)S(1)} %shard_map.44.refs_1_), custom_call_target="tpu_custom_call" | custom-call | flops 8589934592 | bytes 2097152 | tf_op jit(solution)/shard_map/pallas_call | solution.py:243
  33.0 2.9 %shard_map.46 = f32[4,512,128]{2,1,0:T(8,128)} custom-call(bf16[4,256,1024]{2,1,0:T(8,128)(2,1)S(1)} %get-tuple-element.24.query_ref, bf16[2064,128]{1,0:T(8,128)(2,1)S(1)} %collective-permute-done.1.refs_0_, f32[4,128,512]{2,1,0:T(8,128)S(1)} %shard_map.45.refs_1_), custom_call_target="tpu_custom_call" | custom-call | flops 8589934592 | bytes 2097152 | tf_op jit(solution)/shard_map/pallas_call | solution.py:243
  (4 shorter events, 0.0 us)
Async XLA Ops:
  1.3 7.4 %collective-permute-start = (bf16[1040,128]{1,0:T(8,128)(2,1)S(1)}, bf16[1040,128]{1,0:T(8,128)(2,1)S(1)}, u32[]{:S(2)}, u32[]{:S(2)}) collective-permute-start(bf16[1040,128]{1,0:T(8,128)(2,1)S(1)} %get-tuple-element.29), channel_id=1, source_target_pairs={{1,0},{0,1},{3,2},{2,3},{5,4},{4,5},{7,6},{6,7},{9,8},{8,9},{11,10... | collective-permute-start | bytes 798728 | tf_op jit(solution)/shard_map/ppermute | solution.py:259
  2.1 16.3 %collective-permute-start.5 = (bf16[2064,128]{1,0:T(8,128)(2,1)S(1)}, bf16[2064,128]{1,0:T(8,128)(2,1)S(1)}, u32[]{:S(2)}, u32[]{:S(2)}) collective-permute-start(bf16[2064,128]{1,0:T(8,128)(2,1)S(1)} %get-tuple-element.22.own_ref), channel_id=1, source_target_pairs={{2,0},{4,2},{1,3},{6,4},{3,5},{8,6},{5,7},{10,8},{7,9},{12,10},{9,... | collective-permute-start | bytes 1585160 | tf_op jit(solution)/shard_map/ppermute | solution.py:259
  5.2 27.8 %collective-permute-start.1 = (bf16[2064,128]{1,0:T(8,128)(2,1)S(1)}, bf16[2064,128]{1,0:T(8,128)(2,1)S(1)}, u32[]{:S(2)}, u32[]{:S(2)}) collective-permute-start(bf16[2064,128]{1,0:T(8,128)(2,1)S(1)} %get-tuple-element.22.own_ref), channel_id=1, source_target_pairs={{4,1},{6,3},{1,4},{8,5},{3,6},{10,7},{5,8},{12,9},{7,10},{14,11},{... | collective-permute-start | bytes 1585160 | tf_op jit(solution)/shard_map/ppermute | solution.py:259
  7.6 4.2 %collective-permute-start.2 = (bf16[1040,128]{1,0:T(8,128)(2,1)S(1)}, bf16[1040,128]{1,0:T(8,128)(2,1)S(1)}, u32[]{:S(2)}, u32[]{:S(2)}) collective-permute-start(bf16[1040,128]{1,0:T(8,128)(2,1)S(1)} %get-tuple-element.28), channel_id=1, source_target_pairs={{1,0},{0,1},{3,2},{2,3},{5,4},{4,5},{7,6},{6,7},{9,8},{8,9},{11,10... | collective-permute-start | bytes 798728 | tf_op jit(solution)/shard_map/ppermute | solution.py:259
  13.0 12.4 %collective-permute-start.4 = (bf16[1040,128]{1,0:T(8,128)(2,1)S(1)}, bf16[1040,128]{1,0:T(8,128)(2,1)S(1)}, u32[]{:S(2)}, u32[]{:S(2)}) collective-permute-start(bf16[1040,128]{1,0:T(8,128)(2,1)S(1)} %get-tuple-element.29), channel_id=1, source_target_pairs={{3,1},{0,2},{5,3},{2,4},{7,5},{4,6},{9,7},{6,8},{11,9},{8,10},{13,... | collective-permute-start | bytes 798728 | tf_op jit(solution)/shard_map/ppermute | solution.py:259
  15.1 15.1 %collective-permute-start.3 = (bf16[1040,128]{1,0:T(8,128)(2,1)S(1)}, bf16[1040,128]{1,0:T(8,128)(2,1)S(1)}, u32[]{:S(2)}, u32[]{:S(2)}) collective-permute-start(bf16[1040,128]{1,0:T(8,128)(2,1)S(1)} %get-tuple-element.28), channel_id=1, source_target_pairs={{3,1},{0,2},{5,3},{2,4},{7,5},{4,6},{9,7},{6,8},{11,9},{8,10},{13,... | collective-permute-start | bytes 798728 | tf_op jit(solution)/shard_map/ppermute | solution.py:259
  18.4 4.9 %collective-permute-start.6 = (bf16[2064,128]{1,0:T(8,128)(2,1)S(1)}, bf16[2064,128]{1,0:T(8,128)(2,1)S(1)}, u32[]{:S(2)}, u32[]{:S(2)}) collective-permute-start(bf16[2064,128]{1,0:T(8,128)(2,1)S(1)} %collective-permute-done.5.refs_0_), channel_id=1, source_target_pairs={{1,0},{0,1},{3,2},{2,3},{5,4},{4,5},{7,6},{6,7},{9,8},{8,9},{11,10... | collective-permute-start | bytes 1585160 | tf_op jit(solution)/shard_map/ppermute | solution.py:259
  25.4 1.6 %collective-permute-start.7 = (bf16[1040,128]{1,0:T(8,128)(2,1)S(1)}, bf16[1040,128]{1,0:T(8,128)(2,1)S(1)}, u32[]{:S(2)}, u32[]{:S(2)}) collective-permute-start(bf16[1040,128]{1,0:T(8,128)(2,1)S(1)} %collective-permute-done.4.refs_0_), channel_id=1, source_target_pairs={{1,0},{0,1},{3,2},{2,3},{5,4},{4,5},{7,6},{6,7},{9,8},{8,9},{11,10... | collective-permute-start | bytes 798728 | tf_op jit(solution)/shard_map/ppermute | solution.py:259
  30.3 1.5 %collective-permute-start.8 = (bf16[1040,128]{1,0:T(8,128)(2,1)S(1)}, bf16[1040,128]{1,0:T(8,128)(2,1)S(1)}, u32[]{:S(2)}, u32[]{:S(2)}) collective-permute-start(bf16[1040,128]{1,0:T(8,128)(2,1)S(1)} %collective-permute-done.3.refs_0_), channel_id=1, source_target_pairs={{1,0},{0,1},{3,2},{2,3},{5,4},{4,5},{7,6},{6,7},{9,8},{8,9},{11,10... | collective-permute-start | bytes 798728 | tf_op jit(solution)/shard_map/ppermute | solution.py:259

commit v5 on v4

--- a/solution.py
+++ b/solution.py
@@ -12,6 +12,7 @@
 period_metres = 4096
 model_amp = 0.5
 vmem = 24 << 20
+shares = (24, 8, 96, 2, 64, 64, 192, 2)
 
 OWN = (0, 0)
 PAIR = (1, -1)
@@ -159,10 +160,11 @@
         query_ref[f, width:, channels:] = jnp.where(mine, imag, 0.0).astype(jnp.bfloat16)
 
 
-def band_sums(query_ref, keys, f, extra, first=0):
+def band_sums(query_ref, f, keys):
     channels = query_ref.shape[2] // 2
-    spectra = [key_ref[pl.ds((f - first) * channels, channels), :] for key_ref in keys]
+    spectra = [ref[pl.ds((f - first) * channels, channels), :] for ref, first, _ in keys]
     spectra = spectra[0] if len(keys) == 1 else jnp.concatenate(spectra, axis=0)
+    extra = [columns for _, _, columns in keys]
     extra = extra[0] if len(keys) == 1 else jnp.concatenate(extra, axis=0)
     misfit = jnp.dot(
         jnp.concatenate([spectra, extra], axis=1), query_ref[f], preferred_element_type=jnp.float32
@@ -178,54 +180,64 @@
     return key_columns(tail_ref, block, freqs, channels, width)
 
 
-def chip_kernel(axis, left, own_ref, pair_ref, query_ref, total_ref):
+def chip_kernel(axis, low, own_ref, pair_ref, query_ref, total_ref):
     freqs, width, channels = total_ref.shape
     own, pair = block_of(axis, OWN), block_of(axis, PAIR)
     fill_queries(own_ref, query_ref, own)
     own_columns = columns_of(own_ref, own, freqs, channels, width)
     pair_columns = columns_of(pair_ref, pair, freqs, channels, width)
     for f in range(freqs):
-        term = 2.0 * band_sums(query_ref, [own_ref], f, [own_columns])
-        if f < freqs - left:
-            term = term + band_sums(query_ref, [pair_ref], f, [pair_columns])
+        term = 2.0 * band_sums(query_ref, f, [(own_ref, 0, own_columns)])
+        if f < low:
+            term = term + band_sums(query_ref, f, [(pair_ref, 0, pair_columns)])
         total_ref[f] = term * (2.0 / width)
 
 
-def band_kernel(axis, places, first, count, last, query_ref, *refs):
-    keys, (total_ref, out_ref) = refs[: len(places)], refs[len(places) : len(places) + 2]
-    freqs, width, channels = total_ref.shape
+def holds(span, f):
+    return span[0] <= f < span[0] + span[1]
+
+
+def band_kernel(axis, places, spans, held, span, last, query_ref, *refs):
+    keys, refs = refs[: len(places)], refs[len(places) :]
+    total_refs, out_refs = refs[: len(held)], refs[len(held) :]
+    freqs = query_ref.shape[0]
+    _, width, channels = total_refs[0].shape
     extra = [
         columns_of(key_ref, block_of(axis, place), freqs, channels, width)
         for key_ref, place in zip(keys, places)
     ]
     copies = []
-    for f in range(freqs):
-        term = total_ref[f]
-        if first <= f < first + count:
-            term = term + band_sums(query_ref, keys, f, extra, first) * (2.0 / width)
+    for f in range(span[0], span[0] + span[1]):
+        used = [
+            (key_ref, part[0], columns)
+            for key_ref, part, columns in zip(keys, spans, extra)
+            if holds(part, f)
+        ]
+        total = next(ref[f - part[0]] for ref, part in zip(total_refs, held) if holds(part, f))
+        term = total + band_sums(query_ref, f, used) * (2.0 / width)
         if last:
-            result_ref, sems = refs[len(places) + 2 :]
+            out_ref, result_ref, sems = out_refs
             result_ref[f] = term.T
             copies.append(pltpu.make_async_copy(result_ref.at[f], out_ref.at[f], sems.at[f]))
-            copies[f].start()
+            copies[-1].start()
         else:
-            out_ref[f] = term
+            out_refs[0][f - span[0]] = term
     for copy in copies:
         copy.wait()
 
 
-def cost(shape, blocks):
-    pairs = blocks * shape[0] * shape[1] * shape[1]
+def cost(shape, share):
+    pairs = shape[0] * shape[1] * shape[1]
     return pl.CostEstimate(
-        flops=64 * pairs * shape[2], bytes_accessed=1 << 21, transcendentals=2 * pairs
+        flops=share * pairs * shape[2], bytes_accessed=1 << 21, transcendentals=2 * pairs
     )
 
 
-def chip_terms(shape, axis, own, pair, left):
+def chip_terms(shape, axis, low, own, pair, share):
     freqs, channels, width = shape
     whole = pl.BlockSpec(memory_space=pltpu.VMEM)
     return pl.pallas_call(
-        functools.partial(chip_kernel, axis, left),
+        functools.partial(chip_kernel, axis, low),
         out_shape=[
             jax.ShapeDtypeStruct((freqs, 2 * width, 2 * channels), jnp.bfloat16),
             jax.ShapeDtypeStruct((freqs, width, channels), jnp.float32),
@@ -233,22 +245,26 @@
         in_specs=[whole, whole],
         out_specs=[whole, whole],
         compiler_params=pltpu.CompilerParams(vmem_limit_bytes=vmem),
-        cost_estimate=cost(shape, 1),
+        cost_estimate=cost(shape, share),
     )(own, pair)
 
 
-def band_terms(shape, axis, query, total, keys, places, part=None, last=False):
+def band_terms(shape, axis, query, totals, keys, span, share, last=False):
+    freqs, channels, width = shape
     whole = pl.BlockSpec(memory_space=pltpu.VMEM)
-    scratch = [pltpu.VMEM(shape, jnp.float32), pltpu.SemaphoreType.DMA((shape[0],))]
+    out = shape if last else (span[1], width, channels)
+    scratch = [pltpu.VMEM(shape, jnp.float32), pltpu.SemaphoreType.DMA((freqs,))]
+    places, spans = tuple(key[1] for key in keys), tuple(key[2] for key in keys)
+    held = tuple(total[1] for total in totals)
     return pl.pallas_call(
-        functools.partial(band_kernel, axis, tuple(places), *(part or (0, shape[0])), last),
-        out_shape=jax.ShapeDtypeStruct(shape if last else total.shape, jnp.float32),
-        in_specs=[whole] * (len(keys) + 2),
+        functools.partial(band_kernel, axis, places, spans, held, span, last),
+        out_shape=jax.ShapeDtypeStruct(out, jnp.float32),
+        in_specs=[whole] * (1 + len(keys) + len(totals)),
         out_specs=pl.BlockSpec(memory_space=pl.ANY) if last else whole,
         scratch_shapes=scratch if last else [],
         compiler_params=pltpu.CompilerParams(vmem_limit_bytes=vmem),
-        cost_estimate=cost(shape, len(keys)),
-    )(query, *keys, total)
+        cost_estimate=cost(shape, share),
+    )(query, *(key[0] for key in keys), *(total[0] for total in totals))
 
 
 def local(axis, count, spectra, offsets, bins):
@@ -259,31 +275,34 @@
         return lax.ppermute(value, axis, [(i, t) for i, t in sources if 0 <= i < count])
 
     left = shape[0] // 2
-    low, high = (0, shape[0] - left), (shape[0] - left, left)
-    own, own_low, own_high = pack(spectra, offsets, bins, (shape[0] - left, left))
+    every, low, high = (0, shape[0]), (0, shape[0] - left), (shape[0] - left, left)
+    own, own_low, own_high = pack(spectra, offsets, bins, (low[1], high[1]))
     near = fetched(own, NEAR)
     far = fetched(own, FAR)
     pair_low = fetched(own_low, PAIR)
     pair_high = fetched(own_high, PAIR)
 
-    query, total = chip_terms(shape, axis, own, pair_low, left)
+    query, total = chip_terms(shape, axis, low[1], own, pair_low, shares[0])
     terms = functools.partial(band_terms, shape, axis, query)
     own_low, total = lax.optimization_barrier((own_low, total))
     cross_low = fetched(own_low, CROSS)
-    total = terms(total, [pair_high], [PAIR], part=high)
-    own_high, total = lax.optimization_barrier((own_high, total))
+    rest = terms([(total, every)], [(pair_high, PAIR, high)], high, shares[1])
+    own_high, rest = lax.optimization_barrier((own_high, rest))
     cross_high = fetched(own_high, CROSS)
-    near, total = lax.optimization_barrier((near, total))
+    near, rest = lax.optimization_barrier((near, rest))
     near_pair = fetched(near, PAIR)
-    total = terms(total, [near], [NEAR])
-    total = terms(total, [near_pair], [NEAR_OF_PAIR])
-    for cross, part in ((cross_low, low), (cross_high, high)):
-        cross, total = lax.optimization_barrier((cross, total))
-        cross_pair = fetched(cross, PAIR)
-        total = terms(total, [cross], [CROSS], part=part)
-        total = terms(total, [cross_pair], [CROSS_OF_PAIR], part=part)
-    far, total = lax.optimization_barrier((far, total))
-    return terms(total, [far], [FAR], last=True)
+    total = terms([(rest, high), (total, every)], [(near, NEAR, every)], every, shares[2])
+    total = terms([(total, every)], [(near_pair, NEAR_OF_PAIR, every)], every, shares[3])
+    cross_high, total = lax.optimization_barrier((cross_high, total))
+    high_pair = fetched(cross_high, PAIR)
+    rest = terms([(total, every)], [(cross_high, CROSS, high)], high, shares[4])
+    rest = terms([(rest, high)], [(high_pair, CROSS_OF_PAIR, high)], high, shares[5])
+    cross_low, rest = lax.optimization_barrier((cross_low, rest))
+    low_pair = fetched(cross_low, PAIR)
+    first = terms([(total, every)], [(cross_low, CROSS, low)], low, shares[6])
+    far, first = lax.optimization_barrier((far, first))
+    closing = [(low_pair, CROSS_OF_PAIR, low), (far, FAR, every)]
+    return terms([(first, low), (rest, high)], closing, every, shares[7], last=True)
 
 
 def solution(mesh):

time: 36.3 us -> 35.9 us (0.989)
  Pallas kernels: 17.4 us -> 16.9 us
    pallas_call x9 -> x8, Pallas kernels: 16 us -> 15.6 us  [the longest x7 12.5 us: band_terms(): pl.pallas_call(functools.partial(band_kernel, axis, places, spans, held,...]
  transfers between devices with their start and end apart: 9 -> 9, of which waited for: 3 -> 4; matrix products, arithmetic and copies ran while one was open for 0% -> 0% of each run, Pallas kernels for 36% -> 33%
where the time goes in v5:
time: 35.9 us; the launch traced here: 35.7 us
  Pallas kernels  16.9 us (47%)
  starting transfers between devices  15.7 us (44%)
  waiting for transfers between devices  2.85 us (8%)
    ppermute x9, starting transfers between devices, fetched(): lax.ppermute(value, axis, [(i, t) for i, t in sources if 0 <= i < count])  15.7 us
    pallas_call x7, Pallas kernels, band_terms(): pl.pallas_call(functools.partial(band_kernel, axis, places, spans, held,...  12.5 us
    pallas_call x1, Pallas kernels, chip_terms(): pl.pallas_call(functools.partial(chip_kernel, axis, low), out_shape=[jax....  3.11 us
    ppermute x9, waiting for transfers between devices, fetched(): lax.ppermute(value, axis, [(i, t) for i, t in sources if 0 <= i < count])  2.85 us
    pallas_call x1, Pallas kernels, pack(): pl.pallas_call(pack_kernel, out_shape=[jax.ShapeDtypeStruct((part * chann...  1.31 us
  transfers between devices with their start and end apart: 9, of which 4 were waited for; matrix products, arithmetic and copies ran while one was open for 0% of the time, Pallas kernels for 33%

profile of v5, /device:TPU:19, one launch (start us, length us, event | category | flops | bytes accessed | tf_op | source)
XLA Modules:
  0.0 35.7 jit_solution(2165473494298651928)
XLA Ops:
  0.0 1.3 %shard_map.37 = (bf16[2064,128]{1,0:T(8,128)(2,1)S(1)}, bf16[1040,128]{1,0:T(8,128)(2,1)S(1)}, bf16[1040,128]{1,0:T(8,128)(2,1)S(1)}) custom-call(bf16[2048,128]{1,0:T(8,128)(2,1)} %bitcast.2, s32[1,512]{1,0:T(1,128)} %bitcast.3, s32[4]{0:T(128)} %bins_ref.1), custom_call_target="tpu_custom_call" | custom-call | bytes 1048576 | tf_op jit(solution)/shard_map/pallas_call | solution.py:126
  1.3 0.7 %collective-permute-start = (bf16[1040,128]{1,0:T(8,128)(2,1)S(1)}, bf16[1040,128]{1,0:T(8,128)(2,1)S(1)}, u32[]{:S(2)}, u32[]{:S(2)}) collective-permute-start(bf16[1040,128]{1,0:T(8,128)(2,1)S(1)} %get-tuple-element.26), channel_id=1, source_target_pairs={{1,0},{0,1},{3,2},{2,3},{5,4},{4,5},{7,6},{6,7},{9,8},{8,9},{11,10... | collective-permute-start | bytes 798728 | tf_op jit(solution)/shard_map/ppermute | solution.py:275
  2.1 3.1 %collective-permute-start.4 = (bf16[2064,128]{1,0:T(8,128)(2,1)S(1)}, bf16[2064,128]{1,0:T(8,128)(2,1)S(1)}, u32[]{:S(2)}, u32[]{:S(2)}) collective-permute-start(bf16[2064,128]{1,0:T(8,128)(2,1)S(1)} %get-tuple-element.22.own_ref), channel_id=1, source_target_pairs={{2,0},{4,2},{1,3},{6,4},{3,5},{8,6},{5,7},{10,8},{7,9},{12,10},{9,... | collective-permute-start | bytes 1585160 | tf_op jit(solution)/shard_map/ppermute | solution.py:275
  5.2 2.4 %collective-permute-start.8 = (bf16[2064,128]{1,0:T(8,128)(2,1)S(1)}, bf16[2064,128]{1,0:T(8,128)(2,1)S(1)}, u32[]{:S(2)}, u32[]{:S(2)}) collective-permute-start(bf16[2064,128]{1,0:T(8,128)(2,1)S(1)} %get-tuple-element.22.own_ref), channel_id=1, source_target_pairs={{4,1},{6,3},{1,4},{8,5},{3,6},{10,7},{5,8},{12,9},{7,10},{14,11},{... | collective-permute-start | bytes 1585160 | tf_op jit(solution)/shard_map/ppermute | solution.py:275
  7.6 1.1 %collective-permute-start.2 = (bf16[1040,128]{1,0:T(8,128)(2,1)S(1)}, bf16[1040,128]{1,0:T(8,128)(2,1)S(1)}, u32[]{:S(2)}, u32[]{:S(2)}) collective-permute-start(bf16[1040,128]{1,0:T(8,128)(2,1)S(1)} %get-tuple-element.29), channel_id=1, source_target_pairs={{1,0},{0,1},{3,2},{2,3},{5,4},{4,5},{7,6},{6,7},{9,8},{8,9},{11,10... | collective-permute-start | bytes 798728 | tf_op jit(solution)/shard_map/ppermute | solution.py:275
  8.7 3.1 %shard_map.38 = (bf16[4,256,1024]{2,1,0:T(8,128)(2,1)S(1)}, f32[4,128,512]{2,1,0:T(8,128)S(1)}) custom-call(bf16[2064,128]{1,0:T(8,128)(2,1)S(1)} %get-tuple-element.22.own_ref, bf16[1040,128]{1,0:T(8,128)(2,1)S(1)} %collective-permute-done.pair_ref), custom_call_target="tpu_custom_call" | custom-call | flops 3221225472 | bytes 2097152 | tf_op jit(solution)/shard_map/pallas_call | solution.py:239
  11.8 0.0 collective-permute-done.2.refs_0_
  11.8 1.2 %shard_map.39.refs_1_ = f32[2,128,512]{2,1,0:T(8,128)S(1)} custom-call(bf16[4,256,1024]{2,1,0:T(8,128)(2,1)S(1)} %get-tuple-element.24.query_ref, bf16[1040,128]{1,0:T(8,128)(2,1)S(1)} %collective-permute-done.2.refs_0_, f32[4,128,512]{2,1,0:T(8,128)S(1)} %get-tuple-element.28.refs_1_.refs_2_), custom_call_target="tpu_custom_call" | custom-call | flops 1073741824 | bytes 2097152 | tf_op jit(solution)/shard_map/pallas_call | solution.py:259
  13.0 2.2 %collective-permute-start.3 = (bf16[1040,128]{1,0:T(8,128)(2,1)S(1)}, bf16[1040,128]{1,0:T(8,128)(2,1)S(1)}, u32[]{:S(2)}, u32[]{:S(2)}) collective-permute-start(bf16[1040,128]{1,0:T(8,128)(2,1)S(1)} %get-tuple-element.29), channel_id=1, source_target_pairs={{3,1},{0,2},{5,3},{2,4},{7,5},{4,6},{9,7},{6,8},{11,9},{8,10},{13,... | collective-permute-start | bytes 798728 | tf_op jit(solution)/shard_map/ppermute | solution.py:275
  15.1 3.2 %collective-permute-start.1 = (bf16[1040,128]{1,0:T(8,128)(2,1)S(1)}, bf16[1040,128]{1,0:T(8,128)(2,1)S(1)}, u32[]{:S(2)}, u32[]{:S(2)}) collective-permute-start(bf16[1040,128]{1,0:T(8,128)(2,1)S(1)} %get-tuple-element.26), channel_id=1, source_target_pairs={{3,1},{0,2},{5,3},{2,4},{7,5},{4,6},{9,7},{6,8},{11,9},{8,10},{13,... | collective-permute-start | bytes 798728 | tf_op jit(solution)/shard_map/ppermute | solution.py:275
  18.4 2.8 %collective-permute-start.5 = (bf16[2064,128]{1,0:T(8,128)(2,1)S(1)}, bf16[2064,128]{1,0:T(8,128)(2,1)S(1)}, u32[]{:S(2)}, u32[]{:S(2)}) collective-permute-start(bf16[2064,128]{1,0:T(8,128)(2,1)S(1)} %collective-permute-done.4.refs_0_), channel_id=1, source_target_pairs={{1,0},{0,1},{3,2},{2,3},{5,4},{4,5},{7,6},{6,7},{9,8},{8,9},{11,10... | collective-permute-start | bytes 1585160 | tf_op jit(solution)/shard_map/ppermute | solution.py:275
  21.2 2.1 %shard_map.40.refs_1_ = f32[4,128,512]{2,1,0:T(8,128)S(1)} custom-call(bf16[4,256,1024]{2,1,0:T(8,128)(2,1)S(1)} %get-tuple-element.24.query_ref, bf16[2064,128]{1,0:T(8,128)(2,1)S(1)} %collective-permute-done.4.refs_0_, f32[2,128,512]{2,1,0:T(8,128)S(1)} %shard_map.39.refs_1_, f32[4,128,512]{2,1,0:T(8,128)S(1)} %get-tuple-element.28.refs_1_.refs_2_), custom_call_target="tpu_custom_call" | custom-call | flops 12884901888 | bytes 2097152 | tf_op jit(solution)/shard_map/pallas_call | solution.py:259
  23.3 0.0 collective-permute-done.5.refs_0_
  23.3 2.1 %shard_map.41.refs_1_ = f32[4,128,512]{2,1,0:T(8,128)S(1)} custom-call(bf16[4,256,1024]{2,1,0:T(8,128)(2,1)S(1)} %get-tuple-element.24.query_ref, bf16[2064,128]{1,0:T(8,128)(2,1)S(1)} %collective-permute-done.5.refs_0_, f32[4,128,512]{2,1,0:T(8,128)S(1)} %shard_map.40.refs_1_), custom_call_target="tpu_custom_call" | custom-call | flops 268435456 | bytes 2097152 | tf_op jit(solution)/shard_map/pallas_call | solution.py:259
  25.4 0.0 collective-permute-done.3.refs_0_
  25.4 0.1 collective-permute-start.6
  25.5 1.2 %shard_map.42.refs_1_ = f32[2,128,512]{2,1,0:T(8,128)S(1)} custom-call(bf16[4,256,1024]{2,1,0:T(8,128)(2,1)S(1)} %get-tuple-element.24.query_ref, bf16[1040,128]{1,0:T(8,128)(2,1)S(1)} %collective-permute-done.3.refs_0_, f32[4,128,512]{2,1,0:T(8,128)S(1)} %shard_map.41.refs_1_), custom_call_target="tpu_custom_call" | custom-call | flops 8589934592 | bytes 2097152 | tf_op jit(solution)/shard_map/pallas_call | solution.py:259
  26.7 0.4 %collective-permute-done.6.refs_0_ = bf16[1040,128]{1,0:T(8,128)(2,1)S(1)} collective-permute-done((bf16[1040,128]{1,0:T(8,128)(2,1)S(1)}, bf16[1040,128]{1,0:T(8,128)(2,1)S(1)}, u32[]{:S(2)}, u32[]{:S(2)}) %collective-permute-start.6) | collective-permute-done | bytes 266272 | tf_op jit(solution)/shard_map/ppermute | solution.py:275
  27.0 1.1 %shard_map.43.refs_3_ = f32[2,128,512]{2,1,0:T(8,128)S(1)} custom-call(bf16[4,256,1024]{2,1,0:T(8,128)(2,1)S(1)} %get-tuple-element.24.query_ref, bf16[1040,128]{1,0:T(8,128)(2,1)S(1)} %collective-permute-done.6.refs_0_, f32[2,128,512]{2,1,0:T(8,128)S(1)} %shard_map.42.refs_1_), custom_call_target="tpu_custom_call" | custom-call | flops 8589934592 | bytes 2097152 | tf_op jit(solution)/shard_map/pallas_call | solution.py:259
  28.2 2.1 %collective-permute-done.1.refs_0_ = bf16[1040,128]{1,0:T(8,128)(2,1)S(1)} collective-permute-done((bf16[1040,128]{1,0:T(8,128)(2,1)S(1)}, bf16[1040,128]{1,0:T(8,128)(2,1)S(1)}, u32[]{:S(2)}, u32[]{:S(2)}) %collective-permute-start.1) | collective-permute-done | bytes 266272 | tf_op jit(solution)/shard_map/ppermute | solution.py:275
  30.3 1.2 %shard_map.44.refs_2_ = f32[2,128,512]{2,1,0:T(8,128)S(1)} custom-call(bf16[4,256,1024]{2,1,0:T(8,128)(2,1)S(1)} %get-tuple-element.24.query_ref, bf16[1040,128]{1,0:T(8,128)(2,1)S(1)} %collective-permute-done.1.refs_0_, f32[4,128,512]{2,1,0:T(8,128)S(1)} %shard_map.41.refs_1_), custom_call_target="tpu_custom_call" | custom-call | flops 25769803776 | bytes 2097152 | tf_op jit(solution)/shard_map/pallas_call | solution.py:259
  31.5 0.1 collective-permute-done.8.refs_1_
  31.5 0.3 collective-permute-done.7.refs_0_
  31.8 3.7 %shard_map.45 = f32[4,512,128]{2,1,0:T(8,128)} custom-call(bf16[4,256,1024]{2,1,0:T(8,128)(2,1)S(1)} %get-tuple-element.24.query_ref, bf16[1040,128]{1,0:T(8,128)(2,1)S(1)} %collective-permute-done.7.refs_0_, bf16[2064,128]{1,0:T(8,128)(2,1)S(1)} %collective-permute-done.8.refs_1_, f32[2,128,512]{2,1,0:T(8,128)S(1)} %shard_map.44.refs_2_, ...), custom_call_target="tpu_custom_call" | custom-call | flops 268435456 | bytes 2097152 | tf_op jit(solution)/shard_map/pallas_call | solution.py:259
  (3 shorter events, 0.0 us)
Async XLA Ops:
  1.3 7.4 %collective-permute-start = (bf16[1040,128]{1,0:T(8,128)(2,1)S(1)}, bf16[1040,128]{1,0:T(8,128)(2,1)S(1)}, u32[]{:S(2)}, u32[]{:S(2)}) collective-permute-start(bf16[1040,128]{1,0:T(8,128)(2,1)S(1)} %get-tuple-element.26), channel_id=1, source_target_pairs={{1,0},{0,1},{3,2},{2,3},{5,4},{4,5},{7,6},{6,7},{9,8},{8,9},{11,10... | collective-permute-start | bytes 798728 | tf_op jit(solution)/shard_map/ppermute | solution.py:275
  2.1 16.3 %collective-permute-start.4 = (bf16[2064,128]{1,0:T(8,128)(2,1)S(1)}, bf16[2064,128]{1,0:T(8,128)(2,1)S(1)}, u32[]{:S(2)}, u32[]{:S(2)}) collective-permute-start(bf16[2064,128]{1,0:T(8,128)(2,1)S(1)} %get-tuple-element.22.own_ref), channel_id=1, source_target_pairs={{2,0},{4,2},{1,3},{6,4},{3,5},{8,6},{5,7},{10,8},{7,9},{12,10},{9,... | collective-permute-start | bytes 1585160 | tf_op jit(solution)/shard_map/ppermute | solution.py:275
  5.2 26.4 %collective-permute-start.8 = (bf16[2064,128]{1,0:T(8,128)(2,1)S(1)}, bf16[2064,128]{1,0:T(8,128)(2,1)S(1)}, u32[]{:S(2)}, u32[]{:S(2)}) collective-permute-start(bf16[2064,128]{1,0:T(8,128)(2,1)S(1)} %get-tuple-element.22.own_ref), channel_id=1, source_target_pairs={{4,1},{6,3},{1,4},{8,5},{3,6},{10,7},{5,8},{12,9},{7,10},{14,11},{... | collective-permute-start | bytes 1585160 | tf_op jit(solution)/shard_map/ppermute | solution.py:275
  7.6 4.2 %collective-permute-start.2 = (bf16[1040,128]{1,0:T(8,128)(2,1)S(1)}, bf16[1040,128]{1,0:T(8,128)(2,1)S(1)}, u32[]{:S(2)}, u32[]{:S(2)}) collective-permute-start(bf16[1040,128]{1,0:T(8,128)(2,1)S(1)} %get-tuple-element.29), channel_id=1, source_target_pairs={{1,0},{0,1},{3,2},{2,3},{5,4},{4,5},{7,6},{6,7},{9,8},{8,9},{11,10... | collective-permute-start | bytes 798728 | tf_op jit(solution)/shard_map/ppermute | solution.py:275
  13.0 12.5 %collective-permute-start.3 = (bf16[1040,128]{1,0:T(8,128)(2,1)S(1)}, bf16[1040,128]{1,0:T(8,128)(2,1)S(1)}, u32[]{:S(2)}, u32[]{:S(2)}) collective-permute-start(bf16[1040,128]{1,0:T(8,128)(2,1)S(1)} %get-tuple-element.29), channel_id=1, source_target_pairs={{3,1},{0,2},{5,3},{2,4},{7,5},{4,6},{9,7},{6,8},{11,9},{8,10},{13,... | collective-permute-start | bytes 798728 | tf_op jit(solution)/shard_map/ppermute | solution.py:275
  15.1 15.2 %collective-permute-start.1 = (bf16[1040,128]{1,0:T(8,128)(2,1)S(1)}, bf16[1040,128]{1,0:T(8,128)(2,1)S(1)}, u32[]{:S(2)}, u32[]{:S(2)}) collective-permute-start(bf16[1040,128]{1,0:T(8,128)(2,1)S(1)} %get-tuple-element.26), channel_id=1, source_target_pairs={{3,1},{0,2},{5,3},{2,4},{7,5},{4,6},{9,7},{6,8},{11,9},{8,10},{13,... | collective-permute-start | bytes 798728 | tf_op jit(solution)/shard_map/ppermute | solution.py:275
  18.4 4.9 %collective-permute-start.5 = (bf16[2064,128]{1,0:T(8,128)(2,1)S(1)}, bf16[2064,128]{1,0:T(8,128)(2,1)S(1)}, u32[]{:S(2)}, u32[]{:S(2)}) collective-permute-start(bf16[2064,128]{1,0:T(8,128)(2,1)S(1)} %collective-permute-done.4.refs_0_), channel_id=1, source_target_pairs={{1,0},{0,1},{3,2},{2,3},{5,4},{4,5},{7,6},{6,7},{9,8},{8,9},{11,10... | collective-permute-start | bytes 1585160 | tf_op jit(solution)/shard_map/ppermute | solution.py:275
  25.4 1.6 %collective-permute-start.6 = (bf16[1040,128]{1,0:T(8,128)(2,1)S(1)}, bf16[1040,128]{1,0:T(8,128)(2,1)S(1)}, u32[]{:S(2)}, u32[]{:S(2)}) collective-permute-start(bf16[1040,128]{1,0:T(8,128)(2,1)S(1)} %collective-permute-done.3.refs_0_), channel_id=1, source_target_pairs={{1,0},{0,1},{3,2},{2,3},{5,4},{4,5},{7,6},{6,7},{9,8},{8,9},{11,10... | collective-permute-start | bytes 798728 | tf_op jit(solution)/shard_map/ppermute | solution.py:275
  30.3 1.5 %collective-permute-start.7 = (bf16[1040,128]{1,0:T(8,128)(2,1)S(1)}, bf16[1040,128]{1,0:T(8,128)(2,1)S(1)}, u32[]{:S(2)}, u32[]{:S(2)}) collective-permute-start(bf16[1040,128]{1,0:T(8,128)(2,1)S(1)} %collective-permute-done.1.refs_0_), channel_id=1, source_target_pairs={{1,0},{0,1},{3,2},{2,3},{5,4},{4,5},{7,6},{6,7},{9,8},{8,9},{11,10... | collective-permute-start | bytes 798728 | tf_op jit(solution)/shard_map/ppermute | solution.py:275

commit v6 on v5

--- a/solution.py
+++ b/solution.py
@@ -14,13 +14,13 @@
 vmem = 24 << 20
 shares = (24, 8, 96, 2, 64, 64, 192, 2)
 
-OWN = (0, 0)
-PAIR = (1, -1)
-NEAR = (2, -2)
-CROSS = (-2, 2)
-FAR = (-3, 3)
-NEAR_OF_PAIR = (-1, 1)
-CROSS_OF_PAIR = (3, -3)
+OWN = (0, 0, 0, 0)
+PAIR = (1, -1, 1, -1)
+NEAR = (2, 2, -2, -2)
+CROSS = (-2, -2, 2, 2)
+FAR = (-3, 3, -3, 3)
+NEAR_OF_PAIR = (3, 1, -1, -3)
+CROSS_OF_PAIR = (-1, -3, 3, 1)
 
 
 def sine(steps):
@@ -84,7 +84,11 @@
 
 def block_of(axis, place):
     me = lax.axis_index(axis)
-    return me + place[0] + lax.rem(me, 2) * (place[1] - place[0])
+    kind = lax.rem(me, len(place))
+    step = place[0]
+    for i in range(1, len(place)):
+        step = jnp.where(kind == i, place[i], step)
+    return me + step
 
 
 def pack_kernel(spectra_ref, off_ref, bins_ref, *refs):
@@ -214,7 +218,7 @@
             if holds(part, f)
         ]
         total = next(ref[f - part[0]] for ref, part in zip(total_refs, held) if holds(part, f))
-        term = total + band_sums(query_ref, f, used) * (2.0 / width)
+        term = total + band_sums(query_ref, f, used) * (2.0 / width) if used else total
         if last:
             out_ref, result_ref, sems = out_refs
             result_ref[f] = term.T
@@ -271,7 +275,7 @@
     shape = spectra.shape
 
     def fetched(value, place):
-        sources = [(i + place[i % 2], i) for i in range(count)]
+        sources = [(i + place[i % len(place)], i) for i in range(count)]
         return lax.ppermute(value, axis, [(i, t) for i, t in sources if 0 <= i < count])
 
     left = shape[0] // 2

time: 35.9 us -> 35 us (0.975)
  the two profiles are of different devices: /device:TPU:19 before, /device:TPU:17 now
where the time goes in v6:
time: 35 us; the launch traced here: 34.8 us
  Pallas kernels  16.9 us (48%)
  starting transfers between devices  16.1 us (46%)
  waiting for transfers between devices  1.43 us (4%)
    ppermute x9, starting transfers between devices, fetched(): lax.ppermute(value, axis, [(i, t) for i, t in sources if 0 <= i < count])  16.1 us
    pallas_call x7, Pallas kernels, band_terms(): pl.pallas_call(functools.partial(band_kernel, axis, places, spans, held,...  12.5 us
    pallas_call x1, Pallas kernels, chip_terms(): pl.pallas_call(functools.partial(chip_kernel, axis, low), out_shape=[jax....  3.11 us
    ppermute x9, waiting for transfers between devices, fetched(): lax.ppermute(value, axis, [(i, t) for i, t in sources if 0 <= i < count])  1.43 us
    pallas_call x1, Pallas kernels, pack(): pl.pallas_call(pack_kernel, out_shape=[jax.ShapeDtypeStruct((part * chann...  1.31 us
  transfers between devices with their start and end apart: 9, of which 2 were waited for; matrix products, arithmetic and copies ran while one was open for 0% of the time, Pallas kernels for 34%

profile of v6, /device:TPU:17, one launch (start us, length us, event | category | flops | bytes accessed | tf_op | source)
XLA Modules:
  0.0 34.8 jit_solution(4466286428215684533)
XLA Ops:
  0.0 1.3 %shard_map.37 = (bf16[2064,128]{1,0:T(8,128)(2,1)S(1)}, bf16[1040,128]{1,0:T(8,128)(2,1)S(1)}, bf16[1040,128]{1,0:T(8,128)(2,1)S(1)}) custom-call(bf16[2048,128]{1,0:T(8,128)(2,1)} %bitcast.2, s32[1,512]{1,0:T(1,128)} %bitcast.3, s32[4]{0:T(128)} %bins_ref.1), custom_call_target="tpu_custom_call" | custom-call | bytes 1048576 | tf_op jit(solution)/shard_map/pallas_call | solution.py:130
  1.3 0.7 %collective-permute-start = (bf16[1040,128]{1,0:T(8,128)(2,1)S(1)}, bf16[1040,128]{1,0:T(8,128)(2,1)S(1)}, u32[]{:S(2)}, u32[]{:S(2)}) collective-permute-start(bf16[1040,128]{1,0:T(8,128)(2,1)S(1)} %get-tuple-element.26), channel_id=1, source_target_pairs={{1,0},{0,1},{3,2},{2,3},{5,4},{4,5},{7,6},{6,7},{9,8},{8,9},{11,10... | collective-permute-start | bytes 798728 | tf_op jit(solution)/shard_map/ppermute | solution.py:279
  2.1 1.2 %collective-permute-start.4 = (bf16[2064,128]{1,0:T(8,128)(2,1)S(1)}, bf16[2064,128]{1,0:T(8,128)(2,1)S(1)}, u32[]{:S(2)}, u32[]{:S(2)}) collective-permute-start(bf16[2064,128]{1,0:T(8,128)(2,1)S(1)} %get-tuple-element.22.own_ref), channel_id=1, source_target_pairs={{2,0},{3,1},{0,2},{1,3},{6,4},{7,5},{4,6},{5,7},{10,8},{11,9},{8,1... | collective-permute-start | bytes 1585160 | tf_op jit(solution)/shard_map/ppermute | solution.py:279
  3.3 3.4 %collective-permute-start.8 = (bf16[2064,128]{1,0:T(8,128)(2,1)S(1)}, bf16[2064,128]{1,0:T(8,128)(2,1)S(1)}, u32[]{:S(2)}, u32[]{:S(2)}) collective-permute-start(bf16[2064,128]{1,0:T(8,128)(2,1)S(1)} %get-tuple-element.22.own_ref), channel_id=1, source_target_pairs={{4,1},{6,3},{1,4},{8,5},{3,6},{10,7},{5,8},{12,9},{7,10},{14,11},{... | collective-permute-start | bytes 1585160 | tf_op jit(solution)/shard_map/ppermute | solution.py:279
  6.7 0.1 collective-permute-start.2
  6.8 0.0 collective-permute-done.pair_ref
  6.8 3.1 %shard_map.38 = (bf16[4,256,1024]{2,1,0:T(8,128)(2,1)S(1)}, f32[4,128,512]{2,1,0:T(8,128)S(1)}) custom-call(bf16[2064,128]{1,0:T(8,128)(2,1)S(1)} %get-tuple-element.22.own_ref, bf16[1040,128]{1,0:T(8,128)(2,1)S(1)} %collective-permute-done.pair_ref), custom_call_target="tpu_custom_call" | custom-call | flops 3221225472 | bytes 2097152 | tf_op jit(solution)/shard_map/pallas_call | solution.py:243
  9.9 0.0 collective-permute-done.2.refs_0_
  9.9 1.2 %shard_map.39.refs_1_ = f32[2,128,512]{2,1,0:T(8,128)S(1)} custom-call(bf16[4,256,1024]{2,1,0:T(8,128)(2,1)S(1)} %get-tuple-element.24.query_ref, bf16[1040,128]{1,0:T(8,128)(2,1)S(1)} %collective-permute-done.2.refs_0_, f32[4,128,512]{2,1,0:T(8,128)S(1)} %get-tuple-element.28.refs_1_.refs_2_), custom_call_target="tpu_custom_call" | custom-call | flops 1073741824 | bytes 2097152 | tf_op jit(solution)/shard_map/pallas_call | solution.py:263
  11.1 3.0 %collective-permute-start.3 = (bf16[1040,128]{1,0:T(8,128)(2,1)S(1)}, bf16[1040,128]{1,0:T(8,128)(2,1)S(1)}, u32[]{:S(2)}, u32[]{:S(2)}) collective-permute-start(bf16[1040,128]{1,0:T(8,128)(2,1)S(1)} %get-tuple-element.29), channel_id=1, source_target_pairs={{4,2},{5,3},{2,4},{3,5},{8,6},{9,7},{6,8},{7,9},{12,10},{13,11},{1... | collective-permute-start | bytes 798728 | tf_op jit(solution)/shard_map/ppermute | solution.py:279
  14.0 4.3 %collective-permute-start.1 = (bf16[1040,128]{1,0:T(8,128)(2,1)S(1)}, bf16[1040,128]{1,0:T(8,128)(2,1)S(1)}, u32[]{:S(2)}, u32[]{:S(2)}) collective-permute-start(bf16[1040,128]{1,0:T(8,128)(2,1)S(1)} %get-tuple-element.26), channel_id=1, source_target_pairs={{4,2},{5,3},{2,4},{3,5},{8,6},{9,7},{6,8},{7,9},{12,10},{13,11},{1... | collective-permute-start | bytes 798728 | tf_op jit(solution)/shard_map/ppermute | solution.py:279
  18.3 0.0 collective-permute-done.4.refs_0_
  18.4 1.1 %collective-permute-start.5 = (bf16[2064,128]{1,0:T(8,128)(2,1)S(1)}, bf16[2064,128]{1,0:T(8,128)(2,1)S(1)}, u32[]{:S(2)}, u32[]{:S(2)}) collective-permute-start(bf16[2064,128]{1,0:T(8,128)(2,1)S(1)} %collective-permute-done.4.refs_0_), channel_id=1, source_target_pairs={{1,0},{0,1},{3,2},{2,3},{5,4},{4,5},{7,6},{6,7},{9,8},{8,9},{11,10... | collective-permute-start | bytes 1585160 | tf_op jit(solution)/shard_map/ppermute | solution.py:279
  19.4 2.1 %shard_map.40.refs_1_ = f32[4,128,512]{2,1,0:T(8,128)S(1)} custom-call(bf16[4,256,1024]{2,1,0:T(8,128)(2,1)S(1)} %get-tuple-element.24.query_ref, bf16[2064,128]{1,0:T(8,128)(2,1)S(1)} %collective-permute-done.4.refs_0_, f32[2,128,512]{2,1,0:T(8,128)S(1)} %shard_map.39.refs_1_, f32[4,128,512]{2,1,0:T(8,128)S(1)} %get-tuple-element.28.refs_1_.refs_2_), custom_call_target="tpu_custom_call" | custom-call | flops 12884901888 | bytes 2097152 | tf_op jit(solution)/shard_map/pallas_call | solution.py:263
  21.5 2.1 %shard_map.41.refs_1_ = f32[4,128,512]{2,1,0:T(8,128)S(1)} custom-call(bf16[4,256,1024]{2,1,0:T(8,128)(2,1)S(1)} %get-tuple-element.24.query_ref, bf16[2064,128]{1,0:T(8,128)(2,1)S(1)} %collective-permute-done.5.refs_0_, f32[4,128,512]{2,1,0:T(8,128)S(1)} %shard_map.40.refs_1_), custom_call_target="tpu_custom_call" | custom-call | flops 268435456 | bytes 2097152 | tf_op jit(solution)/shard_map/pallas_call | solution.py:263
  23.6 0.9 %collective-permute-start.6 = (bf16[1040,128]{1,0:T(8,128)(2,1)S(1)}, bf16[1040,128]{1,0:T(8,128)(2,1)S(1)}, u32[]{:S(2)}, u32[]{:S(2)}) collective-permute-start(bf16[1040,128]{1,0:T(8,128)(2,1)S(1)} %collective-permute-done.3.refs_0_), channel_id=1, source_target_pairs={{1,0},{0,1},{3,2},{2,3},{5,4},{4,5},{7,6},{6,7},{9,8},{8,9},{11,10... | collective-permute-start | bytes 798728 | tf_op jit(solution)/shard_map/ppermute | solution.py:279
  24.6 1.2 %shard_map.42.refs_1_ = f32[2,128,512]{2,1,0:T(8,128)S(1)} custom-call(bf16[4,256,1024]{2,1,0:T(8,128)(2,1)S(1)} %get-tuple-element.24.query_ref, bf16[1040,128]{1,0:T(8,128)(2,1)S(1)} %collective-permute-done.3.refs_0_, f32[4,128,512]{2,1,0:T(8,128)S(1)} %shard_map.41.refs_1_), custom_call_target="tpu_custom_call" | custom-call | flops 8589934592 | bytes 2097152 | tf_op jit(solution)/shard_map/pallas_call | solution.py:263
  25.7 0.0 collective-permute-done.6.refs_0_
  25.7 1.2 %shard_map.43.refs_3_ = f32[2,128,512]{2,1,0:T(8,128)S(1)} custom-call(bf16[4,256,1024]{2,1,0:T(8,128)(2,1)S(1)} %get-tuple-element.24.query_ref, bf16[1040,128]{1,0:T(8,128)(2,1)S(1)} %collective-permute-done.6.refs_0_, f32[2,128,512]{2,1,0:T(8,128)S(1)} %shard_map.42.refs_1_), custom_call_target="tpu_custom_call" | custom-call | flops 8589934592 | bytes 2097152 | tf_op jit(solution)/shard_map/pallas_call | solution.py:263
  26.9 1.1 %collective-permute-done.1.refs_0_ = bf16[1040,128]{1,0:T(8,128)(2,1)S(1)} collective-permute-done((bf16[1040,128]{1,0:T(8,128)(2,1)S(1)}, bf16[1040,128]{1,0:T(8,128)(2,1)S(1)}, u32[]{:S(2)}, u32[]{:S(2)}) %collective-permute-start.1) | collective-permute-done | bytes 266272 | tf_op jit(solution)/shard_map/ppermute | solution.py:279
  28.0 1.4 %collective-permute-start.7 = (bf16[1040,128]{1,0:T(8,128)(2,1)S(1)}, bf16[1040,128]{1,0:T(8,128)(2,1)S(1)}, u32[]{:S(2)}, u32[]{:S(2)}) collective-permute-start(bf16[1040,128]{1,0:T(8,128)(2,1)S(1)} %collective-permute-done.1.refs_0_), channel_id=1, source_target_pairs={{1,0},{0,1},{3,2},{2,3},{5,4},{4,5},{7,6},{6,7},{9,8},{8,9},{11,10... | collective-permute-start | bytes 798728 | tf_op jit(solution)/shard_map/ppermute | solution.py:279
  29.4 1.2 %shard_map.44.refs_2_ = f32[2,128,512]{2,1,0:T(8,128)S(1)} custom-call(bf16[4,256,1024]{2,1,0:T(8,128)(2,1)S(1)} %get-tuple-element.24.query_ref, bf16[1040,128]{1,0:T(8,128)(2,1)S(1)} %collective-permute-done.1.refs_0_, f32[4,128,512]{2,1,0:T(8,128)S(1)} %shard_map.41.refs_1_), custom_call_target="tpu_custom_call" | custom-call | flops 25769803776 | bytes 2097152 | tf_op jit(solution)/shard_map/pallas_call | solution.py:263
  30.6 0.3 collective-permute-done.8.refs_1_
  30.9 3.7 %shard_map.45 = f32[4,512,128]{2,1,0:T(8,128)} custom-call(bf16[4,256,1024]{2,1,0:T(8,128)(2,1)S(1)} %get-tuple-element.24.query_ref, bf16[1040,128]{1,0:T(8,128)(2,1)S(1)} %collective-permute-done.7.refs_0_, bf16[2064,128]{1,0:T(8,128)(2,1)S(1)} %collective-permute-done.8.refs_1_, f32[2,128,512]{2,1,0:T(8,128)S(1)} %shard_map.44.refs_2_, ...), custom_call_target="tpu_custom_call" | custom-call | flops 268435456 | bytes 2097152 | tf_op jit(solution)/shard_map/pallas_call | solution.py:263
  (3 shorter events, 0.0 us)
Async XLA Ops:
  1.3 5.5 %collective-permute-start = (bf16[1040,128]{1,0:T(8,128)(2,1)S(1)}, bf16[1040,128]{1,0:T(8,128)(2,1)S(1)}, u32[]{:S(2)}, u32[]{:S(2)}) collective-permute-start(bf16[1040,128]{1,0:T(8,128)(2,1)S(1)} %get-tuple-element.26), channel_id=1, source_target_pairs={{1,0},{0,1},{3,2},{2,3},{5,4},{4,5},{7,6},{6,7},{9,8},{8,9},{11,10... | collective-permute-start | bytes 798728 | tf_op jit(solution)/shard_map/ppermute | solution.py:279
  2.1 16.3 %collective-permute-start.4 = (bf16[2064,128]{1,0:T(8,128)(2,1)S(1)}, bf16[2064,128]{1,0:T(8,128)(2,1)S(1)}, u32[]{:S(2)}, u32[]{:S(2)}) collective-permute-start(bf16[2064,128]{1,0:T(8,128)(2,1)S(1)} %get-tuple-element.22.own_ref), channel_id=1, source_target_pairs={{2,0},{3,1},{0,2},{1,3},{6,4},{7,5},{4,6},{5,7},{10,8},{11,9},{8,1... | collective-permute-start | bytes 1585160 | tf_op jit(solution)/shard_map/ppermute | solution.py:279
  3.3 27.6 %collective-permute-start.8 = (bf16[2064,128]{1,0:T(8,128)(2,1)S(1)}, bf16[2064,128]{1,0:T(8,128)(2,1)S(1)}, u32[]{:S(2)}, u32[]{:S(2)}) collective-permute-start(bf16[2064,128]{1,0:T(8,128)(2,1)S(1)} %get-tuple-element.22.own_ref), channel_id=1, source_target_pairs={{4,1},{6,3},{1,4},{8,5},{3,6},{10,7},{5,8},{12,9},{7,10},{14,11},{... | collective-permute-start | bytes 1585160 | tf_op jit(solution)/shard_map/ppermute | solution.py:279
  6.7 3.2 %collective-permute-start.2 = (bf16[1040,128]{1,0:T(8,128)(2,1)S(1)}, bf16[1040,128]{1,0:T(8,128)(2,1)S(1)}, u32[]{:S(2)}, u32[]{:S(2)}) collective-permute-start(bf16[1040,128]{1,0:T(8,128)(2,1)S(1)} %get-tuple-element.29), channel_id=1, source_target_pairs={{1,0},{0,1},{3,2},{2,3},{5,4},{4,5},{7,6},{6,7},{9,8},{8,9},{11,10... | collective-permute-start | bytes 798728 | tf_op jit(solution)/shard_map/ppermute | solution.py:279
  11.1 12.6 %collective-permute-start.3 = (bf16[1040,128]{1,0:T(8,128)(2,1)S(1)}, bf16[1040,128]{1,0:T(8,128)(2,1)S(1)}, u32[]{:S(2)}, u32[]{:S(2)}) collective-permute-start(bf16[1040,128]{1,0:T(8,128)(2,1)S(1)} %get-tuple-element.29), channel_id=1, source_target_pairs={{4,2},{5,3},{2,4},{3,5},{8,6},{9,7},{6,8},{7,9},{12,10},{13,11},{1... | collective-permute-start | bytes 798728 | tf_op jit(solution)/shard_map/ppermute | solution.py:279
  14.0 13.9 %collective-permute-start.1 = (bf16[1040,128]{1,0:T(8,128)(2,1)S(1)}, bf16[1040,128]{1,0:T(8,128)(2,1)S(1)}, u32[]{:S(2)}, u32[]{:S(2)}) collective-permute-start(bf16[1040,128]{1,0:T(8,128)(2,1)S(1)} %get-tuple-element.26), channel_id=1, source_target_pairs={{4,2},{5,3},{2,4},{3,5},{8,6},{9,7},{6,8},{7,9},{12,10},{13,11},{1... | collective-permute-start | bytes 798728 | tf_op jit(solution)/shard_map/ppermute | solution.py:279
  18.4 3.2 %collective-permute-start.5 = (bf16[2064,128]{1,0:T(8,128)(2,1)S(1)}, bf16[2064,128]{1,0:T(8,128)(2,1)S(1)}, u32[]{:S(2)}, u32[]{:S(2)}) collective-permute-start(bf16[2064,128]{1,0:T(8,128)(2,1)S(1)} %collective-permute-done.4.refs_0_), channel_id=1, source_target_pairs={{1,0},{0,1},{3,2},{2,3},{5,4},{4,5},{7,6},{6,7},{9,8},{8,9},{11,10... | collective-permute-start | bytes 1585160 | tf_op jit(solution)/shard_map/ppermute | solution.py:279
  23.6 2.1 %collective-permute-start.6 = (bf16[1040,128]{1,0:T(8,128)(2,1)S(1)}, bf16[1040,128]{1,0:T(8,128)(2,1)S(1)}, u32[]{:S(2)}, u32[]{:S(2)}) collective-permute-start(bf16[1040,128]{1,0:T(8,128)(2,1)S(1)} %collective-permute-done.3.refs_0_), channel_id=1, source_target_pairs={{1,0},{0,1},{3,2},{2,3},{5,4},{4,5},{7,6},{6,7},{9,8},{8,9},{11,10... | collective-permute-start | bytes 798728 | tf_op jit(solution)/shard_map/ppermute | solution.py:279
  28.0 2.9 %collective-permute-start.7 = (bf16[1040,128]{1,0:T(8,128)(2,1)S(1)}, bf16[1040,128]{1,0:T(8,128)(2,1)S(1)}, u32[]{:S(2)}, u32[]{:S(2)}) collective-permute-start(bf16[1040,128]{1,0:T(8,128)(2,1)S(1)} %collective-permute-done.1.refs_0_), channel_id=1, source_target_pairs={{1,0},{0,1},{3,2},{2,3},{5,4},{4,5},{7,6},{6,7},{9,8},{8,9},{11,10... | collective-permute-start | bytes 798728 | tf_op jit(solution)/shard_map/ppermute | solution.py:279

commit v7 on v6

--- a/solution.py
+++ b/solution.py
@@ -12,7 +12,7 @@
 period_metres = 4096
 model_amp = 0.5
 vmem = 24 << 20
-shares = (24, 8, 96, 2, 64, 64, 192, 2)
+shares = (64, 64, 64, 64, 64, 64, 64, 64, 64)
 
 OWN = (0, 0, 0, 0)
 PAIR = (1, -1, 1, -1)
@@ -164,18 +164,31 @@
         query_ref[f, width:, channels:] = jnp.where(mine, imag, 0.0).astype(jnp.bfloat16)
 
 
-def band_sums(query_ref, f, keys):
-    channels = query_ref.shape[2] // 2
-    spectra = [ref[pl.ds((f - first) * channels, channels), :] for ref, first, _ in keys]
-    spectra = spectra[0] if len(keys) == 1 else jnp.concatenate(spectra, axis=0)
+def spectra_of(f, keys):
+    parts = []
+    for ref, first, _ in keys:
+        channels = keys[0][2].shape[0]
+        parts.append(ref[pl.ds((f - first) * channels, channels), :])
+    return parts[0] if len(parts) == 1 else jnp.concatenate(parts, axis=0)
+
+
+def misfit_of(query_ref, f, keys):
     extra = [columns for _, _, columns in keys]
     extra = extra[0] if len(keys) == 1 else jnp.concatenate(extra, axis=0)
-    misfit = jnp.dot(
-        jnp.concatenate([spectra, extra], axis=1), query_ref[f], preferred_element_type=jnp.float32
-    )
-    grad = jnp.tanh(misfit).astype(jnp.bfloat16)
-    sums = jnp.dot(spectra.T, grad, preferred_element_type=jnp.float32)
-    return sums[:, :channels] + turned(sums[:, channels:])
+    key = jnp.concatenate([spectra_of(f, keys), extra], axis=1)
+    return jnp.dot(key, query_ref[f], preferred_element_type=jnp.float32)
+
+
+def band_sums(query_ref, steps, emit):
+    channels = query_ref.shape[2] // 2
+    ahead = misfit_of(query_ref, *steps[0])
+    for i, (f, keys) in enumerate(steps):
+        misfit = ahead
+        if i + 1 < len(steps):
+            ahead = misfit_of(query_ref, *steps[i + 1])
+        grad = jnp.tanh(misfit).astype(jnp.bfloat16)
+        sums = jnp.dot(spectra_of(f, keys).T, grad, preferred_element_type=jnp.float32)
+        emit(i, f, sums[:, :channels] + turned(sums[:, channels:]))
 
 
 def columns_of(key_ref, block, freqs, channels, width):
@@ -190,11 +203,19 @@
     fill_queries(own_ref, query_ref, own)
     own_columns = columns_of(own_ref, own, freqs, channels, width)
     pair_columns = columns_of(pair_ref, pair, freqs, channels, width)
+    steps = []
     for f in range(freqs):
-        term = 2.0 * band_sums(query_ref, f, [(own_ref, 0, own_columns)])
+        steps.append((f, [(own_ref, 0, own_columns)]))
         if f < low:
-            term = term + band_sums(query_ref, f, [(pair_ref, 0, pair_columns)])
-        total_ref[f] = term * (2.0 / width)
+            steps.append((f, [(pair_ref, 0, pair_columns)]))
+
+    def emit(i, f, sums):
+        if steps[i][1][0][0] is own_ref:
+            total_ref[f] = sums * (4.0 / width)
+        else:
+            total_ref[f] += sums * (2.0 / width)
+
+    band_sums(query_ref, steps, emit)
 
 
 def holds(span, f):
@@ -210,15 +231,18 @@
         columns_of(key_ref, block_of(axis, place), freqs, channels, width)
         for key_ref, place in zip(keys, places)
     ]
-    copies = []
+    copies, steps = [], []
     for f in range(span[0], span[0] + span[1]):
         used = [
             (key_ref, part[0], columns)
             for key_ref, part, columns in zip(keys, spans, extra)
             if holds(part, f)
         ]
+        steps.append((f, used))
+
+    def emit(i, f, sums):
         total = next(ref[f - part[0]] for ref, part in zip(total_refs, held) if holds(part, f))
-        term = total + band_sums(query_ref, f, used) * (2.0 / width) if used else total
+        term = total + sums * (2.0 / width)
         if last:
             out_ref, result_ref, sems = out_refs
             result_ref[f] = term.T
@@ -226,6 +250,8 @@
             copies[-1].start()
         else:
             out_refs[0][f - span[0]] = term
+
+    band_sums(query_ref, steps, emit)
     for copy in copies:
         copy.wait()
 
@@ -304,9 +330,9 @@
     cross_low, rest = lax.optimization_barrier((cross_low, rest))
     low_pair = fetched(cross_low, PAIR)
     first = terms([(total, every)], [(cross_low, CROSS, low)], low, shares[6])
+    first = terms([(first, low)], [(low_pair, CROSS_OF_PAIR, low)], low, shares[7])
     far, first = lax.optimization_barrier((far, first))
-    closing = [(low_pair, CROSS_OF_PAIR, low), (far, FAR, every)]
-    return terms([(first, low), (rest, high)], closing, every, shares[7], last=True)
+    return terms([(first, low), (rest, high)], [(far, FAR, every)], every, shares[8], last=True)
 
 
 def solution(mesh):

time: 35 us -> 34.6 us (0.989)
  the two profiles are of different devices: /device:TPU:17 before, /device:TPU:19 now
where the time goes in v7:
time: 34.6 us; the launch traced here: 34.2 us
  Pallas kernels  16.4 us (47%)
  starting transfers between devices  14.2 us (41%)
  waiting for transfers between devices  3.3 us (10%)
    ppermute x9, starting transfers between devices, fetched(): lax.ppermute(value, axis, [(i, t) for i, t in sources if 0 <= i < count])  14.2 us
    pallas_call x8, Pallas kernels, band_terms(): pl.pallas_call(functools.partial(band_kernel, axis, places, spans, held,...  12.2 us
    ppermute x9, waiting for transfers between devices, fetched(): lax.ppermute(value, axis, [(i, t) for i, t in sources if 0 <= i < count])  3.3 us
    pallas_call x1, Pallas kernels, chip_terms(): pl.pallas_call(functools.partial(chip_kernel, axis, low), out_shape=[jax....  2.95 us
    pallas_call x1, Pallas kernels, pack(): pl.pallas_call(pack_kernel, out_shape=[jax.ShapeDtypeStruct((part * chann...  1.31 us
  transfers between devices with their start and end apart: 9, of which 4 were waited for; matrix products, arithmetic and copies ran while one was open for 0% of the time, Pallas kernels for 36%

profile of v7, /device:TPU:19, one launch (start us, length us, event | category | flops | bytes accessed | tf_op | source)
XLA Modules:
  0.0 34.2 jit_solution(7166174897016827253)
XLA Ops:
  0.0 1.3 %shard_map.37 = (bf16[2064,128]{1,0:T(8,128)(2,1)S(1)}, bf16[1040,128]{1,0:T(8,128)(2,1)S(1)}, bf16[1040,128]{1,0:T(8,128)(2,1)S(1)}) custom-call(bf16[2048,128]{1,0:T(8,128)(2,1)} %bitcast.2, s32[1,512]{1,0:T(1,128)} %bitcast.3, s32[4]{0:T(128)} %bins_ref.1), custom_call_target="tpu_custom_call" | custom-call | bytes 1048576 | tf_op jit(solution)/shard_map/pallas_call | solution.py:130
  1.3 0.7 %collective-permute-start = (bf16[1040,128]{1,0:T(8,128)(2,1)S(1)}, bf16[1040,128]{1,0:T(8,128)(2,1)S(1)}, u32[]{:S(2)}, u32[]{:S(2)}) collective-permute-start(bf16[1040,128]{1,0:T(8,128)(2,1)S(1)} %get-tuple-element.26), channel_id=1, source_target_pairs={{1,0},{0,1},{3,2},{2,3},{5,4},{4,5},{7,6},{6,7},{9,8},{8,9},{11,10... | collective-permute-start | bytes 798728 | tf_op jit(solution)/shard_map/ppermute | solution.py:305
  2.1 0.3 collective-permute-start.5
  2.3 3.4 %collective-permute-start.1 = (bf16[2064,128]{1,0:T(8,128)(2,1)S(1)}, bf16[2064,128]{1,0:T(8,128)(2,1)S(1)}, u32[]{:S(2)}, u32[]{:S(2)}) collective-permute-start(bf16[2064,128]{1,0:T(8,128)(2,1)S(1)} %get-tuple-element.22.own_ref), channel_id=1, source_target_pairs={{4,1},{6,3},{1,4},{8,5},{3,6},{10,7},{5,8},{12,9},{7,10},{14,11},{... | collective-permute-start | bytes 1585160 | tf_op jit(solution)/shard_map/ppermute | solution.py:305
  5.7 0.1 collective-permute-start.3
  5.8 0.0 collective-permute-done.pair_ref
  5.8 2.9 %shard_map.38 = (bf16[4,256,1024]{2,1,0:T(8,128)(2,1)S(1)}, f32[4,128,512]{2,1,0:T(8,128)S(1)}) custom-call(bf16[2064,128]{1,0:T(8,128)(2,1)S(1)} %get-tuple-element.22.own_ref, bf16[1040,128]{1,0:T(8,128)(2,1)S(1)} %collective-permute-done.pair_ref), custom_call_target="tpu_custom_call" | custom-call | flops 8589934592 | bytes 2097152 | tf_op jit(solution)/shard_map/pallas_call | solution.py:269
  8.8 1.1 %shard_map.39.refs_1_ = f32[2,128,512]{2,1,0:T(8,128)S(1)} custom-call(bf16[4,256,1024]{2,1,0:T(8,128)(2,1)S(1)} %get-tuple-element.24.query_ref, bf16[1040,128]{1,0:T(8,128)(2,1)S(1)} %collective-permute-done.3.refs_0_, f32[4,128,512]{2,1,0:T(8,128)S(1)} %get-tuple-element.28.refs_1_.refs_2_), custom_call_target="tpu_custom_call" | custom-call | flops 8589934592 | bytes 2097152 | tf_op jit(solution)/shard_map/pallas_call | solution.py:289
  9.9 4.0 %collective-permute-start.4 = (bf16[1040,128]{1,0:T(8,128)(2,1)S(1)}, bf16[1040,128]{1,0:T(8,128)(2,1)S(1)}, u32[]{:S(2)}, u32[]{:S(2)}) collective-permute-start(bf16[1040,128]{1,0:T(8,128)(2,1)S(1)} %get-tuple-element.29), channel_id=1, source_target_pairs={{4,2},{5,3},{2,4},{3,5},{8,6},{9,7},{6,8},{7,9},{12,10},{13,11},{1... | collective-permute-start | bytes 798728 | tf_op jit(solution)/shard_map/ppermute | solution.py:305
  13.9 2.3 %collective-permute-start.2 = (bf16[1040,128]{1,0:T(8,128)(2,1)S(1)}, bf16[1040,128]{1,0:T(8,128)(2,1)S(1)}, u32[]{:S(2)}, u32[]{:S(2)}) collective-permute-start(bf16[1040,128]{1,0:T(8,128)(2,1)S(1)} %get-tuple-element.26), channel_id=1, source_target_pairs={{4,2},{5,3},{2,4},{3,5},{8,6},{9,7},{6,8},{7,9},{12,10},{13,11},{1... | collective-permute-start | bytes 798728 | tf_op jit(solution)/shard_map/ppermute | solution.py:305
  16.3 1.1 %collective-permute-start.6 = (bf16[2064,128]{1,0:T(8,128)(2,1)S(1)}, bf16[2064,128]{1,0:T(8,128)(2,1)S(1)}, u32[]{:S(2)}, u32[]{:S(2)}) collective-permute-start(bf16[2064,128]{1,0:T(8,128)(2,1)S(1)} %collective-permute-done.5.refs_0_), channel_id=1, source_target_pairs={{1,0},{0,1},{3,2},{2,3},{5,4},{4,5},{7,6},{6,7},{9,8},{8,9},{11,10... | collective-permute-start | bytes 1585160 | tf_op jit(solution)/shard_map/ppermute | solution.py:305
  17.4 2.0 %shard_map.40.refs_1_ = f32[4,128,512]{2,1,0:T(8,128)S(1)} custom-call(bf16[4,256,1024]{2,1,0:T(8,128)(2,1)S(1)} %get-tuple-element.24.query_ref, bf16[2064,128]{1,0:T(8,128)(2,1)S(1)} %collective-permute-done.5.refs_0_, f32[2,128,512]{2,1,0:T(8,128)S(1)} %shard_map.39.refs_1_, f32[4,128,512]{2,1,0:T(8,128)S(1)} %get-tuple-element.28.refs_1_.refs_2_), custom_call_target="tpu_custom_call" | custom-call | flops 8589934592 | bytes 2097152 | tf_op jit(solution)/shard_map/pallas_call | solution.py:289
  19.3 1.9 %shard_map.41.refs_1_ = f32[4,128,512]{2,1,0:T(8,128)S(1)} custom-call(bf16[4,256,1024]{2,1,0:T(8,128)(2,1)S(1)} %get-tuple-element.24.query_ref, bf16[2064,128]{1,0:T(8,128)(2,1)S(1)} %collective-permute-done.6.refs_0_, f32[4,128,512]{2,1,0:T(8,128)S(1)} %shard_map.40.refs_1_), custom_call_target="tpu_custom_call" | custom-call | flops 8589934592 | bytes 2097152 | tf_op jit(solution)/shard_map/pallas_call | solution.py:289
  21.3 1.1 %collective-permute-done.4.refs_0_ = bf16[1040,128]{1,0:T(8,128)(2,1)S(1)} collective-permute-done((bf16[1040,128]{1,0:T(8,128)(2,1)S(1)}, bf16[1040,128]{1,0:T(8,128)(2,1)S(1)}, u32[]{:S(2)}, u32[]{:S(2)}) %collective-permute-start.4) | collective-permute-done | bytes 266272 | tf_op jit(solution)/shard_map/ppermute | solution.py:305
  22.4 1.4 %collective-permute-start.7 = (bf16[1040,128]{1,0:T(8,128)(2,1)S(1)}, bf16[1040,128]{1,0:T(8,128)(2,1)S(1)}, u32[]{:S(2)}, u32[]{:S(2)}) collective-permute-start(bf16[1040,128]{1,0:T(8,128)(2,1)S(1)} %collective-permute-done.4.refs_0_), channel_id=1, source_target_pairs={{1,0},{0,1},{3,2},{2,3},{5,4},{4,5},{7,6},{6,7},{9,8},{8,9},{11,10... | collective-permute-start | bytes 798728 | tf_op jit(solution)/shard_map/ppermute | solution.py:305
  23.7 1.1 %shard_map.42.refs_1_ = f32[2,128,512]{2,1,0:T(8,128)S(1)} custom-call(bf16[4,256,1024]{2,1,0:T(8,128)(2,1)S(1)} %get-tuple-element.24.query_ref, bf16[1040,128]{1,0:T(8,128)(2,1)S(1)} %collective-permute-done.4.refs_0_, f32[4,128,512]{2,1,0:T(8,128)S(1)} %shard_map.41.refs_1_), custom_call_target="tpu_custom_call" | custom-call | flops 8589934592 | bytes 2097152 | tf_op jit(solution)/shard_map/pallas_call | solution.py:289
  24.8 0.1 collective-permute-done.7.refs_0_
  24.9 1.1 %shard_map.43.refs_2_ = f32[2,128,512]{2,1,0:T(8,128)S(1)} custom-call(bf16[4,256,1024]{2,1,0:T(8,128)(2,1)S(1)} %get-tuple-element.24.query_ref, bf16[1040,128]{1,0:T(8,128)(2,1)S(1)} %collective-permute-done.7.refs_0_, f32[2,128,512]{2,1,0:T(8,128)S(1)} %shard_map.42.refs_1_), custom_call_target="tpu_custom_call" | custom-call | flops 8589934592 | bytes 2097152 | tf_op jit(solution)/shard_map/pallas_call | solution.py:289
  26.0 2.1 %collective-permute-done.2.refs_0_ = bf16[1040,128]{1,0:T(8,128)(2,1)S(1)} collective-permute-done((bf16[1040,128]{1,0:T(8,128)(2,1)S(1)}, bf16[1040,128]{1,0:T(8,128)(2,1)S(1)}, u32[]{:S(2)}, u32[]{:S(2)}) %collective-permute-start.2) | collective-permute-done | bytes 266272 | tf_op jit(solution)/shard_map/ppermute | solution.py:305
  28.1 0.9 %collective-permute-start.8 = (bf16[1040,128]{1,0:T(8,128)(2,1)S(1)}, bf16[1040,128]{1,0:T(8,128)(2,1)S(1)}, u32[]{:S(2)}, u32[]{:S(2)}) collective-permute-start(bf16[1040,128]{1,0:T(8,128)(2,1)S(1)} %collective-permute-done.2.refs_0_), channel_id=1, source_target_pairs={{1,0},{0,1},{3,2},{2,3},{5,4},{4,5},{7,6},{6,7},{9,8},{8,9},{11,10... | collective-permute-start | bytes 798728 | tf_op jit(solution)/shard_map/ppermute | solution.py:305
  29.0 1.1 %shard_map.44.refs_1_ = f32[2,128,512]{2,1,0:T(8,128)S(1)} custom-call(bf16[4,256,1024]{2,1,0:T(8,128)(2,1)S(1)} %get-tuple-element.24.query_ref, bf16[1040,128]{1,0:T(8,128)(2,1)S(1)} %collective-permute-done.2.refs_0_, f32[4,128,512]{2,1,0:T(8,128)S(1)} %shard_map.41.refs_1_), custom_call_target="tpu_custom_call" | custom-call | flops 8589934592 | bytes 2097152 | tf_op jit(solution)/shard_map/pallas_call | solution.py:289
  30.1 0.1 collective-permute-done.8.refs_0_
  30.1 1.1 %shard_map.45.refs_1_ = f32[2,128,512]{2,1,0:T(8,128)S(1)} custom-call(bf16[4,256,1024]{2,1,0:T(8,128)(2,1)S(1)} %get-tuple-element.24.query_ref, bf16[1040,128]{1,0:T(8,128)(2,1)S(1)} %collective-permute-done.8.refs_0_, f32[2,128,512]{2,1,0:T(8,128)S(1)} %shard_map.44.refs_1_), custom_call_target="tpu_custom_call" | custom-call | flops 8589934592 | bytes 2097152 | tf_op jit(solution)/shard_map/pallas_call | solution.py:289
  31.3 2.8 %shard_map.46 = f32[4,512,128]{2,1,0:T(8,128)} custom-call(bf16[4,256,1024]{2,1,0:T(8,128)(2,1)S(1)} %get-tuple-element.24.query_ref, bf16[2064,128]{1,0:T(8,128)(2,1)S(1)} %collective-permute-done.1.refs_0_, f32[2,128,512]{2,1,0:T(8,128)S(1)} %shard_map.45.refs_1_, f32[2,128,512]{2,1,0:T(8,128)S(1)} %shard_map.43.refs_2_), custom_call_target="tpu_custom_call" | custom-call | flops 8589934592 | bytes 2097152 | tf_op jit(solution)/shard_map/pallas_call | solution.py:289
  (4 shorter events, 0.0 us)
Async XLA Ops:
  1.3 4.5 %collective-permute-start = (bf16[1040,128]{1,0:T(8,128)(2,1)S(1)}, bf16[1040,128]{1,0:T(8,128)(2,1)S(1)}, u32[]{:S(2)}, u32[]{:S(2)}) collective-permute-start(bf16[1040,128]{1,0:T(8,128)(2,1)S(1)} %get-tuple-element.26), channel_id=1, source_target_pairs={{1,0},{0,1},{3,2},{2,3},{5,4},{4,5},{7,6},{6,7},{9,8},{8,9},{11,10... | collective-permute-start | bytes 798728 | tf_op jit(solution)/shard_map/ppermute | solution.py:305
  2.1 14.2 %collective-permute-start.5 = (bf16[2064,128]{1,0:T(8,128)(2,1)S(1)}, bf16[2064,128]{1,0:T(8,128)(2,1)S(1)}, u32[]{:S(2)}, u32[]{:S(2)}) collective-permute-start(bf16[2064,128]{1,0:T(8,128)(2,1)S(1)} %get-tuple-element.22.own_ref), channel_id=1, source_target_pairs={{2,0},{3,1},{0,2},{1,3},{6,4},{7,5},{4,6},{5,7},{10,8},{11,9},{8,1... | collective-permute-start | bytes 1585160 | tf_op jit(solution)/shard_map/ppermute | solution.py:305
  2.3 28.9 %collective-permute-start.1 = (bf16[2064,128]{1,0:T(8,128)(2,1)S(1)}, bf16[2064,128]{1,0:T(8,128)(2,1)S(1)}, u32[]{:S(2)}, u32[]{:S(2)}) collective-permute-start(bf16[2064,128]{1,0:T(8,128)(2,1)S(1)} %get-tuple-element.22.own_ref), channel_id=1, source_target_pairs={{4,1},{6,3},{1,4},{8,5},{3,6},{10,7},{5,8},{12,9},{7,10},{14,11},{... | collective-permute-start | bytes 1585160 | tf_op jit(solution)/shard_map/ppermute | solution.py:305
  5.7 3.1 %collective-permute-start.3 = (bf16[1040,128]{1,0:T(8,128)(2,1)S(1)}, bf16[1040,128]{1,0:T(8,128)(2,1)S(1)}, u32[]{:S(2)}, u32[]{:S(2)}) collective-permute-start(bf16[1040,128]{1,0:T(8,128)(2,1)S(1)} %get-tuple-element.29), channel_id=1, source_target_pairs={{1,0},{0,1},{3,2},{2,3},{5,4},{4,5},{7,6},{6,7},{9,8},{8,9},{11,10... | collective-permute-start | bytes 798728 | tf_op jit(solution)/shard_map/ppermute | solution.py:305
  9.9 12.5 %collective-permute-start.4 = (bf16[1040,128]{1,0:T(8,128)(2,1)S(1)}, bf16[1040,128]{1,0:T(8,128)(2,1)S(1)}, u32[]{:S(2)}, u32[]{:S(2)}) collective-permute-start(bf16[1040,128]{1,0:T(8,128)(2,1)S(1)} %get-tuple-element.29), channel_id=1, source_target_pairs={{4,2},{5,3},{2,4},{3,5},{8,6},{9,7},{6,8},{7,9},{12,10},{13,11},{1... | collective-permute-start | bytes 798728 | tf_op jit(solution)/shard_map/ppermute | solution.py:305
  13.9 14.1 %collective-permute-start.2 = (bf16[1040,128]{1,0:T(8,128)(2,1)S(1)}, bf16[1040,128]{1,0:T(8,128)(2,1)S(1)}, u32[]{:S(2)}, u32[]{:S(2)}) collective-permute-start(bf16[1040,128]{1,0:T(8,128)(2,1)S(1)} %get-tuple-element.26), channel_id=1, source_target_pairs={{4,2},{5,3},{2,4},{3,5},{8,6},{9,7},{6,8},{7,9},{12,10},{13,11},{1... | collective-permute-start | bytes 798728 | tf_op jit(solution)/shard_map/ppermute | solution.py:305
  16.3 3.0 %collective-permute-start.6 = (bf16[2064,128]{1,0:T(8,128)(2,1)S(1)}, bf16[2064,128]{1,0:T(8,128)(2,1)S(1)}, u32[]{:S(2)}, u32[]{:S(2)}) collective-permute-start(bf16[2064,128]{1,0:T(8,128)(2,1)S(1)} %collective-permute-done.5.refs_0_), channel_id=1, source_target_pairs={{1,0},{0,1},{3,2},{2,3},{5,4},{4,5},{7,6},{6,7},{9,8},{8,9},{11,10... | collective-permute-start | bytes 1585160 | tf_op jit(solution)/shard_map/ppermute | solution.py:305
  22.4 2.5 %collective-permute-start.7 = (bf16[1040,128]{1,0:T(8,128)(2,1)S(1)}, bf16[1040,128]{1,0:T(8,128)(2,1)S(1)}, u32[]{:S(2)}, u32[]{:S(2)}) collective-permute-start(bf16[1040,128]{1,0:T(8,128)(2,1)S(1)} %collective-permute-done.4.refs_0_), channel_id=1, source_target_pairs={{1,0},{0,1},{3,2},{2,3},{5,4},{4,5},{7,6},{6,7},{9,8},{8,9},{11,10... | collective-permute-start | bytes 798728 | tf_op jit(solution)/shard_map/ppermute | solution.py:305
  28.1 2.1 %collective-permute-start.8 = (bf16[1040,128]{1,0:T(8,128)(2,1)S(1)}, bf16[1040,128]{1,0:T(8,128)(2,1)S(1)}, u32[]{:S(2)}, u32[]{:S(2)}) collective-permute-start(bf16[1040,128]{1,0:T(8,128)(2,1)S(1)} %collective-permute-done.2.refs_0_), channel_id=1, source_target_pairs={{1,0},{0,1},{3,2},{2,3},{5,4},{4,5},{7,6},{6,7},{9,8},{8,9},{11,10... | collective-permute-start | bytes 798728 | tf_op jit(solution)/shard_map/ppermute | solution.py:305

commit v8 on v7

--- a/solution.py
+++ b/solution.py
@@ -92,16 +92,14 @@
 
 
 def pack_kernel(spectra_ref, off_ref, bins_ref, *refs):
-    out_refs, (off, bins, sems) = refs[:-3], refs[-3:]
-    width = spectra_ref.shape[1]
-    freqs, lines = bins_ref.shape[0], off.shape[1] // width
-    tail = (-(-(lines + rows_of(freqs)) // 16) * 16, width)
-    sources, targets, start = [off_ref, bins_ref], [off, bins], 0
-    for out_ref in out_refs:
-        rows = out_ref.shape[0] - tail[0]
-        sources.append(spectra_ref.at[pl.ds(start, rows)])
-        targets.append(out_ref.at[pl.ds(0, rows)])
-        start = (start + rows) % spectra_ref.shape[0]
+    (own_ref, *part_refs), (off, bins, sems) = refs[:-3], refs[-3:]
+    rows, width = spectra_ref.shape
+    freqs, channels = bins_ref.shape[0], off.shape[1]
+    lines, tail = channels // width, (own_ref.shape[0] - rows, width)
+    sources, targets = [off_ref, bins_ref], [off, bins]
+    for f in range(freqs):
+        sources.append(spectra_ref.at[pl.ds(f * channels, channels)])
+        targets.append(own_ref.at[pl.ds(f * channels, channels)])
     copies = [
         pltpu.make_async_copy(source, target, sems.at[i])
         for i, (source, target) in enumerate(zip(sources, targets))
@@ -117,10 +115,17 @@
     first = tail[0] - rows_of(freqs)
     for f in range(freqs):
         value = jnp.where((row == first + f) | (row == first + freqs + f), bins[f], value)
-    for out_ref in out_refs:
-        out_ref[out_ref.shape[0] - tail[0] :, :] = value.astype(jnp.float32).astype(jnp.bfloat16)
-    for copy in copies[2:]:
-        copy.wait()
+    value = value.astype(jnp.float32).astype(jnp.bfloat16)
+    for out_ref in (own_ref, *part_refs):
+        out_ref[out_ref.shape[0] - tail[0] :, :] = value
+    f = 0
+    for part_ref in part_refs:
+        for place in range((part_ref.shape[0] - tail[0]) // channels):
+            copies[2 + f].wait()
+            part_ref[place * channels : (place + 1) * channels, :] = own_ref[
+                f * channels : (f + 1) * channels, :
+            ]
+            f += 1
 
 
 def pack(spectra, offsets, bins, parts):
@@ -138,7 +143,7 @@
         scratch_shapes=[
             pltpu.VMEM((1, channels), jnp.int32),
             pltpu.SMEM((freqs,), jnp.int32),
-            pltpu.SemaphoreType.DMA((3 + len(parts),)),
+            pltpu.SemaphoreType.DMA((2 + freqs,)),
         ],
         compiler_params=pltpu.CompilerParams(vmem_limit_bytes=vmem),
         cost_estimate=pl.CostEstimate(flops=0, bytes_accessed=1 << 20, transcendentals=0),

time: 34.6 us -> 34.5 us (level)
  no operation moved by 1% of the time
where the time goes in v8:
time: 34.5 us; the launch traced here: 34.1 us
  Pallas kernels  16.3 us (47%)
  starting transfers between devices  14.2 us (41%)
  waiting for transfers between devices  3.33 us (10%)
    ppermute x9, starting transfers between devices, fetched(): lax.ppermute(value, axis, [(i, t) for i, t in sources if 0 <= i < count])  14.2 us
    pallas_call x8, Pallas kernels, band_terms(): pl.pallas_call(functools.partial(band_kernel, axis, places, spans, held,...  12.2 us
    ppermute x9, waiting for transfers between devices, fetched(): lax.ppermute(value, axis, [(i, t) for i, t in sources if 0 <= i < count])  3.33 us
    pallas_call x1, Pallas kernels, chip_terms(): pl.pallas_call(functools.partial(chip_kernel, axis, low), out_shape=[jax....  2.96 us
    pallas_call x1, Pallas kernels, pack(): pl.pallas_call(pack_kernel, out_shape=[jax.ShapeDtypeStruct((part * chann...  1.17 us
  transfers between devices with their start and end apart: 9, of which 4 were waited for; matrix products, arithmetic and copies ran while one was open for 0% of the time, Pallas kernels for 36%

profile of v8, /device:TPU:19, one launch (start us, length us, event | category | flops | bytes accessed | tf_op | source)
XLA Modules:
  0.0 34.1 jit_solution(13281768527825004070)
XLA Ops:
  0.0 1.2 %shard_map.37 = (bf16[2064,128]{1,0:T(8,128)(2,1)S(1)}, bf16[1040,128]{1,0:T(8,128)(2,1)S(1)}, bf16[1040,128]{1,0:T(8,128)(2,1)S(1)}) custom-call(bf16[2048,128]{1,0:T(8,128)(2,1)} %bitcast.2, s32[1,512]{1,0:T(1,128)} %bitcast.3, s32[4]{0:T(128)} %bins_ref.1), custom_call_target="tpu_custom_call" | custom-call | bytes 1048576 | tf_op jit(solution)/shard_map/pallas_call | solution.py:135
  1.2 0.7 %collective-permute-start = (bf16[1040,128]{1,0:T(8,128)(2,1)S(1)}, bf16[1040,128]{1,0:T(8,128)(2,1)S(1)}, u32[]{:S(2)}, u32[]{:S(2)}) collective-permute-start(bf16[1040,128]{1,0:T(8,128)(2,1)S(1)} %get-tuple-element.26), channel_id=1, source_target_pairs={{1,0},{0,1},{3,2},{2,3},{5,4},{4,5},{7,6},{6,7},{9,8},{8,9},{11,10... | collective-permute-start | bytes 798728 | tf_op jit(solution)/shard_map/ppermute | solution.py:310
  1.9 0.3 collective-permute-start.5
  2.2 3.4 %collective-permute-start.1 = (bf16[2064,128]{1,0:T(8,128)(2,1)S(1)}, bf16[2064,128]{1,0:T(8,128)(2,1)S(1)}, u32[]{:S(2)}, u32[]{:S(2)}) collective-permute-start(bf16[2064,128]{1,0:T(8,128)(2,1)S(1)} %get-tuple-element.22.own_ref), channel_id=1, source_target_pairs={{4,1},{6,3},{1,4},{8,5},{3,6},{10,7},{5,8},{12,9},{7,10},{14,11},{... | collective-permute-start | bytes 1585160 | tf_op jit(solution)/shard_map/ppermute | solution.py:310
  5.6 0.1 collective-permute-start.3
  5.7 3.0 %shard_map.38 = (bf16[4,256,1024]{2,1,0:T(8,128)(2,1)S(1)}, f32[4,128,512]{2,1,0:T(8,128)S(1)}) custom-call(bf16[2064,128]{1,0:T(8,128)(2,1)S(1)} %get-tuple-element.22.own_ref, bf16[1040,128]{1,0:T(8,128)(2,1)S(1)} %collective-permute-done.pair_ref), custom_call_target="tpu_custom_call" | custom-call | flops 8589934592 | bytes 2097152 | tf_op jit(solution)/shard_map/pallas_call | solution.py:274
  8.7 0.0 collective-permute-done.3.refs_0_
  8.7 1.1 %shard_map.39.refs_1_ = f32[2,128,512]{2,1,0:T(8,128)S(1)} custom-call(bf16[4,256,1024]{2,1,0:T(8,128)(2,1)S(1)} %get-tuple-element.24.query_ref, bf16[1040,128]{1,0:T(8,128)(2,1)S(1)} %collective-permute-done.3.refs_0_, f32[4,128,512]{2,1,0:T(8,128)S(1)} %get-tuple-element.28.refs_1_.refs_2_), custom_call_target="tpu_custom_call" | custom-call | flops 8589934592 | bytes 2097152 | tf_op jit(solution)/shard_map/pallas_call | solution.py:294
  9.8 4.0 %collective-permute-start.4 = (bf16[1040,128]{1,0:T(8,128)(2,1)S(1)}, bf16[1040,128]{1,0:T(8,128)(2,1)S(1)}, u32[]{:S(2)}, u32[]{:S(2)}) collective-permute-start(bf16[1040,128]{1,0:T(8,128)(2,1)S(1)} %get-tuple-element.29), channel_id=1, source_target_pairs={{4,2},{5,3},{2,4},{3,5},{8,6},{9,7},{6,8},{7,9},{12,10},{13,11},{1... | collective-permute-start | bytes 798728 | tf_op jit(solution)/shard_map/ppermute | solution.py:310
  13.8 2.3 %collective-permute-start.2 = (bf16[1040,128]{1,0:T(8,128)(2,1)S(1)}, bf16[1040,128]{1,0:T(8,128)(2,1)S(1)}, u32[]{:S(2)}, u32[]{:S(2)}) collective-permute-start(bf16[1040,128]{1,0:T(8,128)(2,1)S(1)} %get-tuple-element.26), channel_id=1, source_target_pairs={{4,2},{5,3},{2,4},{3,5},{8,6},{9,7},{6,8},{7,9},{12,10},{13,11},{1... | collective-permute-start | bytes 798728 | tf_op jit(solution)/shard_map/ppermute | solution.py:310
  16.2 1.1 %collective-permute-start.6 = (bf16[2064,128]{1,0:T(8,128)(2,1)S(1)}, bf16[2064,128]{1,0:T(8,128)(2,1)S(1)}, u32[]{:S(2)}, u32[]{:S(2)}) collective-permute-start(bf16[2064,128]{1,0:T(8,128)(2,1)S(1)} %collective-permute-done.5.refs_0_), channel_id=1, source_target_pairs={{1,0},{0,1},{3,2},{2,3},{5,4},{4,5},{7,6},{6,7},{9,8},{8,9},{11,10... | collective-permute-start | bytes 1585160 | tf_op jit(solution)/shard_map/ppermute | solution.py:310
  17.2 2.0 %shard_map.40.refs_1_ = f32[4,128,512]{2,1,0:T(8,128)S(1)} custom-call(bf16[4,256,1024]{2,1,0:T(8,128)(2,1)S(1)} %get-tuple-element.24.query_ref, bf16[2064,128]{1,0:T(8,128)(2,1)S(1)} %collective-permute-done.5.refs_0_, f32[2,128,512]{2,1,0:T(8,128)S(1)} %shard_map.39.refs_1_, f32[4,128,512]{2,1,0:T(8,128)S(1)} %get-tuple-element.28.refs_1_.refs_2_), custom_call_target="tpu_custom_call" | custom-call | flops 8589934592 | bytes 2097152 | tf_op jit(solution)/shard_map/pallas_call | solution.py:294
  19.2 1.9 %shard_map.41.refs_1_ = f32[4,128,512]{2,1,0:T(8,128)S(1)} custom-call(bf16[4,256,1024]{2,1,0:T(8,128)(2,1)S(1)} %get-tuple-element.24.query_ref, bf16[2064,128]{1,0:T(8,128)(2,1)S(1)} %collective-permute-done.6.refs_0_, f32[4,128,512]{2,1,0:T(8,128)S(1)} %shard_map.40.refs_1_), custom_call_target="tpu_custom_call" | custom-call | flops 8589934592 | bytes 2097152 | tf_op jit(solution)/shard_map/pallas_call | solution.py:294
  21.1 1.1 %collective-permute-done.4.refs_0_ = bf16[1040,128]{1,0:T(8,128)(2,1)S(1)} collective-permute-done((bf16[1040,128]{1,0:T(8,128)(2,1)S(1)}, bf16[1040,128]{1,0:T(8,128)(2,1)S(1)}, u32[]{:S(2)}, u32[]{:S(2)}) %collective-permute-start.4) | collective-permute-done | bytes 266272 | tf_op jit(solution)/shard_map/ppermute | solution.py:310
  22.2 1.4 %collective-permute-start.7 = (bf16[1040,128]{1,0:T(8,128)(2,1)S(1)}, bf16[1040,128]{1,0:T(8,128)(2,1)S(1)}, u32[]{:S(2)}, u32[]{:S(2)}) collective-permute-start(bf16[1040,128]{1,0:T(8,128)(2,1)S(1)} %collective-permute-done.4.refs_0_), channel_id=1, source_target_pairs={{1,0},{0,1},{3,2},{2,3},{5,4},{4,5},{7,6},{6,7},{9,8},{8,9},{11,10... | collective-permute-start | bytes 798728 | tf_op jit(solution)/shard_map/ppermute | solution.py:310
  23.6 1.1 %shard_map.42.refs_1_ = f32[2,128,512]{2,1,0:T(8,128)S(1)} custom-call(bf16[4,256,1024]{2,1,0:T(8,128)(2,1)S(1)} %get-tuple-element.24.query_ref, bf16[1040,128]{1,0:T(8,128)(2,1)S(1)} %collective-permute-done.4.refs_0_, f32[4,128,512]{2,1,0:T(8,128)S(1)} %shard_map.41.refs_1_), custom_call_target="tpu_custom_call" | custom-call | flops 8589934592 | bytes 2097152 | tf_op jit(solution)/shard_map/pallas_call | solution.py:294
  24.7 0.1 collective-permute-done.7.refs_0_
  24.7 1.1 %shard_map.43.refs_2_ = f32[2,128,512]{2,1,0:T(8,128)S(1)} custom-call(bf16[4,256,1024]{2,1,0:T(8,128)(2,1)S(1)} %get-tuple-element.24.query_ref, bf16[1040,128]{1,0:T(8,128)(2,1)S(1)} %collective-permute-done.7.refs_0_, f32[2,128,512]{2,1,0:T(8,128)S(1)} %shard_map.42.refs_1_), custom_call_target="tpu_custom_call" | custom-call | flops 8589934592 | bytes 2097152 | tf_op jit(solution)/shard_map/pallas_call | solution.py:294
  25.9 2.1 %collective-permute-done.2.refs_0_ = bf16[1040,128]{1,0:T(8,128)(2,1)S(1)} collective-permute-done((bf16[1040,128]{1,0:T(8,128)(2,1)S(1)}, bf16[1040,128]{1,0:T(8,128)(2,1)S(1)}, u32[]{:S(2)}, u32[]{:S(2)}) %collective-permute-start.2) | collective-permute-done | bytes 266272 | tf_op jit(solution)/shard_map/ppermute | solution.py:310
  27.9 0.9 %collective-permute-start.8 = (bf16[1040,128]{1,0:T(8,128)(2,1)S(1)}, bf16[1040,128]{1,0:T(8,128)(2,1)S(1)}, u32[]{:S(2)}, u32[]{:S(2)}) collective-permute-start(bf16[1040,128]{1,0:T(8,128)(2,1)S(1)} %collective-permute-done.2.refs_0_), channel_id=1, source_target_pairs={{1,0},{0,1},{3,2},{2,3},{5,4},{4,5},{7,6},{6,7},{9,8},{8,9},{11,10... | collective-permute-start | bytes 798728 | tf_op jit(solution)/shard_map/ppermute | solution.py:310
  28.8 1.1 %shard_map.44.refs_1_ = f32[2,128,512]{2,1,0:T(8,128)S(1)} custom-call(bf16[4,256,1024]{2,1,0:T(8,128)(2,1)S(1)} %get-tuple-element.24.query_ref, bf16[1040,128]{1,0:T(8,128)(2,1)S(1)} %collective-permute-done.2.refs_0_, f32[4,128,512]{2,1,0:T(8,128)S(1)} %shard_map.41.refs_1_), custom_call_target="tpu_custom_call" | custom-call | flops 8589934592 | bytes 2097152 | tf_op jit(solution)/shard_map/pallas_call | solution.py:294
  29.9 0.1 collective-permute-done.8.refs_0_
  30.0 1.1 %shard_map.45.refs_1_ = f32[2,128,512]{2,1,0:T(8,128)S(1)} custom-call(bf16[4,256,1024]{2,1,0:T(8,128)(2,1)S(1)} %get-tuple-element.24.query_ref, bf16[1040,128]{1,0:T(8,128)(2,1)S(1)} %collective-permute-done.8.refs_0_, f32[2,128,512]{2,1,0:T(8,128)S(1)} %shard_map.44.refs_1_), custom_call_target="tpu_custom_call" | custom-call | flops 8589934592 | bytes 2097152 | tf_op jit(solution)/shard_map/pallas_call | solution.py:294
  31.1 2.8 %shard_map.46 = f32[4,512,128]{2,1,0:T(8,128)} custom-call(bf16[4,256,1024]{2,1,0:T(8,128)(2,1)S(1)} %get-tuple-element.24.query_ref, bf16[2064,128]{1,0:T(8,128)(2,1)S(1)} %collective-permute-done.1.refs_0_, f32[2,128,512]{2,1,0:T(8,128)S(1)} %shard_map.45.refs_1_, f32[2,128,512]{2,1,0:T(8,128)S(1)} %shard_map.43.refs_2_), custom_call_target="tpu_custom_call" | custom-call | flops 8589934592 | bytes 2097152 | tf_op jit(solution)/shard_map/pallas_call | solution.py:294
  (4 shorter events, 0.0 us)
Async XLA Ops:
  1.2 4.5 %collective-permute-start = (bf16[1040,128]{1,0:T(8,128)(2,1)S(1)}, bf16[1040,128]{1,0:T(8,128)(2,1)S(1)}, u32[]{:S(2)}, u32[]{:S(2)}) collective-permute-start(bf16[1040,128]{1,0:T(8,128)(2,1)S(1)} %get-tuple-element.26), channel_id=1, source_target_pairs={{1,0},{0,1},{3,2},{2,3},{5,4},{4,5},{7,6},{6,7},{9,8},{8,9},{11,10... | collective-permute-start | bytes 798728 | tf_op jit(solution)/shard_map/ppermute | solution.py:310
  1.9 14.2 %collective-permute-start.5 = (bf16[2064,128]{1,0:T(8,128)(2,1)S(1)}, bf16[2064,128]{1,0:T(8,128)(2,1)S(1)}, u32[]{:S(2)}, u32[]{:S(2)}) collective-permute-start(bf16[2064,128]{1,0:T(8,128)(2,1)S(1)} %get-tuple-element.22.own_ref), channel_id=1, source_target_pairs={{2,0},{3,1},{0,2},{1,3},{6,4},{7,5},{4,6},{5,7},{10,8},{11,9},{8,1... | collective-permute-start | bytes 1585160 | tf_op jit(solution)/shard_map/ppermute | solution.py:310
  2.2 28.9 %collective-permute-start.1 = (bf16[2064,128]{1,0:T(8,128)(2,1)S(1)}, bf16[2064,128]{1,0:T(8,128)(2,1)S(1)}, u32[]{:S(2)}, u32[]{:S(2)}) collective-permute-start(bf16[2064,128]{1,0:T(8,128)(2,1)S(1)} %get-tuple-element.22.own_ref), channel_id=1, source_target_pairs={{4,1},{6,3},{1,4},{8,5},{3,6},{10,7},{5,8},{12,9},{7,10},{14,11},{... | collective-permute-start | bytes 1585160 | tf_op jit(solution)/shard_map/ppermute | solution.py:310
  5.6 3.1 %collective-permute-start.3 = (bf16[1040,128]{1,0:T(8,128)(2,1)S(1)}, bf16[1040,128]{1,0:T(8,128)(2,1)S(1)}, u32[]{:S(2)}, u32[]{:S(2)}) collective-permute-start(bf16[1040,128]{1,0:T(8,128)(2,1)S(1)} %get-tuple-element.29), channel_id=1, source_target_pairs={{1,0},{0,1},{3,2},{2,3},{5,4},{4,5},{7,6},{6,7},{9,8},{8,9},{11,10... | collective-permute-start | bytes 798728 | tf_op jit(solution)/shard_map/ppermute | solution.py:310
  9.8 12.5 %collective-permute-start.4 = (bf16[1040,128]{1,0:T(8,128)(2,1)S(1)}, bf16[1040,128]{1,0:T(8,128)(2,1)S(1)}, u32[]{:S(2)}, u32[]{:S(2)}) collective-permute-start(bf16[1040,128]{1,0:T(8,128)(2,1)S(1)} %get-tuple-element.29), channel_id=1, source_target_pairs={{4,2},{5,3},{2,4},{3,5},{8,6},{9,7},{6,8},{7,9},{12,10},{13,11},{1... | collective-permute-start | bytes 798728 | tf_op jit(solution)/shard_map/ppermute | solution.py:310
  13.8 14.1 %collective-permute-start.2 = (bf16[1040,128]{1,0:T(8,128)(2,1)S(1)}, bf16[1040,128]{1,0:T(8,128)(2,1)S(1)}, u32[]{:S(2)}, u32[]{:S(2)}) collective-permute-start(bf16[1040,128]{1,0:T(8,128)(2,1)S(1)} %get-tuple-element.26), channel_id=1, source_target_pairs={{4,2},{5,3},{2,4},{3,5},{8,6},{9,7},{6,8},{7,9},{12,10},{13,11},{1... | collective-permute-start | bytes 798728 | tf_op jit(solution)/shard_map/ppermute | solution.py:310
  16.2 3.0 %collective-permute-start.6 = (bf16[2064,128]{1,0:T(8,128)(2,1)S(1)}, bf16[2064,128]{1,0:T(8,128)(2,1)S(1)}, u32[]{:S(2)}, u32[]{:S(2)}) collective-permute-start(bf16[2064,128]{1,0:T(8,128)(2,1)S(1)} %collective-permute-done.5.refs_0_), channel_id=1, source_target_pairs={{1,0},{0,1},{3,2},{2,3},{5,4},{4,5},{7,6},{6,7},{9,8},{8,9},{11,10... | collective-permute-start | bytes 1585160 | tf_op jit(solution)/shard_map/ppermute | solution.py:310
  22.2 2.5 %collective-permute-start.7 = (bf16[1040,128]{1,0:T(8,128)(2,1)S(1)}, bf16[1040,128]{1,0:T(8,128)(2,1)S(1)}, u32[]{:S(2)}, u32[]{:S(2)}) collective-permute-start(bf16[1040,128]{1,0:T(8,128)(2,1)S(1)} %collective-permute-done.4.refs_0_), channel_id=1, source_target_pairs={{1,0},{0,1},{3,2},{2,3},{5,4},{4,5},{7,6},{6,7},{9,8},{8,9},{11,10... | collective-permute-start | bytes 798728 | tf_op jit(solution)/shard_map/ppermute | solution.py:310
  27.9 2.1 %collective-permute-start.8 = (bf16[1040,128]{1,0:T(8,128)(2,1)S(1)}, bf16[1040,128]{1,0:T(8,128)(2,1)S(1)}, u32[]{:S(2)}, u32[]{:S(2)}) collective-permute-start(bf16[1040,128]{1,0:T(8,128)(2,1)S(1)} %collective-permute-done.2.refs_0_), channel_id=1, source_target_pairs={{1,0},{0,1},{3,2},{2,3},{5,4},{4,5},{7,6},{6,7},{9,8},{8,9},{11,10... | collective-permute-start | bytes 798728 | tf_op jit(solution)/shard_map/ppermute | solution.py:310

commit v9 on v8

--- a/solution.py
+++ b/solution.py
@@ -12,6 +12,7 @@
 period_metres = 4096
 model_amp = 0.5
 vmem = 24 << 20
+chunk = 128
 shares = (64, 64, 64, 64, 64, 64, 64, 64, 64)
 
 OWN = (0, 0, 0, 0)
@@ -64,7 +65,9 @@
 def key_columns(tail_ref, block, freqs, channels, width):
     angle, is_cos = angles(tail_ref, block, freqs, channels)
     high, low = halves(sine(angle + jnp.where(is_cos, period_metres // 4, 0)))
-    return padded([high, low, high, low], width).T.astype(jnp.bfloat16)
+    rows = jnp.concatenate([high, low, high, low], axis=0)
+    rest = jnp.zeros((channels, width - rows.shape[0]), jnp.float32)
+    return jnp.concatenate([rows.T, rest], axis=1).astype(jnp.bfloat16)
 
 
 def query_rows(tail_ref, block, freqs, channels, width):
@@ -250,9 +253,15 @@
         term = total + sums * (2.0 / width)
         if last:
             out_ref, result_ref, sems = out_refs
-            result_ref[f] = term.T
-            copies.append(pltpu.make_async_copy(result_ref.at[f], out_ref.at[f], sems.at[f]))
-            copies[-1].start()
+            for start in range(0, channels, chunk):
+                rows = pl.ds(start, chunk)
+                result_ref[f, rows, :] = term[:, start : start + chunk].T
+                copies.append(
+                    pltpu.make_async_copy(
+                        result_ref.at[f, rows], out_ref.at[f, rows], sems.at[len(copies)]
+                    )
+                )
+                copies[-1].start()
         else:
             out_refs[0][f - span[0]] = term
 
@@ -288,7 +297,7 @@
     freqs, channels, width = shape
     whole = pl.BlockSpec(memory_space=pltpu.VMEM)
     out = shape if last else (span[1], width, channels)
-    scratch = [pltpu.VMEM(shape, jnp.float32), pltpu.SemaphoreType.DMA((freqs,))]
+    scratch = [pltpu.VMEM(shape, jnp.float32), pltpu.SemaphoreType.DMA((freqs * (channels // chunk),))]
     places, spans = tuple(key[1] for key in keys), tuple(key[2] for key in keys)
     held = tuple(total[1] for total in totals)
     return pl.pallas_call(

time: 34.5 us -> 34.5 us (level)
  no operation moved by 1% of the time
where the time goes in v9:
time: 34.5 us; the launch traced here: 34.1 us
  Pallas kernels  16.3 us (47%)
  starting transfers between devices  14.2 us (41%)
  waiting for transfers between devices  3.31 us (10%)
    ppermute x9, starting transfers between devices, fetched(): lax.ppermute(value, axis, [(i, t) for i, t in sources if 0 <= i < count])  14.2 us
    pallas_call x8, Pallas kernels, band_terms(): pl.pallas_call(functools.partial(band_kernel, axis, places, spans, held,...  12.2 us
    ppermute x9, waiting for transfers between devices, fetched(): lax.ppermute(value, axis, [(i, t) for i, t in sources if 0 <= i < count])  3.31 us
    pallas_call x1, Pallas kernels, chip_terms(): pl.pallas_call(functools.partial(chip_kernel, axis, low), out_shape=[jax....  2.96 us
    pallas_call x1, Pallas kernels, pack(): pl.pallas_call(pack_kernel, out_shape=[jax.ShapeDtypeStruct((part * chann...  1.17 us
  transfers between devices with their start and end apart: 9, of which 4 were waited for; matrix products, arithmetic and copies ran while one was open for 0% of the time, Pallas kernels for 36%

profile of v9, /device:TPU:19, one launch (start us, length us, event | category | flops | bytes accessed | tf_op | source)
XLA Modules:
  0.0 34.1 jit_solution(3169207858643246685)
XLA Ops:
  0.0 1.2 %shard_map.37 = (bf16[2064,128]{1,0:T(8,128)(2,1)S(1)}, bf16[1040,128]{1,0:T(8,128)(2,1)S(1)}, bf16[1040,128]{1,0:T(8,128)(2,1)S(1)}) custom-call(bf16[2048,128]{1,0:T(8,128)(2,1)} %bitcast.2, s32[1,512]{1,0:T(1,128)} %bitcast.3, s32[4]{0:T(128)} %bins_ref.1), custom_call_target="tpu_custom_call" | custom-call | bytes 1048576 | tf_op jit(solution)/shard_map/pallas_call | solution.py:138
  1.2 0.7 %collective-permute-start = (bf16[1040,128]{1,0:T(8,128)(2,1)S(1)}, bf16[1040,128]{1,0:T(8,128)(2,1)S(1)}, u32[]{:S(2)}, u32[]{:S(2)}) collective-permute-start(bf16[1040,128]{1,0:T(8,128)(2,1)S(1)} %get-tuple-element.26), channel_id=1, source_target_pairs={{1,0},{0,1},{3,2},{2,3},{5,4},{4,5},{7,6},{6,7},{9,8},{8,9},{11,10... | collective-permute-start | bytes 798728 | tf_op jit(solution)/shard_map/ppermute | solution.py:319
  1.9 0.3 collective-permute-start.5
  2.2 3.4 %collective-permute-start.1 = (bf16[2064,128]{1,0:T(8,128)(2,1)S(1)}, bf16[2064,128]{1,0:T(8,128)(2,1)S(1)}, u32[]{:S(2)}, u32[]{:S(2)}) collective-permute-start(bf16[2064,128]{1,0:T(8,128)(2,1)S(1)} %get-tuple-element.22.own_ref), channel_id=1, source_target_pairs={{4,1},{6,3},{1,4},{8,5},{3,6},{10,7},{5,8},{12,9},{7,10},{14,11},{... | collective-permute-start | bytes 1585160 | tf_op jit(solution)/shard_map/ppermute | solution.py:319
  5.6 0.1 collective-permute-start.3
  5.7 0.0 collective-permute-done.pair_ref
  5.7 3.0 %shard_map.38 = (bf16[4,256,1024]{2,1,0:T(8,128)(2,1)S(1)}, f32[4,128,512]{2,1,0:T(8,128)S(1)}) custom-call(bf16[2064,128]{1,0:T(8,128)(2,1)S(1)} %get-tuple-element.22.own_ref, bf16[1040,128]{1,0:T(8,128)(2,1)S(1)} %collective-permute-done.pair_ref), custom_call_target="tpu_custom_call" | custom-call | flops 8589934592 | bytes 2097152 | tf_op jit(solution)/shard_map/pallas_call | solution.py:283
  8.7 1.1 %shard_map.39.refs_1_ = f32[2,128,512]{2,1,0:T(8,128)S(1)} custom-call(bf16[4,256,1024]{2,1,0:T(8,128)(2,1)S(1)} %get-tuple-element.24.query_ref, bf16[1040,128]{1,0:T(8,128)(2,1)S(1)} %collective-permute-done.3.refs_0_, f32[4,128,512]{2,1,0:T(8,128)S(1)} %get-tuple-element.28.refs_1_.refs_2_), custom_call_target="tpu_custom_call" | custom-call | flops 8589934592 | bytes 2097152 | tf_op jit(solution)/shard_map/pallas_call | solution.py:303
  9.8 4.1 %collective-permute-start.4 = (bf16[1040,128]{1,0:T(8,128)(2,1)S(1)}, bf16[1040,128]{1,0:T(8,128)(2,1)S(1)}, u32[]{:S(2)}, u32[]{:S(2)}) collective-permute-start(bf16[1040,128]{1,0:T(8,128)(2,1)S(1)} %get-tuple-element.29), channel_id=1, source_target_pairs={{4,2},{5,3},{2,4},{3,5},{8,6},{9,7},{6,8},{7,9},{12,10},{13,11},{1... | collective-permute-start | bytes 798728 | tf_op jit(solution)/shard_map/ppermute | solution.py:319
  13.8 2.3 %collective-permute-start.2 = (bf16[1040,128]{1,0:T(8,128)(2,1)S(1)}, bf16[1040,128]{1,0:T(8,128)(2,1)S(1)}, u32[]{:S(2)}, u32[]{:S(2)}) collective-permute-start(bf16[1040,128]{1,0:T(8,128)(2,1)S(1)} %get-tuple-element.26), channel_id=1, source_target_pairs={{4,2},{5,3},{2,4},{3,5},{8,6},{9,7},{6,8},{7,9},{12,10},{13,11},{1... | collective-permute-start | bytes 798728 | tf_op jit(solution)/shard_map/ppermute | solution.py:319
  16.1 1.1 %collective-permute-start.6 = (bf16[2064,128]{1,0:T(8,128)(2,1)S(1)}, bf16[2064,128]{1,0:T(8,128)(2,1)S(1)}, u32[]{:S(2)}, u32[]{:S(2)}) collective-permute-start(bf16[2064,128]{1,0:T(8,128)(2,1)S(1)} %collective-permute-done.5.refs_0_), channel_id=1, source_target_pairs={{1,0},{0,1},{3,2},{2,3},{5,4},{4,5},{7,6},{6,7},{9,8},{8,9},{11,10... | collective-permute-start | bytes 1585160 | tf_op jit(solution)/shard_map/ppermute | solution.py:319
  17.2 2.0 %shard_map.40.refs_1_ = f32[4,128,512]{2,1,0:T(8,128)S(1)} custom-call(bf16[4,256,1024]{2,1,0:T(8,128)(2,1)S(1)} %get-tuple-element.24.query_ref, bf16[2064,128]{1,0:T(8,128)(2,1)S(1)} %collective-permute-done.5.refs_0_, f32[2,128,512]{2,1,0:T(8,128)S(1)} %shard_map.39.refs_1_, f32[4,128,512]{2,1,0:T(8,128)S(1)} %get-tuple-element.28.refs_1_.refs_2_), custom_call_target="tpu_custom_call" | custom-call | flops 8589934592 | bytes 2097152 | tf_op jit(solution)/shard_map/pallas_call | solution.py:303
  19.2 1.9 %shard_map.41.refs_1_ = f32[4,128,512]{2,1,0:T(8,128)S(1)} custom-call(bf16[4,256,1024]{2,1,0:T(8,128)(2,1)S(1)} %get-tuple-element.24.query_ref, bf16[2064,128]{1,0:T(8,128)(2,1)S(1)} %collective-permute-done.6.refs_0_, f32[4,128,512]{2,1,0:T(8,128)S(1)} %shard_map.40.refs_1_), custom_call_target="tpu_custom_call" | custom-call | flops 8589934592 | bytes 2097152 | tf_op jit(solution)/shard_map/pallas_call | solution.py:303
  21.2 1.1 %collective-permute-done.4.refs_0_ = bf16[1040,128]{1,0:T(8,128)(2,1)S(1)} collective-permute-done((bf16[1040,128]{1,0:T(8,128)(2,1)S(1)}, bf16[1040,128]{1,0:T(8,128)(2,1)S(1)}, u32[]{:S(2)}, u32[]{:S(2)}) %collective-permute-start.4) | collective-permute-done | bytes 266272 | tf_op jit(solution)/shard_map/ppermute | solution.py:319
  22.2 1.4 %collective-permute-start.7 = (bf16[1040,128]{1,0:T(8,128)(2,1)S(1)}, bf16[1040,128]{1,0:T(8,128)(2,1)S(1)}, u32[]{:S(2)}, u32[]{:S(2)}) collective-permute-start(bf16[1040,128]{1,0:T(8,128)(2,1)S(1)} %collective-permute-done.4.refs_0_), channel_id=1, source_target_pairs={{1,0},{0,1},{3,2},{2,3},{5,4},{4,5},{7,6},{6,7},{9,8},{8,9},{11,10... | collective-permute-start | bytes 798728 | tf_op jit(solution)/shard_map/ppermute | solution.py:319
  23.6 1.1 %shard_map.42.refs_1_ = f32[2,128,512]{2,1,0:T(8,128)S(1)} custom-call(bf16[4,256,1024]{2,1,0:T(8,128)(2,1)S(1)} %get-tuple-element.24.query_ref, bf16[1040,128]{1,0:T(8,128)(2,1)S(1)} %collective-permute-done.4.refs_0_, f32[4,128,512]{2,1,0:T(8,128)S(1)} %shard_map.41.refs_1_), custom_call_target="tpu_custom_call" | custom-call | flops 8589934592 | bytes 2097152 | tf_op jit(solution)/shard_map/pallas_call | solution.py:303
  24.7 0.1 collective-permute-done.7.refs_0_
  24.7 1.1 %shard_map.43.refs_2_ = f32[2,128,512]{2,1,0:T(8,128)S(1)} custom-call(bf16[4,256,1024]{2,1,0:T(8,128)(2,1)S(1)} %get-tuple-element.24.query_ref, bf16[1040,128]{1,0:T(8,128)(2,1)S(1)} %collective-permute-done.7.refs_0_, f32[2,128,512]{2,1,0:T(8,128)S(1)} %shard_map.42.refs_1_), custom_call_target="tpu_custom_call" | custom-call | flops 8589934592 | bytes 2097152 | tf_op jit(solution)/shard_map/pallas_call | solution.py:303
  25.9 2.1 %collective-permute-done.2.refs_0_ = bf16[1040,128]{1,0:T(8,128)(2,1)S(1)} collective-permute-done((bf16[1040,128]{1,0:T(8,128)(2,1)S(1)}, bf16[1040,128]{1,0:T(8,128)(2,1)S(1)}, u32[]{:S(2)}, u32[]{:S(2)}) %collective-permute-start.2) | collective-permute-done | bytes 266272 | tf_op jit(solution)/shard_map/ppermute | solution.py:319
  27.9 0.9 %collective-permute-start.8 = (bf16[1040,128]{1,0:T(8,128)(2,1)S(1)}, bf16[1040,128]{1,0:T(8,128)(2,1)S(1)}, u32[]{:S(2)}, u32[]{:S(2)}) collective-permute-start(bf16[1040,128]{1,0:T(8,128)(2,1)S(1)} %collective-permute-done.2.refs_0_), channel_id=1, source_target_pairs={{1,0},{0,1},{3,2},{2,3},{5,4},{4,5},{7,6},{6,7},{9,8},{8,9},{11,10... | collective-permute-start | bytes 798728 | tf_op jit(solution)/shard_map/ppermute | solution.py:319
  28.8 1.1 %shard_map.44.refs_1_ = f32[2,128,512]{2,1,0:T(8,128)S(1)} custom-call(bf16[4,256,1024]{2,1,0:T(8,128)(2,1)S(1)} %get-tuple-element.24.query_ref, bf16[1040,128]{1,0:T(8,128)(2,1)S(1)} %collective-permute-done.2.refs_0_, f32[4,128,512]{2,1,0:T(8,128)S(1)} %shard_map.41.refs_1_), custom_call_target="tpu_custom_call" | custom-call | flops 8589934592 | bytes 2097152 | tf_op jit(solution)/shard_map/pallas_call | solution.py:303
  29.9 0.1 collective-permute-done.8.refs_0_
  30.0 1.1 %shard_map.45.refs_1_ = f32[2,128,512]{2,1,0:T(8,128)S(1)} custom-call(bf16[4,256,1024]{2,1,0:T(8,128)(2,1)S(1)} %get-tuple-element.24.query_ref, bf16[1040,128]{1,0:T(8,128)(2,1)S(1)} %collective-permute-done.8.refs_0_, f32[2,128,512]{2,1,0:T(8,128)S(1)} %shard_map.44.refs_1_), custom_call_target="tpu_custom_call" | custom-call | flops 8589934592 | bytes 2097152 | tf_op jit(solution)/shard_map/pallas_call | solution.py:303
  31.1 2.9 %shard_map.46 = f32[4,512,128]{2,1,0:T(8,128)} custom-call(bf16[4,256,1024]{2,1,0:T(8,128)(2,1)S(1)} %get-tuple-element.24.query_ref, bf16[2064,128]{1,0:T(8,128)(2,1)S(1)} %collective-permute-done.1.refs_0_, f32[2,128,512]{2,1,0:T(8,128)S(1)} %shard_map.45.refs_1_, f32[2,128,512]{2,1,0:T(8,128)S(1)} %shard_map.43.refs_2_), custom_call_target="tpu_custom_call" | custom-call | flops 8589934592 | bytes 2097152 | tf_op jit(solution)/shard_map/pallas_call | solution.py:303
  (4 shorter events, 0.0 us)
Async XLA Ops:
  1.2 4.5 %collective-permute-start = (bf16[1040,128]{1,0:T(8,128)(2,1)S(1)}, bf16[1040,128]{1,0:T(8,128)(2,1)S(1)}, u32[]{:S(2)}, u32[]{:S(2)}) collective-permute-start(bf16[1040,128]{1,0:T(8,128)(2,1)S(1)} %get-tuple-element.26), channel_id=1, source_target_pairs={{1,0},{0,1},{3,2},{2,3},{5,4},{4,5},{7,6},{6,7},{9,8},{8,9},{11,10... | collective-permute-start | bytes 798728 | tf_op jit(solution)/shard_map/ppermute | solution.py:319
  1.9 14.2 %collective-permute-start.5 = (bf16[2064,128]{1,0:T(8,128)(2,1)S(1)}, bf16[2064,128]{1,0:T(8,128)(2,1)S(1)}, u32[]{:S(2)}, u32[]{:S(2)}) collective-permute-start(bf16[2064,128]{1,0:T(8,128)(2,1)S(1)} %get-tuple-element.22.own_ref), channel_id=1, source_target_pairs={{2,0},{3,1},{0,2},{1,3},{6,4},{7,5},{4,6},{5,7},{10,8},{11,9},{8,1... | collective-permute-start | bytes 1585160 | tf_op jit(solution)/shard_map/ppermute | solution.py:319
  2.2 28.9 %collective-permute-start.1 = (bf16[2064,128]{1,0:T(8,128)(2,1)S(1)}, bf16[2064,128]{1,0:T(8,128)(2,1)S(1)}, u32[]{:S(2)}, u32[]{:S(2)}) collective-permute-start(bf16[2064,128]{1,0:T(8,128)(2,1)S(1)} %get-tuple-element.22.own_ref), channel_id=1, source_target_pairs={{4,1},{6,3},{1,4},{8,5},{3,6},{10,7},{5,8},{12,9},{7,10},{14,11},{... | collective-permute-start | bytes 1585160 | tf_op jit(solution)/shard_map/ppermute | solution.py:319
  5.6 3.1 %collective-permute-start.3 = (bf16[1040,128]{1,0:T(8,128)(2,1)S(1)}, bf16[1040,128]{1,0:T(8,128)(2,1)S(1)}, u32[]{:S(2)}, u32[]{:S(2)}) collective-permute-start(bf16[1040,128]{1,0:T(8,128)(2,1)S(1)} %get-tuple-element.29), channel_id=1, source_target_pairs={{1,0},{0,1},{3,2},{2,3},{5,4},{4,5},{7,6},{6,7},{9,8},{8,9},{11,10... | collective-permute-start | bytes 798728 | tf_op jit(solution)/shard_map/ppermute | solution.py:319
  9.8 12.5 %collective-permute-start.4 = (bf16[1040,128]{1,0:T(8,128)(2,1)S(1)}, bf16[1040,128]{1,0:T(8,128)(2,1)S(1)}, u32[]{:S(2)}, u32[]{:S(2)}) collective-permute-start(bf16[1040,128]{1,0:T(8,128)(2,1)S(1)} %get-tuple-element.29), channel_id=1, source_target_pairs={{4,2},{5,3},{2,4},{3,5},{8,6},{9,7},{6,8},{7,9},{12,10},{13,11},{1... | collective-permute-start | bytes 798728 | tf_op jit(solution)/shard_map/ppermute | solution.py:319
  13.8 14.1 %collective-permute-start.2 = (bf16[1040,128]{1,0:T(8,128)(2,1)S(1)}, bf16[1040,128]{1,0:T(8,128)(2,1)S(1)}, u32[]{:S(2)}, u32[]{:S(2)}) collective-permute-start(bf16[1040,128]{1,0:T(8,128)(2,1)S(1)} %get-tuple-element.26), channel_id=1, source_target_pairs={{4,2},{5,3},{2,4},{3,5},{8,6},{9,7},{6,8},{7,9},{12,10},{13,11},{1... | collective-permute-start | bytes 798728 | tf_op jit(solution)/shard_map/ppermute | solution.py:319
  16.1 3.1 %collective-permute-start.6 = (bf16[2064,128]{1,0:T(8,128)(2,1)S(1)}, bf16[2064,128]{1,0:T(8,128)(2,1)S(1)}, u32[]{:S(2)}, u32[]{:S(2)}) collective-permute-start(bf16[2064,128]{1,0:T(8,128)(2,1)S(1)} %collective-permute-done.5.refs_0_), channel_id=1, source_target_pairs={{1,0},{0,1},{3,2},{2,3},{5,4},{4,5},{7,6},{6,7},{9,8},{8,9},{11,10... | collective-permute-start | bytes 1585160 | tf_op jit(solution)/shard_map/ppermute | solution.py:319
  22.2 2.5 %collective-permute-start.7 = (bf16[1040,128]{1,0:T(8,128)(2,1)S(1)}, bf16[1040,128]{1,0:T(8,128)(2,1)S(1)}, u32[]{:S(2)}, u32[]{:S(2)}) collective-permute-start(bf16[1040,128]{1,0:T(8,128)(2,1)S(1)} %collective-permute-done.4.refs_0_), channel_id=1, source_target_pairs={{1,0},{0,1},{3,2},{2,3},{5,4},{4,5},{7,6},{6,7},{9,8},{8,9},{11,10... | collective-permute-start | bytes 798728 | tf_op jit(solution)/shard_map/ppermute | solution.py:319
  27.9 2.1 %collective-permute-start.8 = (bf16[1040,128]{1,0:T(8,128)(2,1)S(1)}, bf16[1040,128]{1,0:T(8,128)(2,1)S(1)}, u32[]{:S(2)}, u32[]{:S(2)}) collective-permute-start(bf16[1040,128]{1,0:T(8,128)(2,1)S(1)} %collective-permute-done.2.refs_0_), channel_id=1, source_target_pairs={{1,0},{0,1},{3,2},{2,3},{5,4},{4,5},{7,6},{6,7},{9,8},{8,9},{11,10... | collective-permute-start | bytes 798728 | tf_op jit(solution)/shard_map/ppermute | solution.py:319

commit v10 on v8

--- a/solution.py
+++ b/solution.py
@@ -16,10 +16,10 @@
 
 OWN = (0, 0, 0, 0)
 PAIR = (1, -1, 1, -1)
-NEAR = (2, 2, -2, -2)
+NEAR = (3, 1, -1, -3)
 CROSS = (-2, -2, 2, 2)
 FAR = (-3, 3, -3, 3)
-NEAR_OF_PAIR = (3, 1, -1, -3)
+NEAR_OF_PAIR = (2, 2, -2, -2)
 CROSS_OF_PAIR = (-1, -3, 3, 1)
 
 

time: 34.5 us -> 34.5 us (level)
  waiting for transfers between devices: 3.33 us -> 2.86 us
  starting transfers between devices: 14.2 us -> 14.6 us
    ppermute x9, waiting for transfers between devices: 3.33 us -> 2.86 us  [fetched(): lax.ppermute(value, axis, [(i, t) for i, t in sources if 0 <= i < count])]
    ppermute x9, starting transfers between devices: 14.2 us -> 14.6 us  [fetched(): lax.ppermute(value, axis, [(i, t) for i, t in sources if 0 <= i < count])]
where the time goes in v10:
time: 34.5 us; the launch traced here: 34 us
  Pallas kernels  16.3 us (47%)
  starting transfers between devices  14.6 us (42%)
  waiting for transfers between devices  2.86 us (8%)
    ppermute x9, starting transfers between devices, fetched(): lax.ppermute(value, axis, [(i, t) for i, t in sources if 0 <= i < count])  14.6 us
    pallas_call x8, Pallas kernels, band_terms(): pl.pallas_call(functools.partial(band_kernel, axis, places, spans, held,...  12.2 us
    pallas_call x1, Pallas kernels, chip_terms(): pl.pallas_call(functools.partial(chip_kernel, axis, low), out_shape=[jax....  2.95 us
    ppermute x9, waiting for transfers between devices, fetched(): lax.ppermute(value, axis, [(i, t) for i, t in sources if 0 <= i < count])  2.86 us
    pallas_call x1, Pallas kernels, pack(): pl.pallas_call(pack_kernel, out_shape=[jax.ShapeDtypeStruct((part * chann...  1.17 us
  transfers between devices with their start and end apart: 9, of which 4 were waited for; matrix products, arithmetic and copies ran while one was open for 0% of the time, Pallas kernels for 36%

profile of v10, /device:TPU:19, one launch (start us, length us, event | category | flops | bytes accessed | tf_op | source)
XLA Modules:
  0.0 34.0 jit_solution(17361560351687195437)
XLA Ops:
  0.0 1.2 %shard_map.37 = (bf16[2064,128]{1,0:T(8,128)(2,1)S(1)}, bf16[1040,128]{1,0:T(8,128)(2,1)S(1)}, bf16[1040,128]{1,0:T(8,128)(2,1)S(1)}) custom-call(bf16[2048,128]{1,0:T(8,128)(2,1)} %bitcast.2, s32[1,512]{1,0:T(1,128)} %bitcast.3, s32[4]{0:T(128)} %bins_ref.1), custom_call_target="tpu_custom_call" | custom-call | bytes 1048576 | tf_op jit(solution)/shard_map/pallas_call | solution.py:135
  1.2 0.7 %collective-permute-start = (bf16[1040,128]{1,0:T(8,128)(2,1)S(1)}, bf16[1040,128]{1,0:T(8,128)(2,1)S(1)}, u32[]{:S(2)}, u32[]{:S(2)}) collective-permute-start(bf16[1040,128]{1,0:T(8,128)(2,1)S(1)} %get-tuple-element.26), channel_id=1, source_target_pairs={{1,0},{0,1},{3,2},{2,3},{5,4},{4,5},{7,6},{6,7},{9,8},{8,9},{11,10... | collective-permute-start | bytes 798728 | tf_op jit(solution)/shard_map/ppermute | solution.py:310
  1.9 0.2 collective-permute-start.5
  2.1 3.5 %collective-permute-start.1 = (bf16[2064,128]{1,0:T(8,128)(2,1)S(1)}, bf16[2064,128]{1,0:T(8,128)(2,1)S(1)}, u32[]{:S(2)}, u32[]{:S(2)}) collective-permute-start(bf16[2064,128]{1,0:T(8,128)(2,1)S(1)} %get-tuple-element.22.own_ref), channel_id=1, source_target_pairs={{4,1},{6,3},{1,4},{8,5},{3,6},{10,7},{5,8},{12,9},{7,10},{14,11},{... | collective-permute-start | bytes 1585160 | tf_op jit(solution)/shard_map/ppermute | solution.py:310
  5.6 0.1 collective-permute-start.3
  5.7 0.0 collective-permute-done.pair_ref
  5.7 3.0 %shard_map.38 = (bf16[4,256,1024]{2,1,0:T(8,128)(2,1)S(1)}, f32[4,128,512]{2,1,0:T(8,128)S(1)}) custom-call(bf16[2064,128]{1,0:T(8,128)(2,1)S(1)} %get-tuple-element.22.own_ref, bf16[1040,128]{1,0:T(8,128)(2,1)S(1)} %collective-permute-done.pair_ref), custom_call_target="tpu_custom_call" | custom-call | flops 8589934592 | bytes 2097152 | tf_op jit(solution)/shard_map/pallas_call | solution.py:274
  8.7 1.1 %shard_map.39.refs_1_ = f32[2,128,512]{2,1,0:T(8,128)S(1)} custom-call(bf16[4,256,1024]{2,1,0:T(8,128)(2,1)S(1)} %get-tuple-element.24.query_ref, bf16[1040,128]{1,0:T(8,128)(2,1)S(1)} %collective-permute-done.3.refs_0_, f32[4,128,512]{2,1,0:T(8,128)S(1)} %get-tuple-element.28.refs_1_.refs_2_), custom_call_target="tpu_custom_call" | custom-call | flops 8589934592 | bytes 2097152 | tf_op jit(solution)/shard_map/pallas_call | solution.py:294
  9.8 4.1 %collective-permute-start.4 = (bf16[1040,128]{1,0:T(8,128)(2,1)S(1)}, bf16[1040,128]{1,0:T(8,128)(2,1)S(1)}, u32[]{:S(2)}, u32[]{:S(2)}) collective-permute-start(bf16[1040,128]{1,0:T(8,128)(2,1)S(1)} %get-tuple-element.29), channel_id=1, source_target_pairs={{4,2},{5,3},{2,4},{3,5},{8,6},{9,7},{6,8},{7,9},{12,10},{13,11},{1... | collective-permute-start | bytes 798728 | tf_op jit(solution)/shard_map/ppermute | solution.py:310
  13.9 2.3 %collective-permute-start.2 = (bf16[1040,128]{1,0:T(8,128)(2,1)S(1)}, bf16[1040,128]{1,0:T(8,128)(2,1)S(1)}, u32[]{:S(2)}, u32[]{:S(2)}) collective-permute-start(bf16[1040,128]{1,0:T(8,128)(2,1)S(1)} %get-tuple-element.26), channel_id=1, source_target_pairs={{4,2},{5,3},{2,4},{3,5},{8,6},{9,7},{6,8},{7,9},{12,10},{13,11},{1... | collective-permute-start | bytes 798728 | tf_op jit(solution)/shard_map/ppermute | solution.py:310
  16.2 1.1 %collective-permute-start.6 = (bf16[2064,128]{1,0:T(8,128)(2,1)S(1)}, bf16[2064,128]{1,0:T(8,128)(2,1)S(1)}, u32[]{:S(2)}, u32[]{:S(2)}) collective-permute-start(bf16[2064,128]{1,0:T(8,128)(2,1)S(1)} %collective-permute-done.5.refs_0_), channel_id=1, source_target_pairs={{1,0},{0,1},{3,2},{2,3},{5,4},{4,5},{7,6},{6,7},{9,8},{8,9},{11,10... | collective-permute-start | bytes 1585160 | tf_op jit(solution)/shard_map/ppermute | solution.py:310
  17.3 2.0 %shard_map.40.refs_1_ = f32[4,128,512]{2,1,0:T(8,128)S(1)} custom-call(bf16[4,256,1024]{2,1,0:T(8,128)(2,1)S(1)} %get-tuple-element.24.query_ref, bf16[2064,128]{1,0:T(8,128)(2,1)S(1)} %collective-permute-done.5.refs_0_, f32[2,128,512]{2,1,0:T(8,128)S(1)} %shard_map.39.refs_1_, f32[4,128,512]{2,1,0:T(8,128)S(1)} %get-tuple-element.28.refs_1_.refs_2_), custom_call_target="tpu_custom_call" | custom-call | flops 8589934592 | bytes 2097152 | tf_op jit(solution)/shard_map/pallas_call | solution.py:294
  19.2 1.9 %shard_map.41.refs_1_ = f32[4,128,512]{2,1,0:T(8,128)S(1)} custom-call(bf16[4,256,1024]{2,1,0:T(8,128)(2,1)S(1)} %get-tuple-element.24.query_ref, bf16[2064,128]{1,0:T(8,128)(2,1)S(1)} %collective-permute-done.6.refs_0_, f32[4,128,512]{2,1,0:T(8,128)S(1)} %shard_map.40.refs_1_), custom_call_target="tpu_custom_call" | custom-call | flops 8589934592 | bytes 2097152 | tf_op jit(solution)/shard_map/pallas_call | solution.py:294
  21.2 0.9 %collective-permute-done.4.refs_0_ = bf16[1040,128]{1,0:T(8,128)(2,1)S(1)} collective-permute-done((bf16[1040,128]{1,0:T(8,128)(2,1)S(1)}, bf16[1040,128]{1,0:T(8,128)(2,1)S(1)}, u32[]{:S(2)}, u32[]{:S(2)}) %collective-permute-start.4) | collective-permute-done | bytes 266272 | tf_op jit(solution)/shard_map/ppermute | solution.py:310
  22.1 1.6 %collective-permute-start.7 = (bf16[1040,128]{1,0:T(8,128)(2,1)S(1)}, bf16[1040,128]{1,0:T(8,128)(2,1)S(1)}, u32[]{:S(2)}, u32[]{:S(2)}) collective-permute-start(bf16[1040,128]{1,0:T(8,128)(2,1)S(1)} %collective-permute-done.4.refs_0_), channel_id=1, source_target_pairs={{1,0},{0,1},{3,2},{2,3},{5,4},{4,5},{7,6},{6,7},{9,8},{8,9},{11,10... | collective-permute-start | bytes 798728 | tf_op jit(solution)/shard_map/ppermute | solution.py:310
  23.6 1.1 %shard_map.42.refs_1_ = f32[2,128,512]{2,1,0:T(8,128)S(1)} custom-call(bf16[4,256,1024]{2,1,0:T(8,128)(2,1)S(1)} %get-tuple-element.24.query_ref, bf16[1040,128]{1,0:T(8,128)(2,1)S(1)} %collective-permute-done.4.refs_0_, f32[4,128,512]{2,1,0:T(8,128)S(1)} %shard_map.41.refs_1_), custom_call_target="tpu_custom_call" | custom-call | flops 8589934592 | bytes 2097152 | tf_op jit(solution)/shard_map/pallas_call | solution.py:294
  24.7 0.1 collective-permute-done.7.refs_0_
  24.8 1.1 %shard_map.43.refs_2_ = f32[2,128,512]{2,1,0:T(8,128)S(1)} custom-call(bf16[4,256,1024]{2,1,0:T(8,128)(2,1)S(1)} %get-tuple-element.24.query_ref, bf16[1040,128]{1,0:T(8,128)(2,1)S(1)} %collective-permute-done.7.refs_0_, f32[2,128,512]{2,1,0:T(8,128)S(1)} %shard_map.42.refs_1_), custom_call_target="tpu_custom_call" | custom-call | flops 8589934592 | bytes 2097152 | tf_op jit(solution)/shard_map/pallas_call | solution.py:294
  25.9 1.8 %collective-permute-done.2.refs_0_ = bf16[1040,128]{1,0:T(8,128)(2,1)S(1)} collective-permute-done((bf16[1040,128]{1,0:T(8,128)(2,1)S(1)}, bf16[1040,128]{1,0:T(8,128)(2,1)S(1)}, u32[]{:S(2)}, u32[]{:S(2)}) %collective-permute-start.2) | collective-permute-done | bytes 266272 | tf_op jit(solution)/shard_map/ppermute | solution.py:310
  27.8 1.0 %collective-permute-start.8 = (bf16[1040,128]{1,0:T(8,128)(2,1)S(1)}, bf16[1040,128]{1,0:T(8,128)(2,1)S(1)}, u32[]{:S(2)}, u32[]{:S(2)}) collective-permute-start(bf16[1040,128]{1,0:T(8,128)(2,1)S(1)} %collective-permute-done.2.refs_0_), channel_id=1, source_target_pairs={{1,0},{0,1},{3,2},{2,3},{5,4},{4,5},{7,6},{6,7},{9,8},{8,9},{11,10... | collective-permute-start | bytes 798728 | tf_op jit(solution)/shard_map/ppermute | solution.py:310
  28.8 1.1 %shard_map.44.refs_1_ = f32[2,128,512]{2,1,0:T(8,128)S(1)} custom-call(bf16[4,256,1024]{2,1,0:T(8,128)(2,1)S(1)} %get-tuple-element.24.query_ref, bf16[1040,128]{1,0:T(8,128)(2,1)S(1)} %collective-permute-done.2.refs_0_, f32[4,128,512]{2,1,0:T(8,128)S(1)} %shard_map.41.refs_1_), custom_call_target="tpu_custom_call" | custom-call | flops 8589934592 | bytes 2097152 | tf_op jit(solution)/shard_map/pallas_call | solution.py:294
  29.9 0.1 collective-permute-done.8.refs_0_
  30.0 1.1 %shard_map.45.refs_1_ = f32[2,128,512]{2,1,0:T(8,128)S(1)} custom-call(bf16[4,256,1024]{2,1,0:T(8,128)(2,1)S(1)} %get-tuple-element.24.query_ref, bf16[1040,128]{1,0:T(8,128)(2,1)S(1)} %collective-permute-done.8.refs_0_, f32[2,128,512]{2,1,0:T(8,128)S(1)} %shard_map.44.refs_1_), custom_call_target="tpu_custom_call" | custom-call | flops 8589934592 | bytes 2097152 | tf_op jit(solution)/shard_map/pallas_call | solution.py:294
  31.1 2.8 %shard_map.46 = f32[4,512,128]{2,1,0:T(8,128)} custom-call(bf16[4,256,1024]{2,1,0:T(8,128)(2,1)S(1)} %get-tuple-element.24.query_ref, bf16[2064,128]{1,0:T(8,128)(2,1)S(1)} %collective-permute-done.1.refs_0_, f32[2,128,512]{2,1,0:T(8,128)S(1)} %shard_map.45.refs_1_, f32[2,128,512]{2,1,0:T(8,128)S(1)} %shard_map.43.refs_2_), custom_call_target="tpu_custom_call" | custom-call | flops 8589934592 | bytes 2097152 | tf_op jit(solution)/shard_map/pallas_call | solution.py:294
  (4 shorter events, 0.0 us)
Async XLA Ops:
  1.2 4.5 %collective-permute-start = (bf16[1040,128]{1,0:T(8,128)(2,1)S(1)}, bf16[1040,128]{1,0:T(8,128)(2,1)S(1)}, u32[]{:S(2)}, u32[]{:S(2)}) collective-permute-start(bf16[1040,128]{1,0:T(8,128)(2,1)S(1)} %get-tuple-element.26), channel_id=1, source_target_pairs={{1,0},{0,1},{3,2},{2,3},{5,4},{4,5},{7,6},{6,7},{9,8},{8,9},{11,10... | collective-permute-start | bytes 798728 | tf_op jit(solution)/shard_map/ppermute | solution.py:310
  1.9 14.2 %collective-permute-start.5 = (bf16[2064,128]{1,0:T(8,128)(2,1)S(1)}, bf16[2064,128]{1,0:T(8,128)(2,1)S(1)}, u32[]{:S(2)}, u32[]{:S(2)}) collective-permute-start(bf16[2064,128]{1,0:T(8,128)(2,1)S(1)} %get-tuple-element.22.own_ref), channel_id=1, source_target_pairs={{3,0},{2,1},{1,2},{0,3},{7,4},{6,5},{5,6},{4,7},{11,8},{10,9},{9,1... | collective-permute-start | bytes 1585160 | tf_op jit(solution)/shard_map/ppermute | solution.py:310
  2.1 28.9 %collective-permute-start.1 = (bf16[2064,128]{1,0:T(8,128)(2,1)S(1)}, bf16[2064,128]{1,0:T(8,128)(2,1)S(1)}, u32[]{:S(2)}, u32[]{:S(2)}) collective-permute-start(bf16[2064,128]{1,0:T(8,128)(2,1)S(1)} %get-tuple-element.22.own_ref), channel_id=1, source_target_pairs={{4,1},{6,3},{1,4},{8,5},{3,6},{10,7},{5,8},{12,9},{7,10},{14,11},{... | collective-permute-start | bytes 1585160 | tf_op jit(solution)/shard_map/ppermute | solution.py:310
  5.6 3.1 %collective-permute-start.3 = (bf16[1040,128]{1,0:T(8,128)(2,1)S(1)}, bf16[1040,128]{1,0:T(8,128)(2,1)S(1)}, u32[]{:S(2)}, u32[]{:S(2)}) collective-permute-start(bf16[1040,128]{1,0:T(8,128)(2,1)S(1)} %get-tuple-element.29), channel_id=1, source_target_pairs={{1,0},{0,1},{3,2},{2,3},{5,4},{4,5},{7,6},{6,7},{9,8},{8,9},{11,10... | collective-permute-start | bytes 798728 | tf_op jit(solution)/shard_map/ppermute | solution.py:310
  9.8 12.3 %collective-permute-start.4 = (bf16[1040,128]{1,0:T(8,128)(2,1)S(1)}, bf16[1040,128]{1,0:T(8,128)(2,1)S(1)}, u32[]{:S(2)}, u32[]{:S(2)}) collective-permute-start(bf16[1040,128]{1,0:T(8,128)(2,1)S(1)} %get-tuple-element.29), channel_id=1, source_target_pairs={{4,2},{5,3},{2,4},{3,5},{8,6},{9,7},{6,8},{7,9},{12,10},{13,11},{1... | collective-permute-start | bytes 798728 | tf_op jit(solution)/shard_map/ppermute | solution.py:310
  13.9 13.9 %collective-permute-start.2 = (bf16[1040,128]{1,0:T(8,128)(2,1)S(1)}, bf16[1040,128]{1,0:T(8,128)(2,1)S(1)}, u32[]{:S(2)}, u32[]{:S(2)}) collective-permute-start(bf16[1040,128]{1,0:T(8,128)(2,1)S(1)} %get-tuple-element.26), channel_id=1, source_target_pairs={{4,2},{5,3},{2,4},{3,5},{8,6},{9,7},{6,8},{7,9},{12,10},{13,11},{1... | collective-permute-start | bytes 798728 | tf_op jit(solution)/shard_map/ppermute | solution.py:310
  16.2 3.1 %collective-permute-start.6 = (bf16[2064,128]{1,0:T(8,128)(2,1)S(1)}, bf16[2064,128]{1,0:T(8,128)(2,1)S(1)}, u32[]{:S(2)}, u32[]{:S(2)}) collective-permute-start(bf16[2064,128]{1,0:T(8,128)(2,1)S(1)} %collective-permute-done.5.refs_0_), channel_id=1, source_target_pairs={{1,0},{0,1},{3,2},{2,3},{5,4},{4,5},{7,6},{6,7},{9,8},{8,9},{11,10... | collective-permute-start | bytes 1585160 | tf_op jit(solution)/shard_map/ppermute | solution.py:310
  22.1 2.8 %collective-permute-start.7 = (bf16[1040,128]{1,0:T(8,128)(2,1)S(1)}, bf16[1040,128]{1,0:T(8,128)(2,1)S(1)}, u32[]{:S(2)}, u32[]{:S(2)}) collective-permute-start(bf16[1040,128]{1,0:T(8,128)(2,1)S(1)} %collective-permute-done.4.refs_0_), channel_id=1, source_target_pairs={{1,0},{0,1},{3,2},{2,3},{5,4},{4,5},{7,6},{6,7},{9,8},{8,9},{11,10... | collective-permute-start | bytes 798728 | tf_op jit(solution)/shard_map/ppermute | solution.py:310
  27.8 2.2 %collective-permute-start.8 = (bf16[1040,128]{1,0:T(8,128)(2,1)S(1)}, bf16[1040,128]{1,0:T(8,128)(2,1)S(1)}, u32[]{:S(2)}, u32[]{:S(2)}) collective-permute-start(bf16[1040,128]{1,0:T(8,128)(2,1)S(1)} %collective-permute-done.2.refs_0_), channel_id=1, source_target_pairs={{1,0},{0,1},{3,2},{2,3},{5,4},{4,5},{7,6},{6,7},{9,8},{8,9},{11,10... | collective-permute-start | bytes 798728 | tf_op jit(solution)/shard_map/ppermute | solution.py:310

commit v11 on v9

--- a/solution.py
+++ b/solution.py
@@ -17,10 +17,10 @@
 
 OWN = (0, 0, 0, 0)
 PAIR = (1, -1, 1, -1)
-NEAR = (2, 2, -2, -2)
+NEAR = (3, 1, -1, -3)
 CROSS = (-2, -2, 2, 2)
 FAR = (-3, 3, -3, 3)
-NEAR_OF_PAIR = (3, 1, -1, -3)
+NEAR_OF_PAIR = (2, 2, -2, -2)
 CROSS_OF_PAIR = (-1, -3, 3, 1)
 
 

time: 34.5 us -> 34.6 us (level)
  waiting for transfers between devices: 3.31 us -> 2.87 us
  starting transfers between devices: 14.2 us -> 14.6 us
    ppermute x9, waiting for transfers between devices: 3.31 us -> 2.87 us  [fetched(): lax.ppermute(value, axis, [(i, t) for i, t in sources if 0 <= i < count])]
    ppermute x9, starting transfers between devices: 14.2 us -> 14.6 us  [fetched(): lax.ppermute(value, axis, [(i, t) for i, t in sources if 0 <= i < count])]
where the time goes in v11:
time: 34.6 us; the launch traced here: 34.1 us
  Pallas kernels  16.3 us (47%)
  starting transfers between devices  14.6 us (42%)
  waiting for transfers between devices  2.87 us (8%)
    ppermute x9, starting transfers between devices, fetched(): lax.ppermute(value, axis, [(i, t) for i, t in sources if 0 <= i < count])  14.6 us
    pallas_call x8, Pallas kernels, band_terms(): pl.pallas_call(functools.partial(band_kernel, axis, places, spans, held,...  12.2 us
    pallas_call x1, Pallas kernels, chip_terms(): pl.pallas_call(functools.partial(chip_kernel, axis, low), out_shape=[jax....  2.95 us
    ppermute x9, waiting for transfers between devices, fetched(): lax.ppermute(value, axis, [(i, t) for i, t in sources if 0 <= i < count])  2.87 us
    pallas_call x1, Pallas kernels, pack(): pl.pallas_call(pack_kernel, out_shape=[jax.ShapeDtypeStruct((part * chann...  1.17 us
  transfers between devices with their start and end apart: 9, of which 4 were waited for; matrix products, arithmetic and copies ran while one was open for 0% of the time, Pallas kernels for 36%

profile of v11, /device:TPU:19, one launch (start us, length us, event | category | flops | bytes accessed | tf_op | source)
XLA Modules:
  0.0 34.1 jit_solution(8554414058048689517)
XLA Ops:
  0.0 1.2 %shard_map.37 = (bf16[2064,128]{1,0:T(8,128)(2,1)S(1)}, bf16[1040,128]{1,0:T(8,128)(2,1)S(1)}, bf16[1040,128]{1,0:T(8,128)(2,1)S(1)}) custom-call(bf16[2048,128]{1,0:T(8,128)(2,1)} %bitcast.2, s32[1,512]{1,0:T(1,128)} %bitcast.3, s32[4]{0:T(128)} %bins_ref.1), custom_call_target="tpu_custom_call" | custom-call | bytes 1048576 | tf_op jit(solution)/shard_map/pallas_call | solution.py:138
  1.2 0.7 %collective-permute-start = (bf16[1040,128]{1,0:T(8,128)(2,1)S(1)}, bf16[1040,128]{1,0:T(8,128)(2,1)S(1)}, u32[]{:S(2)}, u32[]{:S(2)}) collective-permute-start(bf16[1040,128]{1,0:T(8,128)(2,1)S(1)} %get-tuple-element.26), channel_id=1, source_target_pairs={{1,0},{0,1},{3,2},{2,3},{5,4},{4,5},{7,6},{6,7},{9,8},{8,9},{11,10... | collective-permute-start | bytes 798728 | tf_op jit(solution)/shard_map/ppermute | solution.py:319
  1.9 0.2 collective-permute-start.5
  2.1 3.5 %collective-permute-start.1 = (bf16[2064,128]{1,0:T(8,128)(2,1)S(1)}, bf16[2064,128]{1,0:T(8,128)(2,1)S(1)}, u32[]{:S(2)}, u32[]{:S(2)}) collective-permute-start(bf16[2064,128]{1,0:T(8,128)(2,1)S(1)} %get-tuple-element.22.own_ref), channel_id=1, source_target_pairs={{4,1},{6,3},{1,4},{8,5},{3,6},{10,7},{5,8},{12,9},{7,10},{14,11},{... | collective-permute-start | bytes 1585160 | tf_op jit(solution)/shard_map/ppermute | solution.py:319
  5.6 0.1 collective-permute-start.3
  5.7 3.0 %shard_map.38 = (bf16[4,256,1024]{2,1,0:T(8,128)(2,1)S(1)}, f32[4,128,512]{2,1,0:T(8,128)S(1)}) custom-call(bf16[2064,128]{1,0:T(8,128)(2,1)S(1)} %get-tuple-element.22.own_ref, bf16[1040,128]{1,0:T(8,128)(2,1)S(1)} %collective-permute-done.pair_ref), custom_call_target="tpu_custom_call" | custom-call | flops 8589934592 | bytes 2097152 | tf_op jit(solution)/shard_map/pallas_call | solution.py:283
  8.7 1.1 %shard_map.39.refs_1_ = f32[2,128,512]{2,1,0:T(8,128)S(1)} custom-call(bf16[4,256,1024]{2,1,0:T(8,128)(2,1)S(1)} %get-tuple-element.24.query_ref, bf16[1040,128]{1,0:T(8,128)(2,1)S(1)} %collective-permute-done.3.refs_0_, f32[4,128,512]{2,1,0:T(8,128)S(1)} %get-tuple-element.28.refs_1_.refs_2_), custom_call_target="tpu_custom_call" | custom-call | flops 8589934592 | bytes 2097152 | tf_op jit(solution)/shard_map/pallas_call | solution.py:303
  9.8 4.1 %collective-permute-start.4 = (bf16[1040,128]{1,0:T(8,128)(2,1)S(1)}, bf16[1040,128]{1,0:T(8,128)(2,1)S(1)}, u32[]{:S(2)}, u32[]{:S(2)}) collective-permute-start(bf16[1040,128]{1,0:T(8,128)(2,1)S(1)} %get-tuple-element.29), channel_id=1, source_target_pairs={{4,2},{5,3},{2,4},{3,5},{8,6},{9,7},{6,8},{7,9},{12,10},{13,11},{1... | collective-permute-start | bytes 798728 | tf_op jit(solution)/shard_map/ppermute | solution.py:319
  13.9 2.3 %collective-permute-start.2 = (bf16[1040,128]{1,0:T(8,128)(2,1)S(1)}, bf16[1040,128]{1,0:T(8,128)(2,1)S(1)}, u32[]{:S(2)}, u32[]{:S(2)}) collective-permute-start(bf16[1040,128]{1,0:T(8,128)(2,1)S(1)} %get-tuple-element.26), channel_id=1, source_target_pairs={{4,2},{5,3},{2,4},{3,5},{8,6},{9,7},{6,8},{7,9},{12,10},{13,11},{1... | collective-permute-start | bytes 798728 | tf_op jit(solution)/shard_map/ppermute | solution.py:319
  16.2 0.0 collective-permute-done.5.refs_0_
  16.2 1.1 %collective-permute-start.6 = (bf16[2064,128]{1,0:T(8,128)(2,1)S(1)}, bf16[2064,128]{1,0:T(8,128)(2,1)S(1)}, u32[]{:S(2)}, u32[]{:S(2)}) collective-permute-start(bf16[2064,128]{1,0:T(8,128)(2,1)S(1)} %collective-permute-done.5.refs_0_), channel_id=1, source_target_pairs={{1,0},{0,1},{3,2},{2,3},{5,4},{4,5},{7,6},{6,7},{9,8},{8,9},{11,10... | collective-permute-start | bytes 1585160 | tf_op jit(solution)/shard_map/ppermute | solution.py:319
  17.3 2.0 %shard_map.40.refs_1_ = f32[4,128,512]{2,1,0:T(8,128)S(1)} custom-call(bf16[4,256,1024]{2,1,0:T(8,128)(2,1)S(1)} %get-tuple-element.24.query_ref, bf16[2064,128]{1,0:T(8,128)(2,1)S(1)} %collective-permute-done.5.refs_0_, f32[2,128,512]{2,1,0:T(8,128)S(1)} %shard_map.39.refs_1_, f32[4,128,512]{2,1,0:T(8,128)S(1)} %get-tuple-element.28.refs_1_.refs_2_), custom_call_target="tpu_custom_call" | custom-call | flops 8589934592 | bytes 2097152 | tf_op jit(solution)/shard_map/pallas_call | solution.py:303
  19.3 1.9 %shard_map.41.refs_1_ = f32[4,128,512]{2,1,0:T(8,128)S(1)} custom-call(bf16[4,256,1024]{2,1,0:T(8,128)(2,1)S(1)} %get-tuple-element.24.query_ref, bf16[2064,128]{1,0:T(8,128)(2,1)S(1)} %collective-permute-done.6.refs_0_, f32[4,128,512]{2,1,0:T(8,128)S(1)} %shard_map.40.refs_1_), custom_call_target="tpu_custom_call" | custom-call | flops 8589934592 | bytes 2097152 | tf_op jit(solution)/shard_map/pallas_call | solution.py:303
  21.2 0.9 %collective-permute-done.4.refs_0_ = bf16[1040,128]{1,0:T(8,128)(2,1)S(1)} collective-permute-done((bf16[1040,128]{1,0:T(8,128)(2,1)S(1)}, bf16[1040,128]{1,0:T(8,128)(2,1)S(1)}, u32[]{:S(2)}, u32[]{:S(2)}) %collective-permute-start.4) | collective-permute-done | bytes 266272 | tf_op jit(solution)/shard_map/ppermute | solution.py:319
  22.1 1.6 %collective-permute-start.7 = (bf16[1040,128]{1,0:T(8,128)(2,1)S(1)}, bf16[1040,128]{1,0:T(8,128)(2,1)S(1)}, u32[]{:S(2)}, u32[]{:S(2)}) collective-permute-start(bf16[1040,128]{1,0:T(8,128)(2,1)S(1)} %collective-permute-done.4.refs_0_), channel_id=1, source_target_pairs={{1,0},{0,1},{3,2},{2,3},{5,4},{4,5},{7,6},{6,7},{9,8},{8,9},{11,10... | collective-permute-start | bytes 798728 | tf_op jit(solution)/shard_map/ppermute | solution.py:319
  23.6 1.1 %shard_map.42.refs_1_ = f32[2,128,512]{2,1,0:T(8,128)S(1)} custom-call(bf16[4,256,1024]{2,1,0:T(8,128)(2,1)S(1)} %get-tuple-element.24.query_ref, bf16[1040,128]{1,0:T(8,128)(2,1)S(1)} %collective-permute-done.4.refs_0_, f32[4,128,512]{2,1,0:T(8,128)S(1)} %shard_map.41.refs_1_), custom_call_target="tpu_custom_call" | custom-call | flops 8589934592 | bytes 2097152 | tf_op jit(solution)/shard_map/pallas_call | solution.py:303
  24.7 0.1 collective-permute-done.7.refs_0_
  24.8 1.1 %shard_map.43.refs_2_ = f32[2,128,512]{2,1,0:T(8,128)S(1)} custom-call(bf16[4,256,1024]{2,1,0:T(8,128)(2,1)S(1)} %get-tuple-element.24.query_ref, bf16[1040,128]{1,0:T(8,128)(2,1)S(1)} %collective-permute-done.7.refs_0_, f32[2,128,512]{2,1,0:T(8,128)S(1)} %shard_map.42.refs_1_), custom_call_target="tpu_custom_call" | custom-call | flops 8589934592 | bytes 2097152 | tf_op jit(solution)/shard_map/pallas_call | solution.py:303
  25.9 1.8 %collective-permute-done.2.refs_0_ = bf16[1040,128]{1,0:T(8,128)(2,1)S(1)} collective-permute-done((bf16[1040,128]{1,0:T(8,128)(2,1)S(1)}, bf16[1040,128]{1,0:T(8,128)(2,1)S(1)}, u32[]{:S(2)}, u32[]{:S(2)}) %collective-permute-start.2) | collective-permute-done | bytes 266272 | tf_op jit(solution)/shard_map/ppermute | solution.py:319
  27.8 1.0 %collective-permute-start.8 = (bf16[1040,128]{1,0:T(8,128)(2,1)S(1)}, bf16[1040,128]{1,0:T(8,128)(2,1)S(1)}, u32[]{:S(2)}, u32[]{:S(2)}) collective-permute-start(bf16[1040,128]{1,0:T(8,128)(2,1)S(1)} %collective-permute-done.2.refs_0_), channel_id=1, source_target_pairs={{1,0},{0,1},{3,2},{2,3},{5,4},{4,5},{7,6},{6,7},{9,8},{8,9},{11,10... | collective-permute-start | bytes 798728 | tf_op jit(solution)/shard_map/ppermute | solution.py:319
  28.8 1.1 %shard_map.44.refs_1_ = f32[2,128,512]{2,1,0:T(8,128)S(1)} custom-call(bf16[4,256,1024]{2,1,0:T(8,128)(2,1)S(1)} %get-tuple-element.24.query_ref, bf16[1040,128]{1,0:T(8,128)(2,1)S(1)} %collective-permute-done.2.refs_0_, f32[4,128,512]{2,1,0:T(8,128)S(1)} %shard_map.41.refs_1_), custom_call_target="tpu_custom_call" | custom-call | flops 8589934592 | bytes 2097152 | tf_op jit(solution)/shard_map/pallas_call | solution.py:303
  29.9 0.1 collective-permute-done.8.refs_0_
  30.0 1.1 %shard_map.45.refs_1_ = f32[2,128,512]{2,1,0:T(8,128)S(1)} custom-call(bf16[4,256,1024]{2,1,0:T(8,128)(2,1)S(1)} %get-tuple-element.24.query_ref, bf16[1040,128]{1,0:T(8,128)(2,1)S(1)} %collective-permute-done.8.refs_0_, f32[2,128,512]{2,1,0:T(8,128)S(1)} %shard_map.44.refs_1_), custom_call_target="tpu_custom_call" | custom-call | flops 8589934592 | bytes 2097152 | tf_op jit(solution)/shard_map/pallas_call | solution.py:303
  31.1 2.9 %shard_map.46 = f32[4,512,128]{2,1,0:T(8,128)} custom-call(bf16[4,256,1024]{2,1,0:T(8,128)(2,1)S(1)} %get-tuple-element.24.query_ref, bf16[2064,128]{1,0:T(8,128)(2,1)S(1)} %collective-permute-done.1.refs_0_, f32[2,128,512]{2,1,0:T(8,128)S(1)} %shard_map.45.refs_1_, f32[2,128,512]{2,1,0:T(8,128)S(1)} %shard_map.43.refs_2_), custom_call_target="tpu_custom_call" | custom-call | flops 8589934592 | bytes 2097152 | tf_op jit(solution)/shard_map/pallas_call | solution.py:303
  (4 shorter events, 0.0 us)
Async XLA Ops:
  1.2 4.5 %collective-permute-start = (bf16[1040,128]{1,0:T(8,128)(2,1)S(1)}, bf16[1040,128]{1,0:T(8,128)(2,1)S(1)}, u32[]{:S(2)}, u32[]{:S(2)}) collective-permute-start(bf16[1040,128]{1,0:T(8,128)(2,1)S(1)} %get-tuple-element.26), channel_id=1, source_target_pairs={{1,0},{0,1},{3,2},{2,3},{5,4},{4,5},{7,6},{6,7},{9,8},{8,9},{11,10... | collective-permute-start | bytes 798728 | tf_op jit(solution)/shard_map/ppermute | solution.py:319
  1.9 14.2 %collective-permute-start.5 = (bf16[2064,128]{1,0:T(8,128)(2,1)S(1)}, bf16[2064,128]{1,0:T(8,128)(2,1)S(1)}, u32[]{:S(2)}, u32[]{:S(2)}) collective-permute-start(bf16[2064,128]{1,0:T(8,128)(2,1)S(1)} %get-tuple-element.22.own_ref), channel_id=1, source_target_pairs={{3,0},{2,1},{1,2},{0,3},{7,4},{6,5},{5,6},{4,7},{11,8},{10,9},{9,1... | collective-permute-start | bytes 1585160 | tf_op jit(solution)/shard_map/ppermute | solution.py:319
  2.1 28.9 %collective-permute-start.1 = (bf16[2064,128]{1,0:T(8,128)(2,1)S(1)}, bf16[2064,128]{1,0:T(8,128)(2,1)S(1)}, u32[]{:S(2)}, u32[]{:S(2)}) collective-permute-start(bf16[2064,128]{1,0:T(8,128)(2,1)S(1)} %get-tuple-element.22.own_ref), channel_id=1, source_target_pairs={{4,1},{6,3},{1,4},{8,5},{3,6},{10,7},{5,8},{12,9},{7,10},{14,11},{... | collective-permute-start | bytes 1585160 | tf_op jit(solution)/shard_map/ppermute | solution.py:319
  5.6 3.1 %collective-permute-start.3 = (bf16[1040,128]{1,0:T(8,128)(2,1)S(1)}, bf16[1040,128]{1,0:T(8,128)(2,1)S(1)}, u32[]{:S(2)}, u32[]{:S(2)}) collective-permute-start(bf16[1040,128]{1,0:T(8,128)(2,1)S(1)} %get-tuple-element.29), channel_id=1, source_target_pairs={{1,0},{0,1},{3,2},{2,3},{5,4},{4,5},{7,6},{6,7},{9,8},{8,9},{11,10... | collective-permute-start | bytes 798728 | tf_op jit(solution)/shard_map/ppermute | solution.py:319
  9.8 12.3 %collective-permute-start.4 = (bf16[1040,128]{1,0:T(8,128)(2,1)S(1)}, bf16[1040,128]{1,0:T(8,128)(2,1)S(1)}, u32[]{:S(2)}, u32[]{:S(2)}) collective-permute-start(bf16[1040,128]{1,0:T(8,128)(2,1)S(1)} %get-tuple-element.29), channel_id=1, source_target_pairs={{4,2},{5,3},{2,4},{3,5},{8,6},{9,7},{6,8},{7,9},{12,10},{13,11},{1... | collective-permute-start | bytes 798728 | tf_op jit(solution)/shard_map/ppermute | solution.py:319
  13.9 13.9 %collective-permute-start.2 = (bf16[1040,128]{1,0:T(8,128)(2,1)S(1)}, bf16[1040,128]{1,0:T(8,128)(2,1)S(1)}, u32[]{:S(2)}, u32[]{:S(2)}) collective-permute-start(bf16[1040,128]{1,0:T(8,128)(2,1)S(1)} %get-tuple-element.26), channel_id=1, source_target_pairs={{4,2},{5,3},{2,4},{3,5},{8,6},{9,7},{6,8},{7,9},{12,10},{13,11},{1... | collective-permute-start | bytes 798728 | tf_op jit(solution)/shard_map/ppermute | solution.py:319
  16.2 3.1 %collective-permute-start.6 = (bf16[2064,128]{1,0:T(8,128)(2,1)S(1)}, bf16[2064,128]{1,0:T(8,128)(2,1)S(1)}, u32[]{:S(2)}, u32[]{:S(2)}) collective-permute-start(bf16[2064,128]{1,0:T(8,128)(2,1)S(1)} %collective-permute-done.5.refs_0_), channel_id=1, source_target_pairs={{1,0},{0,1},{3,2},{2,3},{5,4},{4,5},{7,6},{6,7},{9,8},{8,9},{11,10... | collective-permute-start | bytes 1585160 | tf_op jit(solution)/shard_map/ppermute | solution.py:319
  22.1 2.8 %collective-permute-start.7 = (bf16[1040,128]{1,0:T(8,128)(2,1)S(1)}, bf16[1040,128]{1,0:T(8,128)(2,1)S(1)}, u32[]{:S(2)}, u32[]{:S(2)}) collective-permute-start(bf16[1040,128]{1,0:T(8,128)(2,1)S(1)} %collective-permute-done.4.refs_0_), channel_id=1, source_target_pairs={{1,0},{0,1},{3,2},{2,3},{5,4},{4,5},{7,6},{6,7},{9,8},{8,9},{11,10... | collective-permute-start | bytes 798728 | tf_op jit(solution)/shard_map/ppermute | solution.py:319
  27.8 2.2 %collective-permute-start.8 = (bf16[1040,128]{1,0:T(8,128)(2,1)S(1)}, bf16[1040,128]{1,0:T(8,128)(2,1)S(1)}, u32[]{:S(2)}, u32[]{:S(2)}) collective-permute-start(bf16[1040,128]{1,0:T(8,128)(2,1)S(1)} %collective-permute-done.2.refs_0_), channel_id=1, source_target_pairs={{1,0},{0,1},{3,2},{2,3},{5,4},{4,5},{7,6},{6,7},{9,8},{8,9},{11,10... | collective-permute-start | bytes 798728 | tf_op jit(solution)/shard_map/ppermute | solution.py:319
